TPU v7x, 32 devices: a whole 2x2x4 slice. The times are simulated.
32 devices in a mesh: dp: 4 (over z), seq: 8 (over y, x, core).
Axes of the slice: x: 2, y: 2, z: 4, core: 2. Of those that a mesh axis runs over, the one named last changes fastest.
Arguments:
- tokens: bfloat16 [8, 512, 2048], P('dp', 'seq'), may hold values from -6 to 6
- lengths: int32 [8], P('dp'), may hold values from 64 to 512, as said below
- norm_gain: float32 [2048], replicated, may hold values from 0.25 to 1.75
- mix_weight: bfloat16 [2048, 8224], P(('dp', 'seq')), may hold values from -0.125 to 0.125
- conv_weight: float32 [4, 6144], replicated, may hold values from -3 to 3
- decay_rate: float32 [16], replicated, may hold values from 0.0002 to 0.05
- out_gain: float32 [128], replicated, may hold values from 0.25 to 1.75
- out_weight: bfloat16 [2048, 2048], P(('dp', 'seq')), may hold values from -0.1875 to 0.1875
- mlp_gain: float32 [2048], replicated, may hold values from 0.25 to 1.75
- mlp_in_weight: bfloat16 [2048, 11264], P(('dp', 'seq')), may hold values from -0.125 to 0.125
- mlp_out_weight: bfloat16 [2048, 5632], P(('dp', 'seq')), may hold values from -0.15625 to 0.15625
- grad_out: bfloat16 [8, 512, 2048], P('dp', 'seq'), may hold values from -6 to 6
Outputs:
- result: bfloat16 [8, 512, 2048], P('dp', 'seq')
- grad_tokens: float32 [8, 512, 2048], P('dp', 'seq')
- grad_norm_gain: float32 [2048], replicated
- grad_mix_weight: float32 [2048, 8224], P(('dp', 'seq'))
- grad_conv_weight: float32 [4, 6144], replicated
- grad_decay_rate: float32 [16], replicated
- grad_out_gain: float32 [128], replicated
- grad_out_weight: float32 [2048, 2048], P(('dp', 'seq'))
- grad_mlp_gain: float32 [2048], replicated
- grad_mlp_in_weight: float32 [2048, 11264], P(('dp', 'seq'))
- grad_mlp_out_weight: float32 [2048, 5632], P(('dp', 'seq'))
Inputs may be any that keep to these rules, and one draw needn't show every extreme that they name: `lengths`: in each data group of 2 consecutive sequences, one sequence drawn from the seed is valid over all 512 positions.
All inputs are finite; a program needn't handle non-finite values.
Results may differ from a plain program's by a relative error of at most 0.017.
Values may be sent and summed in bfloat16 or wider, within the bound.
No kernel may reach another device: no remote copies, remote signals or barrier semaphores. Data moves between devices by JAX's collectives and lax.ppermute only.
A program may use at most 704 MiB of HBM per device.

v0:
```python
from functools import partial

import jax
import jax.numpy as jnp
from jax import lax
from jax.sharding import PartitionSpec as P

BLOCK = 64


eps_norm = 1e-05
eps_key = 1e-06
highest = lax.Precision.HIGHEST


def from_behind(value, axis, by):
    peers = lax.axis_size(axis)
    pairs = [(i, i + by) for i in range(peers) if 0 <= i + by < peers]
    return lax.ppermute(value, axis, pairs)


def rms_scale(rows_in, gain):
    return (
        rows_in * lax.rsqrt(jnp.mean(rows_in * rows_in, axis=-1, keepdims=True) + eps_norm) * gain
    )


def key_norm(rows_in):
    return rows_in * lax.rsqrt(jnp.sum(rows_in * rows_in, axis=-1, keepdims=True) + eps_key)


def conv_mix(extended, conv_weight):
    conv_taps = conv_weight.shape[0]
    row_count = extended.shape[-2] - conv_taps + 1
    running = jnp.zeros(extended.shape[:-2] + (row_count, extended.shape[-1]), jnp.float32)
    for tap_index in range(conv_taps):
        running = (
            running + extended[..., tap_index : tap_index + row_count, :] * conv_weight[tap_index]
        )
    return running


def prepare(extended, conv_weight, head_count):
    mixed_rows = jax.nn.silu(conv_mix(extended, conv_weight))
    model_width = mixed_rows.shape[-1] // 3
    head_width = model_width // head_count
    head_shape = mixed_rows.shape[:-1] + (head_count, head_width)
    queries = key_norm(mixed_rows[..., :model_width].reshape(head_shape)) * float(head_width) ** (
        -0.5
    )
    key_rows = key_norm(mixed_rows[..., model_width : 2 * model_width].reshape(head_shape))
    values = mixed_rows[..., 2 * model_width :].reshape(head_shape)
    return (queries, key_rows, values)


def finish(heads_out, gate_pre, out_gain):
    normed = rms_scale(heads_out, out_gain)
    return normed.reshape(gate_pre.shape) * jax.nn.silu(gate_pre)


def swiglu(gate_up):
    hidden_units = gate_up.shape[-1] // 2
    return jax.nn.silu(gate_up[..., :hidden_units]) * gate_up[..., hidden_units:]


def delta_block(state_now, block_in):
    queries, key_rows, values, logdecay, strength = block_in
    block_size = queries.shape[0]
    cumulative = jnp.cumsum(logdecay)
    spread = cumulative[:, None] - cumulative[None, :]
    row_index = lax.broadcasted_iota(jnp.int32, (block_size, block_size), 0)
    col_index = lax.broadcasted_iota(jnp.int32, (block_size, block_size), 1)
    below = (row_index > col_index).astype(jnp.float32)
    upto = (row_index >= col_index).astype(jnp.float32)
    fading = jnp.exp(jnp.minimum(spread, 0.0))
    lower_part = (
        below * fading * strength[:, None] * jnp.dot(key_rows, key_rows.T, precision=highest)
    )
    identity_block = jnp.eye(block_size, dtype=jnp.float32)
    inverse = identity_block - lower_part
    power_term = jnp.dot(lower_part, lower_part, precision=highest)
    factor_count = block_size.bit_length() - 2
    for factor_index in range(factor_count):
        inverse = jnp.dot(inverse, identity_block + power_term, precision=highest)
        if factor_index + 1 < factor_count:
            power_term = jnp.dot(power_term, power_term, precision=highest)
    growth = jnp.exp(cumulative)
    weighted = jnp.dot(inverse, key_rows * (strength * growth)[:, None], precision=highest)
    targets = jnp.dot(inverse, values * strength[:, None], precision=highest)
    fresh_values = targets - jnp.dot(weighted, state_now, precision=highest)
    scores = upto * fading * jnp.dot(queries, key_rows.T, precision=highest)
    output = jnp.dot(queries * growth[:, None], state_now, precision=highest) + jnp.dot(
        scores, fresh_values, precision=highest
    )
    last_decay = cumulative[-1]
    carried = jnp.exp(last_decay) * state_now + jnp.dot(
        (key_rows * jnp.exp(last_decay - cumulative)[:, None]).T, fresh_values, precision=highest
    )
    return (carried, output)


def delta_rule(queries, key_rows, values, logit_decay, logit_strength, decay_scale, block_len):
    length, key_width = queries.shape
    value_width = values.shape[1]
    block_count = length // block_len
    logdecay = -decay_scale * jax.nn.softplus(logit_decay)
    strength = jax.nn.sigmoid(logit_strength)
    blocks = (
        queries.reshape(block_count, block_len, key_width),
        key_rows.reshape(block_count, block_len, key_width),
        values.reshape(block_count, block_len, value_width),
        logdecay.reshape(block_count, block_len),
        strength.reshape(block_count, block_len),
    )
    initial = jnp.zeros((key_width, value_width), jnp.float32)
    final_state, outputs = lax.scan(jax.checkpoint(delta_block), initial, blocks)
    return outputs.reshape(length, value_width)


def all_heads(queries, key_rows, values, logit_decay, logit_strength, rates, block_len):
    per_head = jax.vmap(
        partial(delta_rule, block_len=block_len), in_axes=(1, 1, 1, 1, 1, 0), out_axes=1
    )
    per_batch = jax.vmap(per_head, in_axes=(0, 0, 0, 0, 0, None), out_axes=0)
    return per_batch(queries, key_rows, values, logit_decay, logit_strength, rates)


def shards(
    tokens,
    lengths,
    norm_gain,
    mix_weight,
    conv_weight,
    decay_rate,
    out_gain,
    out_weight,
    mlp_gain,
    mlp_in_weight,
    mlp_out_weight,
    grad_out,
):
    micro_count, seq_rows, model_width = tokens.shape
    head_count = decay_rate.shape[0]
    local_heads = head_count // lax.axis_size("seq")
    conv_taps = conv_weight.shape[0]
    hidden_units = mlp_out_weight.shape[1]
    qkv_width = 3 * model_width
    main_width = 4 * model_width
    owner_rows = model_width // lax.axis_size(("dp", "seq"))
    owner_place = lax.axis_index(("dp", "seq"))
    seq_place = lax.axis_index("seq")
    positions = seq_place * seq_rows + lax.broadcasted_iota(jnp.int32, (micro_count, seq_rows), 1)
    valid_mask = (positions < lengths[:, None]).astype(jnp.float32)[..., None]
    inputs = tokens.astype(jnp.float32)
    normed, norm_back = jax.vjp(rms_scale, inputs, norm_gain)
    normed_low = normed.astype(jnp.bfloat16)
    mix_full, out_full = (
        lax.all_gather(mix_weight, ("dp", "seq"), axis=0, tiled=True),
        lax.all_gather(out_weight, ("dp", "seq"), axis=0, tiled=True),
    )
    projected = jnp.dot(normed_low, mix_full, preferred_element_type=jnp.float32).astype(
        jnp.bfloat16
    )
    mixed_in = projected[..., :qkv_width]
    gate_pre = projected[..., qkv_width : qkv_width + model_width]
    logit_decay = projected[..., qkv_width + model_width : qkv_width + model_width + head_count]
    logit_strength = projected[..., qkv_width + model_width + head_count :]
    edge_rows = from_behind(mixed_in[:, seq_rows - (conv_taps - 1) :, :], "seq", 1)
    extended = jnp.concatenate([edge_rows, mixed_in], axis=1).astype(jnp.float32)
    (queries, key_rows, values), prep_back = jax.vjp(
        partial(prepare, head_count=head_count), extended, conv_weight
    )
    sent_heads = (
        lax.all_to_all(
            queries.astype(jnp.bfloat16), "seq", split_axis=2, concat_axis=1, tiled=True
        ),
        lax.all_to_all(
            key_rows.astype(jnp.bfloat16), "seq", split_axis=2, concat_axis=1, tiled=True
        ),
        lax.all_to_all(values.astype(jnp.bfloat16), "seq", split_axis=2, concat_axis=1, tiled=True),
        lax.all_to_all(logit_decay, "seq", split_axis=2, concat_axis=1, tiled=True),
        lax.all_to_all(logit_strength, "seq", split_axis=2, concat_axis=1, tiled=True),
    )
    head_rates = lax.dynamic_slice_in_dim(decay_rate, seq_place * local_heads, local_heads)
    head_out, delta_back = jax.vjp(
        partial(all_heads, block_len=BLOCK),
        sent_heads[0].astype(jnp.float32),
        sent_heads[1].astype(jnp.float32),
        sent_heads[2].astype(jnp.float32),
        sent_heads[3].astype(jnp.float32),
        sent_heads[4].astype(jnp.float32),
        head_rates,
    )
    returned = lax.all_to_all(
        head_out.astype(jnp.bfloat16), "seq", split_axis=1, concat_axis=2, tiled=True
    )
    mixed_rows, finish_back = jax.vjp(
        finish, returned.astype(jnp.float32), gate_pre.astype(jnp.float32), out_gain
    )
    mixed_low = mixed_rows.astype(jnp.bfloat16)
    hidden = inputs + jnp.dot(mixed_low, out_full, preferred_element_type=jnp.float32)
    second, second_back = jax.vjp(rms_scale, hidden, mlp_gain)
    second_low = second.astype(jnp.bfloat16)
    in_full, down_full = (
        lax.all_gather(mlp_in_weight, ("dp", "seq"), axis=0, tiled=True),
        lax.all_gather(mlp_out_weight, ("dp", "seq"), axis=0, tiled=True),
    )
    gate_up = jnp.dot(second_low, in_full, preferred_element_type=jnp.float32).astype(jnp.bfloat16)
    activated, swiglu_back = jax.vjp(swiglu, gate_up.astype(jnp.float32))
    activated_low = activated.astype(jnp.bfloat16)
    feed_out = lax.dot_general(
        activated_low, down_full, (((2,), (1,)), ((), ())), preferred_element_type=jnp.float32
    )
    result = (valid_mask * (hidden + feed_out)).astype(jnp.bfloat16)
    cotangent = valid_mask * grad_out.astype(jnp.float32)
    cot_low = cotangent.astype(jnp.bfloat16)
    in_again, down_again = (
        lax.all_gather(mlp_in_weight, ("dp", "seq"), axis=0, tiled=True),
        lax.all_gather(mlp_out_weight, ("dp", "seq"), axis=0, tiled=True),
    )
    grad_act = jnp.dot(cot_low, down_again, preferred_element_type=jnp.float32)
    (grad_gate_up,) = swiglu_back(grad_act)
    grad_gate_low = grad_gate_up.astype(jnp.bfloat16)
    grad_second = lax.dot_general(
        grad_gate_low, in_again, (((2,), (1,)), ((), ())), preferred_element_type=jnp.float32
    )
    grad_hidden_norm, grad_mlp_gain = second_back(grad_second)
    grad_hidden = cotangent + grad_hidden_norm
    grad_branch_low = grad_hidden.astype(jnp.bfloat16)
    flat_second = second_low.reshape(-1, model_width)
    flat_gate_grad = grad_gate_low.reshape(-1, 2 * hidden_units)
    flat_cot = cot_low.reshape(-1, model_width)
    flat_act = activated_low.reshape(-1, hidden_units)
    flat_mixed = mixed_low.reshape(-1, model_width)
    flat_branch_grad = grad_branch_low.reshape(-1, model_width)
    in_term = jnp.einsum(
        "tr,tc->rc", flat_second, flat_gate_grad, preferred_element_type=jnp.float32
    )
    down_term = jnp.einsum("tr,tc->rc", flat_cot, flat_act, preferred_element_type=jnp.float32)
    out_term = jnp.einsum(
        "tr,tc->rc", flat_mixed, flat_branch_grad, preferred_element_type=jnp.float32
    )
    mlp_sums = lax.psum_scatter(
        jnp.concatenate([in_term, down_term, out_term], axis=1),
        ("dp", "seq"),
        scatter_dimension=0,
        tiled=True,
    )
    mix_again, out_again = (
        lax.all_gather(mix_weight, ("dp", "seq"), axis=0, tiled=True),
        lax.all_gather(out_weight, ("dp", "seq"), axis=0, tiled=True),
    )
    grad_mixed = lax.dot_general(
        grad_branch_low, out_again, (((2,), (1,)), ((), ())), preferred_element_type=jnp.float32
    )
    grad_returned, grad_gate, grad_out_gain = finish_back(grad_mixed)
    grad_heads = lax.all_to_all(
        grad_returned.astype(jnp.bfloat16), "seq", split_axis=2, concat_axis=1, tiled=True
    )
    grad_query, grad_keys, grad_values, grad_decay, grad_strength, grad_rates = delta_back(
        grad_heads.astype(jnp.float32)
    )
    returned_grads = (
        lax.all_to_all(
            grad_query.astype(jnp.bfloat16), "seq", split_axis=1, concat_axis=2, tiled=True
        ),
        lax.all_to_all(
            grad_keys.astype(jnp.bfloat16), "seq", split_axis=1, concat_axis=2, tiled=True
        ),
        lax.all_to_all(
            grad_values.astype(jnp.bfloat16), "seq", split_axis=1, concat_axis=2, tiled=True
        ),
        lax.all_to_all(
            grad_decay.astype(jnp.bfloat16), "seq", split_axis=1, concat_axis=2, tiled=True
        ),
        lax.all_to_all(
            grad_strength.astype(jnp.bfloat16), "seq", split_axis=1, concat_axis=2, tiled=True
        ),
    )
    grad_extended, grad_conv = prep_back(
        (
            returned_grads[0].astype(jnp.float32),
            returned_grads[1].astype(jnp.float32),
            returned_grads[2].astype(jnp.float32),
        )
    )
    spilled = from_behind(
        grad_extended[:, : conv_taps - 1, :].astype(jnp.bfloat16), "seq", -1
    ).astype(jnp.float32)
    grad_mixed_in = (
        grad_extended[:, conv_taps - 1 :, :].at[:, seq_rows - (conv_taps - 1) :, :].add(spilled)
    )
    grad_projected = jnp.concatenate(
        [
            grad_mixed_in,
            grad_gate,
            returned_grads[3].astype(jnp.float32),
            returned_grads[4].astype(jnp.float32),
        ],
        axis=2,
    ).astype(jnp.bfloat16)
    grad_normed = lax.dot_general(
        grad_projected, mix_again, (((2,), (1,)), ((), ())), preferred_element_type=jnp.float32
    )
    grad_inputs_norm, grad_norm_gain = norm_back(grad_normed)
    grad_tokens = grad_hidden + grad_inputs_norm
    flat_normed = normed_low.reshape(-1, model_width)
    flat_proj_grad = grad_projected.reshape(-1, grad_projected.shape[-1])
    flat_proj_main = flat_proj_grad[:, :main_width]
    flat_proj_logits = flat_proj_grad[:, main_width:]
    mixer_sums = lax.psum_scatter(
        jnp.einsum("tr,tc->rc", flat_normed, flat_proj_main, preferred_element_type=jnp.float32),
        ("dp", "seq"),
        scatter_dimension=0,
        tiled=True,
    )
    logit_term = jnp.einsum(
        "tr,tc->rc", flat_normed, flat_proj_logits, preferred_element_type=jnp.float32
    )
    rate_terms = lax.dynamic_update_slice(
        jnp.zeros((head_count,), jnp.float32), grad_rates, (seq_place * local_heads,)
    )
    summed_small = lax.psum(
        (grad_norm_gain, grad_conv, rate_terms, grad_out_gain, grad_mlp_gain, logit_term),
        ("dp", "seq"),
    )
    logit_rows = lax.dynamic_slice_in_dim(summed_small[5], owner_place * owner_rows, owner_rows, 0)
    grad_mix = jnp.concatenate([mixer_sums, logit_rows], axis=1)
    return (
        result,
        grad_tokens,
        summed_small[0],
        grad_mix,
        summed_small[1],
        summed_small[2],
        summed_small[3],
        mlp_sums[:, 3 * hidden_units :],
        summed_small[4],
        mlp_sums[:, : 2 * hidden_units],
        mlp_sums[:, 2 * hidden_units : 3 * hidden_units],
    )


def solution(mesh):
    in_specs = (
        P("dp", "seq", None),
        P("dp"),
        P(),
        P(("dp", "seq"), None),
        P(),
        P(),
        P(),
        P(("dp", "seq"), None),
        P(),
        P(("dp", "seq"), None),
        P(("dp", "seq"), None),
        P("dp", "seq", None),
    )
    out_specs = (
        P("dp", "seq", None),
        P("dp", "seq", None),
        P(),
        P(("dp", "seq"), None),
        P(),
        P(),
        P(),
        P(("dp", "seq"), None),
        P(),
        P(("dp", "seq"), None),
        P(("dp", "seq"), None),
    )
    return jax.shard_map(shards, mesh=mesh, in_specs=in_specs, out_specs=out_specs, check_vma=False)
```

profile of v0, /device:TPU:0, one launch (start us, length us, event | category | flops | bytes accessed | tf_op | source)
XLA Modules:
  0.0 3681.2 jit_solution(9922101554554904321)
XLA Ops:
  10.6 200.4 %all-gather.5.cloned.1.call-done = bf16[2048,8224]{1,0:T(8,128)(2,1)} async-done(((bf16[64,8224]{1,0:T(8,128)(2,1)}), bf16[2048,8224]{1,0:T(8,128)(2,1)}) %all-gather.5.cloned.1.call-update) | async-done | bytes 33685520 | tf_op jit(solution)/shard_map/all_gather | solution.py:158
  211.0 15.6 fusion.176
  240.3 4.4 all-to-all-done.2
  262.8 10.4 all-to-all-done.3
  277.9 10.2 all-to-all-done.1
  294.4 7.2 all-to-all-done.4
  302.9 101.5 %while.44 = (s32[]{:T(128)}, f32[2,2,128,128]{3,2,1,0:T(8,128)S(1)}, bf16[8,2,2,64,128]{4,3,0,2,1:T(8,128)(2,1)S(1)}, f32[8,2,2,128,128]{4,3,2,1,0:T(8,128)}, f3...) while((s32[]{:T(128)}, ...), condition=%wide.region_5.6_spmd.clone.clone, body=%wide.region_3.5_spmd.clone.clone.sunk | while | flops 403529984 | bytes 6059785 | solution.py:116
  409.3 9.6 all-to-all-done.5
  428.7 5.1 multiply_reduce_fusion.13
  433.8 121.2 %all-gather.9.cloned.1.call-done = bf16[2048,11264]{1,0:T(8,128)(2,1)} async-done(((bf16[64,11264]{1,0:T(8,128)(2,1)}), bf16[2048,11264]{1,0:T(8,128)(2,1)}) %all-gather.9.cloned.1.call-update) | async-done | bytes 46137360 | tf_op jit(solution)/shard_map/all_gather | solution.py:205
  555.0 20.8 fusion.173
  575.8 124.7 %all-gather.11.cloned.1.call-done = bf16[2048,5632]{1,0:T(8,128)(2,1)} async-done(((bf16[64,5632]{1,0:T(8,128)(2,1)}), bf16[2048,5632]{1,0:T(8,128)(2,1)}) %all-gather.11.cloned.1.call-update) | async-done | bytes 23068688 | tf_op jit(solution)/shard_map/all_gather | solution.py:206
  700.5 16.3 fusion.235
  716.8 23.5 multiply_reduce_fusion.10
  741.5 8.4 multiply_reduce_fusion.11
  760.8 9.7 all-to-all-done.6
  775.9 332.6 %while.43 = (s32[]{:T(128)}, f32[2,2,128,128]{3,2,1,0:T(8,128)}, bf16[8,2,2,64,128]{4,3,0,2,1:T(8,128)(2,1)}, bf16[8,2,2,64,128]{4,3,0,2,1:T(8,128)(2,1)}, bf16[...) while((s32[]{:T(128)}, f32[2,2,128,128]{3,2,1,0:T(8,128)}, ...), condition=%wide.region_22.23_spmd.clone, body=%wide.region_10.0_spmd.clone.sunk | while | flops 1084925952 | bytes 22030588 | solution.py:116
  1133.0 8.3 all-to-all-done.8
  1141.4 4.2 all-to-all-start.7
  1151.2 4.0 all-to-all-done.7
  1184.1 4.1 add_add_fusion.2
  1203.9 26.1 fusion.201
  1231.4 8.1 convolution_bitcast_fusion.2
  1239.5 18.0 convolution_bitcast_fusion.1
  1257.5 34.7 convolution_bitcast_fusion
  1292.2 108.8 %pad_maximum_fusion = f32[2048,18944]{1,0:T(8,128)} fusion(f32[2048,2048]{1,0:T(8,128)} %convolution_bitcast_fusion.2, f32[2048,5632]{1,0:T(8,128)} %convolution_bitcast_fusion.1, f32[2048,11264]{1,0:T(8,128)} %convolution_bitcast_fusion), kind=kLoop, calls=%fused_computation.216 | loop fusion | flops 77594624 | bytes 310378496 | tf_op jit(solution)/shard_map/concatenate | solution.py:244
  1401.8 13.2 fusion.198
  1415.7 4.4 concatenate.28
  1420.2 16.8 fusion.208
  1437.0 45.9 %all-reduce.14 = (f32[2048]{0:T(1024)}, f32[16]{0:T(128)}, f32[128]{0:T(128)}, f32[2048]{0:T(1024)}) all-reduce(f32[2048]{0:T(1024)S(1)} %get-tuple-element.728, f32[16]{0:T(128)S(1)} %negate_dynamic-update-slice_fusion, f32[128]{0:T(128)S(1)} %bitcast_reduce_fusion, ...), channel_id=1, replica_groups=mesh['dp'=4,'seq'=8] {'dp','seq'}, use_global_device_ids=true, to_apply=%region_27.28 | all-reduce | flops 4240 | bytes 33920 | tf_op jit(solution)/shard_map/psum | solution.py:323
  1484.9 554.2 %reduce-scatter.3.cloned.1.call-done = f32[64,8192]{1,0:T(8,128)} async-done(((f32[2048,8192]{1,0:T(8,128)}), f32[64,8192]{1,0:T(8,128)}) %reduce-scatter.3.cloned.1.call-update) | async-done | bytes 2097168 | tf_op jit(solution)/shard_map/reduce_scatter | solution.py:311
  2042.2 1623.2 %reduce-scatter.5.cloned.1.call-done = f32[64,18944]{1,0:T(8,128)} async-done(((f32[2048,18944]{1,0:T(8,128)}), f32[64,18944]{1,0:T(8,128)}) %reduce-scatter.5.cloned.1.call-update) | async-done | bytes 4849680 | tf_op jit(solution)/shard_map/reduce_scatter | solution.py:243
  (1658 shorter events, 596.5 us)
Async XLA Ops:
  7.2 203.8 %all-gather.5.cloned.1.call-start = ((), (), s32[]{:S(2)}) async-start(), calls=%async_computation.14 | async-start | bytes 35143680 | tf_op jit(solution)/shard_map/all_gather | solution.py:158
  7.9 420.7 %all-gather.7.cloned.1.call-start = ((), (), s32[]{:S(2)}) async-start(), calls=%async_computation.15 | async-start | bytes 8650752 | tf_op jit(solution)/shard_map/all_gather | solution.py:159
  8.7 546.3 %all-gather.9.cloned.1.call-start = ((), (), s32[]{:S(2)}) async-start(), calls=%async_computation.16 | async-start | bytes 47579136 | tf_op jit(solution)/shard_map/all_gather | solution.py:205
  9.4 691.0 %all-gather.11.cloned.1.call-start = ((), (), s32[]{:S(2)}) async-start(), calls=%async_computation.17 | async-start | bytes 23789568 | tf_op jit(solution)/shard_map/all_gather | solution.py:206
  10.2 216.4 %copy-start.92 = (f32[2,64]{1,0:T(2,128)}, f32[2,64]{1,0:T(2,128)S(1)}, u32[]{:S(2)}) copy-start(f32[2,64]{1,0:T(2,128)S(1)} %fusion.218) | copy-start | bytes 1540
  10.2 216.4 %copy-start.90 = (f32[2,64]{1,0:T(2,128)}, f32[2,64]{1,0:T(2,128)S(1)}, u32[]{:S(2)}) copy-start(f32[2,64]{1,0:T(2,128)S(1)} %fusion.249) | copy-start | bytes 1540
  10.3 237.4 %copy-start.54 = (f32[1,6144]{1,0:T(1,128)}, f32[1,6144]{1,0:T(1,128)S(1)}, u32[]{:S(2)}) copy-start(f32[1,6144]{1,0:T(1,128)S(1)} %get-tuple-element.826) | copy-start | bytes 73732
  10.3 237.4 %copy-start.56 = (f32[1,6144]{1,0:T(1,128)}, f32[1,6144]{1,0:T(1,128)S(1)}, u32[]{:S(2)}) copy-start(f32[1,6144]{1,0:T(1,128)S(1)} %get-tuple-element.827) | copy-start | bytes 73732
  10.3 237.4 %copy-start.58 = (f32[1,6144]{1,0:T(1,128)}, f32[1,6144]{1,0:T(1,128)S(1)}, u32[]{:S(2)}) copy-start(f32[1,6144]{1,0:T(1,128)S(1)} %get-tuple-element.828) | copy-start | bytes 73732
  10.3 237.4 %copy-start.60 = (f32[1,6144]{1,0:T(1,128)}, f32[1,6144]{1,0:T(1,128)S(1)}, u32[]{:S(2)}) copy-start(f32[1,6144]{1,0:T(1,128)S(1)} %get-tuple-element.829) | copy-start | bytes 73732
  10.6 216.1 %copy-start.23 = (bf16[2,64,2048]{2,1,0:T(8,128)(2,1)}, bf16[2,64,2048]{2,1,0:T(8,128)(2,1)S(1)}, u32[]{:S(2)}) copy-start(bf16[2,64,2048]{2,1,0:T(8,128)(2,1)S(1)} %fusion.207) | copy-start | bytes 1572868
  10.6 221.0 %copy-start.98 = (f32[16]{0:T(128)S(1)}, f32[16]{0:T(128)}, u32[]{:S(2)}) copy-start(f32[16]{0:T(128)} %param.23) | copy-start | bytes 196
  228.2 7.8 all-to-all-start
  233.8 12.0 collective-permute-start
  236.1 8.6 all-to-all-start.2
  254.4 18.8 all-to-all-start.3
  273.2 15.0 all-to-all-start.1
  288.2 13.4 all-to-all-start.4
  405.7 13.2 all-to-all-start.5
  409.3 330.9 %copy-start.86 = (f32[2,64]{1,0:T(2,128)}, f32[2,64]{1,0:T(2,128)S(1)}, u32[]{:S(2)}) copy-start(f32[2,64]{1,0:T(2,128)S(1)} %compare_convert_fusion) | copy-start | bytes 1540
  433.8 306.5 %copy-start.52 = (f32[2,64]{1,0:T(2,128)}, f32[2,64]{1,0:T(2,128)S(1)}, u32[]{:S(2)}) copy-start(f32[2,64]{1,0:T(2,128)S(1)} %fusion.250) | copy-start | bytes 1540
  555.0 145.5 %copy-start.35 = (bf16[2,64,2048]{2,1,0:T(8,128)(2,1)S(1)}, bf16[2,64,2048]{2,1,0:T(8,128)(2,1)}, u32[]{:S(2)}) copy-start(bf16[2,64,2048]{2,1,0:T(8,128)(2,1)} %param.29) | copy-start | bytes 1572868
  757.3 13.2 all-to-all-start.6
  1112.5 7.8 all-to-all-start.10
  1120.4 7.8 all-to-all-start.11
  1128.2 13.2 all-to-all-start.8
  1141.4 13.9 all-to-all-start.7
  1155.3 13.9 all-to-all-start.9
  1158.8 325.4 %all-reduce.18.cloned.1.call-start = ((), (), s32[]{:S(2)}) async-start(), calls=%async_computation.20 | async-start | bytes 2293760 | tf_op jit(solution)/shard_map/psum | solution.py:323
  1197.5 4.6 collective-permute-start.1
  1202.0 837.1 %reduce-scatter.3.cloned.1.call-start = ((), (), s32[]{:S(2)}) async-start(), calls=%async_computation.18 | async-start | bytes 69206016 | tf_op jit(solution)/shard_map/reduce_scatter | solution.py:311
  1230.0 2435.4 %reduce-scatter.5.cloned.1.call-start = ((), (), s32[]{:S(2)}) async-start(), calls=%async_computation.19 | async-start | bytes 160038912 | tf_op jit(solution)/shard_map/reduce_scatter | solution.py:243
  (221 other events, 1779.1 us)
Sparse Core Ops, SparseCore 0:
  10.9 200.0 all-gather.4
  213.8 84.0 all-gather.6
  300.8 254.0 all-gather.8
  557.7 142.7 all-gather.10
  1202.2 131.4 all-reduce.17
  1336.0 703.1 reduce-scatter.2
  2041.7 1623.7 reduce-scatter.4
where the time goes:
time: 3700 us; the launch traced here: 3680 us
  waiting for transfers between devices  2690 us (73%)
  matrix products  498 us (13%)
  other arithmetic  196 us (5%)
  local copies, waits for them, and re-layouts  177 us (5%)
  starting transfers between devices  46.8 us (1%)
  blocking collectives  45.9 us (1%)
    reduce_scatter x1, waiting for transfers between devices, shards(): lax.psum_scatter(jnp.concatenate([in_term, down_term, out_term], axis=1),...  1620 us
    reduce_scatter x1, waiting for transfers between devices, shards(): lax.psum_scatter(jnp.einsum('tr,tc->rc', flat_normed, flat_proj_main, pre...  554 us
    all_gather x1, waiting for transfers between devices, shards(): lax.all_gather(mix_weight, ('dp', 'seq'), axis=0, tiled=True)  200 us
    all_gather x1, waiting for transfers between devices, shards(): lax.all_gather(mlp_out_weight, ('dp', 'seq'), axis=0, tiled=True)  125 us
    all_gather x1, waiting for transfers between devices, shards(): lax.all_gather(mlp_in_weight, ('dp', 'seq'), axis=0, tiled=True)  121 us
    concatenate x1, other arithmetic, shards(): jnp.concatenate([in_term, down_term, out_term], axis=1)  109 us
  transfers between devices with their start and end apart: 21, of which 15 were waited for; matrix products, arithmetic and copies ran while one was open for 12% of the time, Pallas kernels for 0%

commit v1 on v0

v1 whole, which is shorter than its diff:
```python
from functools import partial

import jax
import jax.numpy as jnp
from jax import lax
from jax.experimental import pallas as pl
from jax.experimental.pallas import tpu as pltpu
from jax.sharding import PartitionSpec as P

eps_norm = 1e-05
eps_key = 1e-06
LANES = 128
PAIR = 2
f32 = jnp.float32
low = jnp.bfloat16


def rms_scale(rows_in, gain):
    return (
        rows_in * lax.rsqrt(jnp.mean(rows_in * rows_in, axis=-1, keepdims=True) + eps_norm) * gain
    )


def swiglu(gate_up):
    hidden_units = gate_up.shape[-1] // 2
    return jax.nn.silu(gate_up[..., :hidden_units]) * gate_up[..., hidden_units:]


def mm(left, right):
    return jnp.dot(left.astype(low), right.astype(low), preferred_element_type=f32)


def mm_nt(left, right):
    return lax.dot_general(
        left.astype(low), right.astype(low), (((1,), (1,)), ((), ())), preferred_element_type=f32
    )


def halves(v):
    if isinstance(v, tuple):
        return v
    if v.dtype == low:
        return (v,)
    top = v.astype(low)
    return top, (v - top.astype(f32)).astype(low)


def dot_fine(left, right, dims):
    left, right = halves(left), halves(right)
    total = None
    for i, a in enumerate(left):
        for j, b in enumerate(right):
            if i + j < 2:
                term = lax.dot_general(a, b, (dims, ((), ())), preferred_element_type=f32)
                total = term if total is None else total + term
    return total


def fine(left, right):
    return dot_fine(left, right, ((1,), (0,)))


def fine_nt(left, right):
    return dot_fine(left, right, ((1,), (1,)))


def mm_exact(left, right):
    return jnp.dot(left, right, precision=lax.Precision.HIGHEST, preferred_element_type=f32)


def softplus(v):
    return jnp.maximum(v, 0.0) + jnp.log1p(jnp.exp(-jnp.abs(v)))


def grid_of(size):
    row = lax.broadcasted_iota(jnp.int32, (size, size), 0)
    col = lax.broadcasted_iota(jnp.int32, (size, size), 1)
    return row, col


def lower_inverses(parts, row, col):
    size = parts[0].shape[0]
    joined = (row // 2 == col // 2) & (row > col)
    unit = (row == col).astype(f32)
    inverses = [unit - jnp.where(joined, part, 0.0) for part in parts]
    width = 2
    while width < size:
        joined = (row // (2 * width) == col // (2 * width)) & (row // width > col // width)
        corners = [jnp.where(joined, part, 0.0) for part in parts]
        moved = [mm(corner, inverse) for corner, inverse in zip(corners, inverses)]
        steps = [mm(inverse, move) for inverse, move in zip(inverses, moved)]
        inverses = [inverse - change for inverse, change in zip(inverses, steps)]
        width *= 2
    return inverses


def fill_taps(ext, slot, m, proj, pos, prev, first, qkv):
    rows = proj.shape[2]
    ext[slot, 8 : 8 + rows, :] = proj[pos, m, :, :qkv].astype(f32)
    tail = proj[prev, m, rows - 16 :, :qkv].astype(f32)[8:]
    ext[slot, 0:8, :] = jnp.where(first, 0.0, tail)


def conv_rows(ext, m, conv, rows):
    taps = conv.shape[0]
    total = conv[0:1, :] * ext[m, 9 - taps : 9 - taps + rows, :]
    for j in range(1, taps):
        total = total + conv[j : j + 1, :] * ext[m, 9 - taps + j : 9 - taps + j + rows, :]
    return total


def forward_kernel(
    local_heads,
    perm,
    proj,
    logit,
    conv,
    rates,
    gain,
    mixed,
    heads_out,
    qkv_out,
    gates,
    inv_t,
    weighted_t,
    fresh,
    states,
    ext,
    targets,
    weighted,
    scores,
    keys_t,
    state,
):
    blocks, micro, rows, _ = proj.shape
    cols = local_heads * LANES
    qkv = 3 * cols
    row, col = grid_of(rows)
    upto = (row >= col).astype(f32)
    lane = lax.broadcasted_iota(jnp.int32, (rows, LANES), 1)
    scale = float(LANES) ** -0.5

    def prepare(i, carry):
        work = []
        for part in range(PAIR):
            b = i * PAIR + part
            pos, prev = perm[b], perm[jnp.maximum(b - 1, 0)]
            for m in range(micro):
                slot = part * micro + m
                fill_taps(ext, slot, m, proj, pos, prev, b == 0, qkv)
                conv_out = conv_rows(ext, slot, conv, rows)
                act = conv_out * jax.nn.sigmoid(conv_out)
                logits = logit[pos, m].astype(f32)
                decay = -rates[...] * softplus(logits)
                strength = jax.nn.sigmoid(logits)
                total = mm_exact(upto, decay)
                total_t = total.T
                gates[b, m] = jnp.where(lane < local_heads, total, strength)
                growth = jnp.exp(total)
                fade = jnp.exp(total[rows - 1 : rows, :] - total)
                for h in range(local_heads):
                    raw_q = act[:, h * LANES : (h + 1) * LANES]
                    raw_k = act[:, cols + h * LANES : cols + (h + 1) * LANES]
                    q = raw_q * (
                        lax.rsqrt(jnp.sum(raw_q * raw_q, axis=1, keepdims=True) + eps_key) * scale
                    )
                    k = raw_k * lax.rsqrt(jnp.sum(raw_k * raw_k, axis=1, keepdims=True) + eps_key)
                    q = q.astype(low)
                    k = k.astype(low)
                    v = act[:, 2 * cols + h * LANES : 2 * cols + (h + 1) * LANES].astype(low)
                    qkv_out[b, m, :, h * LANES : (h + 1) * LANES] = q
                    qkv_out[b, m, :, cols + h * LANES : cols + (h + 1) * LANES] = k
                    qkv_out[b, m, :, 2 * cols + h * LANES : 2 * cols + (h + 1) * LANES] = v
                    beta = strength[:, local_heads + h : local_heads + h + 1]
                    spread = jnp.exp(
                        jnp.minimum(total[:, h : h + 1] - total_t[h : h + 1, :], 0.0)
                    )
                    work.append(
                        (b, m * local_heads + h, q, k, v, beta, spread, growth[:, h : h + 1], fade[:, h : h + 1])
                    )
        same = [mm_nt(k, k) for _, _, _, k, *_ in work]
        cross = [mm_nt(q, k) for _, _, q, k, *_ in work]
        parts = [
            jnp.where(row > col, item[6] * item[5] * dots, 0.0) for item, dots in zip(work, same)
        ]
        inverses = lower_inverses(parts, row, col)
        keyed = [fine(inv, item[3].astype(f32) * (item[5] * item[7])) for inv, item in zip(inverses, work)]
        valued = [fine(inv, item[4].astype(f32) * item[5]) for inv, item in zip(inverses, work)]
        for n, (b, p, q, k, v, beta, spread, grow, shrink) in enumerate(work):
            inv_t[b, p] = inverses[n].T
            weighted[b, p] = keyed[n]
            weighted_t[b, p] = keyed[n].T
            targets[b, p] = valued[n]
            scores[b, p] = upto * spread * cross[n]
            keys_t[b, p] = (k.astype(f32) * shrink).T
        return carry

    lax.fori_loop(0, blocks // PAIR, prepare, 0)
    state[...] = jnp.zeros_like(state)

    def step(b, carry):
        pos = perm[b]
        growth = [jnp.exp(gates[b, m]) for m in range(micro)]
        chains = [(m, h, m * local_heads + h) for m in range(micro) for h in range(local_heads)]
        now = [state[p] for _, _, p in chains]
        now_halves = [halves(v) for v in now]
        new = [
            targets[b, p] - fine(weighted[b, p], parts) for (_, _, p), parts in zip(chains, now_halves)
        ]
        new_halves = [halves(v) for v in new]
        moved = [fine(keys_t[b, p], parts) for (_, _, p), parts in zip(chains, new_halves)]
        for (m, h, p), old, fed in zip(chains, now, moved):
            states[b, p] = old
            state[p] = growth[m][rows - 1 : rows, h : h + 1] * old + fed
        outs = []
        for (m, h, p), fill, parts in zip(chains, new_halves, now_halves):
            q = qkv_out[b, m, :, h * LANES : (h + 1) * LANES].astype(f32)
            outs.append(fine(q * growth[m][:, h : h + 1], parts) + fine(scores[b, p], fill))
        for (m, h, p), fill, out in zip(chains, new, outs):
            fresh[b, p] = fill
            out = out.astype(low)
            heads_out[b, m, :, h * LANES : (h + 1) * LANES] = out
            out = out.astype(f32)
            gate = proj[pos, m, :, 3 * cols + h * LANES : 3 * cols + (h + 1) * LANES].astype(f32)
            normed = out * lax.rsqrt(jnp.mean(out * out, axis=1, keepdims=True) + eps_norm) * gain[...]
            mixed[pos, m, :, h * LANES : (h + 1) * LANES] = (
                normed * (gate * jax.nn.sigmoid(gate))
            ).astype(low)
        return carry

    lax.fori_loop(0, blocks, step, 0)


def backward_kernel(
    local_heads,
    perm,
    grad_mixed,
    proj,
    logit,
    conv,
    rates,
    gain,
    heads_out,
    qkv_in,
    gates,
    inv_t,
    weighted_t,
    fresh,
    states,
    grad_proj,
    grad_logit,
    grad_conv,
    grad_rates,
    grad_gain,
    ext,
    dext,
    ahead,
    conv_sum,
    grad_out,
    value_part,
    state_part,
    grad_fresh,
    grad_states,
    grad_state,
):
    blocks, micro, rows, _ = proj.shape
    cols = local_heads * LANES
    qkv = 3 * cols
    taps = conv.shape[0]
    row, col = grid_of(rows)
    lane = lax.broadcasted_iota(jnp.int32, (rows, LANES), 1)
    last = lax.broadcasted_iota(jnp.int32, (rows, 1), 0) == rows - 1
    scale = float(LANES) ** -0.5
    upto_t = (col >= row).astype(f32)
    grad_gain[...] = jnp.zeros_like(grad_gain)
    grad_rates[...] = jnp.zeros_like(grad_rates)
    conv_sum[...] = jnp.zeros_like(conv_sum)
    ahead[...] = jnp.zeros_like(ahead)
    grad_state[...] = jnp.zeros_like(grad_state)

    def prepare(b, carry):
        pos = perm[b]
        work = []
        for m in range(micro):
            total = gates[b, m]
            growth = jnp.exp(total)
            total_t = total.T
            for h in range(local_heads):
                p = m * local_heads + h
                here = slice(h * LANES, (h + 1) * LANES)
                out = heads_out[b, m, :, here].astype(f32)
                gate = proj[pos, m, :, 3 * cols + h * LANES : 3 * cols + (h + 1) * LANES].astype(f32)
                dmixed = grad_mixed[pos, m, :, here].astype(f32)
                root = lax.rsqrt(jnp.mean(out * out, axis=1, keepdims=True) + eps_norm)
                unit = out * root
                sig = jax.nn.sigmoid(gate)
                dnormed = dmixed * (gate * sig)
                grad_proj[pos, m, :, 3 * cols + h * LANES : 3 * cols + (h + 1) * LANES] = (
                    dmixed * (unit * gain[...]) * (sig * (1.0 + gate * (1.0 - sig)))
                ).astype(low)
                grad_gain[...] += jnp.sum(dnormed * unit, axis=0, keepdims=True)
                dunit = dnormed * gain[...]
                dout = root * (dunit - unit * jnp.mean(unit * dunit, axis=1, keepdims=True))
                dout = dout.astype(low)
                grad_out[b, p] = dout.astype(grad_out.dtype)
                q = qkv_in[b, m, :, here]
                k = qkv_in[b, m, :, cols + h * LANES : cols + (h + 1) * LANES]
                spread_t = jnp.exp(jnp.minimum(total_t[h : h + 1, :] - total[:, h : h + 1], 0.0))
                grown_t = (q.astype(f32) * growth[:, h : h + 1]).T
                work.append((p, q, k, dout, upto_t * spread_t, grown_t))
        dots = [mm_nt(k, q) for _, q, k, *_ in work]
        parts = [fine(spread * dot, dout) for (_, _, _, dout, spread, _), dot in zip(work, dots)]
        fed = [fine(grown_t, dout) for _, _, _, dout, _, grown_t in work]
        for (p, *_), part, feed in zip(work, parts, fed):
            value_part[b, p] = part
            state_part[b, p] = feed
        return carry

    lax.fori_loop(0, blocks, prepare, 0)

    def step(i, carry):
        b = blocks - 1 - i
        chains = [(m, h, m * local_heads + h) for m in range(micro) for h in range(local_heads)]
        total = [gates[b, m] for m in range(micro)]
        fade = [jnp.exp(v[rows - 1 : rows, :] - v) for v in total]
        later = [grad_state[p] for _, _, p in chains]
        dnew = []
        for (m, h, p), grad in zip(chains, later):
            k = qkv_in[b, m, :, cols + h * LANES : cols + (h + 1) * LANES].astype(f32)
            dnew.append(value_part[b, p] + fine(k * fade[m][:, h : h + 1], grad))
        moved = [fine(weighted_t[b, p], grad) for (_, _, p), grad in zip(chains, dnew)]
        for (m, h, p), grad, fill, move in zip(chains, later, dnew, moved):
            grad_states[b, p] = grad
            grad_fresh[b, p] = fill
            carried = jnp.exp(total[m][rows - 1 : rows, h : h + 1])
            grad_state[p] = state_part[b, p] + carried * grad - move
        return carry

    lax.fori_loop(0, blocks, step, 0)

    def finish(i, carry):
        b = blocks - 1 - i
        pos, prev = perm[b], perm[jnp.maximum(b - 1, 0)]
        work = []
        for m in range(micro):
            total = gates[b, m]
            total_t = total.T
            growth = jnp.exp(total)
            fade = jnp.exp(total[rows - 1 : rows, :] - total)
            for h in range(local_heads):
                p = m * local_heads + h
                q = qkv_in[b, m, :, h * LANES : (h + 1) * LANES]
                k = qkv_in[b, m, :, cols + h * LANES : cols + (h + 1) * LANES]
                v = qkv_in[b, m, :, 2 * cols + h * LANES : 2 * cols + (h + 1) * LANES]
                beta = total[:, local_heads + h : local_heads + h + 1]
                spread = jnp.exp(jnp.minimum(total[:, h : h + 1] - total_t[h : h + 1, :], 0.0))
                work.append(
                    (p, q, k, v, beta, spread, growth[:, h : h + 1], fade[:, h : h + 1], growth[rows - 1 : rows, h : h + 1])
                )
        number = range(len(work))
        queries = [item[1] for item in work]
        keys = [item[2] for item in work]
        douts = [grad_out[b, item[0]].astype(low) for item in work]
        news = [halves(fresh[b, item[0]]) for item in work]
        nows = [halves(states[b, item[0]]) for item in work]
        laters = [halves(grad_states[b, item[0]]) for item in work]
        dright = [fine(inv_t[b, item[0]], grad_fresh[b, item[0]]) for item in work]
        dgrown = [fine_nt(douts[n], nows[n]) for n in number]
        dshrunk = [fine_nt(news[n], laters[n]) for n in number]
        dots = [mm_nt(queries[n], keys[n]) for n in number]
        same = [mm_nt(keys[n], keys[n]) for n in number]
        dscores = [fine_nt(douts[n], news[n]) for n in number]
        dright_halves = [halves(v) for v in dright]
        dweighted = [-fine_nt(dright_halves[n], nows[n]) for n in number]
        dbelow = [fine_nt(dright_halves[n], news[n]) for n in number]
        keyed, moved = [], []
        for n in number:
            beta, spread = work[n][4], work[n][5]
            dscores[n] = dscores[n] * jnp.where(row >= col, spread, 0.0)
            dbelow[n] = dbelow[n] * jnp.where(row > col, -spread, 0.0)
            keyed.append(dbelow[n] * same[n])
            moved.append(dscores[n] * dots[n] + keyed[n] * beta)
            dbelow[n] = dbelow[n] * beta
        dq = [fine(dscores[n], keys[n]) for n in number]
        dk = [fine(dscores[n].T, queries[n]) for n in number]
        dk_same = [fine(dbelow[n] + dbelow[n].T, keys[n]) for n in number]
        for m in range(micro):
            fill_taps(ext, m, m, proj, pos, prev, b == 0, qkv)
            conv_out = conv_rows(ext, m, conv, rows)
            sig = jax.nn.sigmoid(conv_out)
            act = conv_out * sig
            slope = sig * (1.0 + conv_out * (1.0 - sig))
            dtotal = jnp.zeros((rows, LANES), f32)
            dstrength = jnp.zeros((rows, LANES), f32)
            for h in range(local_heads):
                n = m * local_heads + h
                p, q, k, v, beta, spread, grow, shrink, carried = work[n]
                q32, k32, v32 = q.astype(f32), k.astype(f32), v.astype(f32)
                dquery = grow * dgrown[n] + dq[n]
                dkey = (beta * grow) * dweighted[n] + shrink * dshrunk[n] + dk[n] + dk_same[n]
                dvalue = beta * dright[n]
                weighed = dweighted[n] * k32 * grow
                shrunk = dshrunk[n] * k32 * shrink
                dstr = jnp.sum(dright[n] * v32 + weighed, axis=1, keepdims=True) + jnp.sum(
                    keyed[n], axis=1, keepdims=True
                )
                dtot = jnp.sum(
                    dgrown[n] * q32 * grow + weighed * beta - shrunk, axis=1, keepdims=True
                ) + jnp.sum(moved[n] - moved[n].T, axis=1, keepdims=True)
                end = jnp.sum(shrunk) + jnp.sum(carried * (states[b, p] * grad_states[b, p]))
                dtot = dtot + jnp.where(last, end, 0.0)
                dtotal = dtotal + jnp.where(lane == h, dtot, 0.0)
                dstrength = dstrength + jnp.where(lane == local_heads + h, dstr, 0.0)
                for part, grad in ((0, dquery), (1, dkey), (2, dvalue)):
                    at = part * cols + h * LANES
                    grad = grad.astype(low).astype(f32)
                    if part == 0:
                        grad = grad * scale
                    if part < 2:
                        raw = act[:, at : at + LANES]
                        root = lax.rsqrt(jnp.sum(raw * raw, axis=1, keepdims=True) + eps_key)
                        unit = raw * root
                        grad = root * (grad - unit * jnp.sum(unit * grad, axis=1, keepdims=True))
                    dext[m, 0:rows, at : at + LANES] = grad * slope[:, at : at + LANES]
            dext[m, rows : rows + 8, :] = ahead[m]
            dconv = dext[m, 0:rows, :]
            ahead[m] = dconv[0:8, :]
            du = conv[taps - 1 : taps, :] * dconv
            for j in range(taps - 1):
                du = du + conv[j : j + 1, :] * dext[m, taps - 1 - j : taps - 1 - j + rows, :]
            grad_proj[pos, m, :, :qkv] = du.astype(low)
            for j in range(taps):
                term = dconv * ext[m, 9 - taps + j : 9 - taps + j + rows, :]
                conv_sum[j] += jnp.sum(term.reshape(rows // 8, 8, qkv), axis=0)
            logits = logit[pos, m].astype(f32)
            ddecay = mm_exact(upto_t, dtotal)
            strength = gates[b, m]
            dlogit = jnp.where(
                lane < local_heads,
                -rates[...] * jax.nn.sigmoid(logits) * ddecay,
                strength * (1.0 - strength) * dstrength,
            )
            grad_logit[pos, m] = jnp.where(lane < 2 * local_heads, dlogit, 0.0).astype(low)
            grad_rates[...] -= jnp.sum(softplus(logits) * ddecay, axis=0, keepdims=True)
        return carry

    lax.fori_loop(0, blocks, finish, 0)
    for j in range(taps):
        grad_conv[j : j + 1, :] = jnp.sum(conv_sum[j], axis=0, keepdims=True)


def in_vmem():
    return pl.BlockSpec(memory_space=pltpu.VMEM)


def heads_forward(perm, proj, logit, conv, rates, gain, local_heads):
    blocks, micro, rows, _ = proj.shape
    cols = local_heads * LANES
    chains = micro * local_heads

    def shape(dims, kind):
        return jax.ShapeDtypeStruct(dims, kind)

    return pl.pallas_call(
        partial(forward_kernel, local_heads),
        out_shape=(
            shape((blocks, micro, rows, cols), low),
            shape((blocks, micro, rows, cols), low),
            shape((blocks, micro, rows, 3 * cols), low),
            shape((blocks, micro, rows, LANES), f32),
            shape((blocks, chains, rows, rows), f32),
            shape((blocks, chains, LANES, rows), f32),
            shape((blocks, chains, rows, LANES), f32),
            shape((blocks, chains, LANES, LANES), f32),
        ),
        in_specs=[pl.BlockSpec(memory_space=pltpu.SMEM)] + [in_vmem()] * 5,
        out_specs=(in_vmem(),) * 8,
        scratch_shapes=[
            pltpu.VMEM((PAIR * micro, rows + 8, 3 * cols), f32),
            pltpu.VMEM((blocks, chains, rows, LANES), f32),
            pltpu.VMEM((blocks, chains, rows, LANES), f32),
            pltpu.VMEM((blocks, chains, rows, rows), f32),
            pltpu.VMEM((blocks, chains, LANES, rows), f32),
            pltpu.VMEM((chains, LANES, LANES), f32),
        ],
        compiler_params=pltpu.CompilerParams(vmem_limit_bytes=50 * 1024 * 1024),
        name="heads_forward",
    )(perm, proj, logit, conv, rates, gain)


def heads_backward(perm, grad_mixed, proj, logit, conv, rates, gain, kept, local_heads):
    blocks, micro, rows, wide = proj.shape
    cols = local_heads * LANES
    chains = micro * local_heads
    taps = conv.shape[0]

    def shape(dims, kind):
        return jax.ShapeDtypeStruct(dims, kind)

    return pl.pallas_call(
        partial(backward_kernel, local_heads),
        out_shape=(
            shape((blocks, micro, rows, wide), low),
            shape((blocks, micro, rows, LANES), low),
            shape((taps, 3 * cols), f32),
            shape((1, LANES), f32),
            shape((1, LANES), f32),
        ),
        in_specs=[pl.BlockSpec(memory_space=pltpu.SMEM)] + [in_vmem()] * 13,
        out_specs=(in_vmem(),) * 5,
        scratch_shapes=[
            pltpu.VMEM((micro, rows + 8, 3 * cols), f32),
            pltpu.VMEM((micro, rows + 8, 3 * cols), f32),
            pltpu.VMEM((micro, 8, 3 * cols), f32),
            pltpu.VMEM((taps, 8, 3 * cols), f32),
            pltpu.VMEM((blocks, chains, rows, LANES), f32),
            pltpu.VMEM((blocks, chains, rows, LANES), f32),
            pltpu.VMEM((blocks, chains, LANES, LANES), f32),
            pltpu.VMEM((blocks, chains, rows, LANES), f32),
            pltpu.VMEM((blocks, chains, LANES, LANES), f32),
            pltpu.VMEM((chains, LANES, LANES), f32),
        ],
        compiler_params=pltpu.CompilerParams(vmem_limit_bytes=50 * 1024 * 1024),
        name="heads_backward",
    )(perm, grad_mixed, proj, logit, conv, rates, gain, *kept)


both = ("dp", "seq")


def swap(value, axis, bit):
    return lax.ppermute(value, axis, [(i, i ^ bit) for i in range(lax.axis_size(axis))])


def after(value, *others):
    return lax.optimization_barrier((value, *others))[0]


def gather_places():
    peers = lax.axis_size("seq")
    place = jnp.arange(peers, dtype=jnp.int32)
    if peers != 8:
        return place
    place = place ^ lax.axis_index("seq").astype(jnp.int32)
    return place // 2 + 4 * (place % 2)


def gather_seq(rows_in):
    if lax.axis_size("seq") != 8:
        return lax.all_gather(rows_in, "seq", axis=0, tiled=True)
    half = rows_in.shape[0] // 2
    top, bottom = rows_in[:half], rows_in[half:]
    top_x, bottom_y = swap(top, "seq", 2), swap(bottom, "seq", 4)
    top_y = swap(jnp.concatenate([top, top_x]), "seq", 4)
    bottom_x = swap(jnp.concatenate([bottom, bottom_y]), "seq", 2)
    near = jnp.concatenate(
        [top, bottom, top_x, bottom_x[:half], top_y[:half], bottom_y, top_y[half:], bottom_x[half:]]
    )
    return jnp.concatenate([near, swap(near, "seq", 1)])


def scatter_seq(partial_rows):
    peers = lax.axis_size("seq")
    if peers != 8:
        return lax.psum_scatter(
            partial_rows.astype(low), "seq", scatter_dimension=0, tiled=True
        ).astype(f32)
    terms = partial_rows.astype(low).reshape(peers, -1, partial_rows.shape[-1])
    half = terms.shape[1] // 2
    near = terms[:4].astype(f32) + swap(terms[4:], "seq", 1).astype(f32)
    top, bottom = near[:, :half].astype(low), near[:, half:].astype(low)
    top_x = swap(top[1::2], "seq", 2)
    bottom_y = swap(bottom[2:], "seq", 4)
    top = near[0::2, :half] + top_x.astype(f32)
    bottom = near[:2, half:] + bottom_y.astype(f32)
    top_y = swap(top[1].astype(low), "seq", 4)
    bottom_x = swap(bottom[1].astype(low), "seq", 2)
    return jnp.concatenate([top[0] + top_y.astype(f32), bottom[0] + bottom_x.astype(f32)])


def sum_all(value):
    for axis in both:
        bit = 1
        while bit < lax.axis_size(axis):
            value = value + swap(value, axis, bit)
            bit *= 2
    return value


def gather_dp_small(value):
    groups = lax.axis_size("dp")
    parts, bit = value[None], 1
    while bit < groups:
        parts = jnp.concatenate([parts, swap(parts, "dp", bit)])
        bit *= 2
    places = jnp.arange(groups, dtype=jnp.int32) ^ lax.axis_index("dp").astype(jnp.int32)
    return jnp.take(parts, places, axis=0)


def to_columns(pieces):
    rows_here = lax.all_to_all(pieces, "seq", split_axis=0, concat_axis=0, tiled=True)
    return rows_here.reshape(-1, pieces.shape[-1])


def gather_dp(rows_here):
    return lax.all_gather(rows_here, "dp", axis=0, tiled=True)


def columns_back(term):
    peers = lax.axis_size("seq")
    own = lax.psum_scatter(term.astype(low), "dp", scatter_dimension=0, tiled=True)
    own = own.reshape(peers, own.shape[0] // peers, own.shape[1])
    return lax.all_to_all(own, "seq", split_axis=0, concat_axis=0, tiled=True).transpose(1, 0, 2)


def row_pairs(inverse):
    groups, peers = lax.axis_size("dp"), lax.axis_size("seq")
    pairs = [(j * groups + d, d * peers + j) for d in range(groups) for j in range(peers)]
    return [(b, a) for a, b in pairs] if inverse else pairs


def dot32(left, right):
    return jnp.dot(left, right, preferred_element_type=f32)


def dot_t(left, right):
    return lax.dot_general(left, right, (((1,), (1,)), ((), ())), preferred_element_type=f32)


def t_dot(left, right):
    return lax.dot_general(left, right, (((0,), (0,)), ((), ())), preferred_element_type=f32)


def shards(
    tokens,
    lengths,
    norm_gain,
    mix_weight,
    conv_weight,
    decay_rate,
    out_gain,
    out_weight,
    mlp_gain,
    mlp_in_weight,
    mlp_out_weight,
    grad_out,
):
    micro, seq_rows, width = tokens.shape
    heads = decay_rate.shape[0]
    groups = lax.axis_size("dp")
    peers = lax.axis_size("seq")
    here = lax.axis_index("seq")
    local_heads = heads // peers
    taps = conv_weight.shape[0]
    units = mlp_out_weight.shape[1]
    local_units = units // peers
    own_rows = mix_weight.shape[0]
    cols = width // peers
    logit_cols = 2 * local_heads

    positions = here * seq_rows + lax.broadcasted_iota(jnp.int32, (micro, seq_rows), 1)
    valid = (positions < lengths[:, None]).astype(f32).reshape(-1, 1)
    inputs = tokens.reshape(-1, width).astype(f32)

    main = mix_weight[:, : 4 * width].reshape(own_rows, 4, peers, cols)
    logits = mix_weight[:, 4 * width :].reshape(own_rows, 2, peers, local_heads)
    mix_rows = to_columns(
        jnp.concatenate(
            [
                main.transpose(2, 0, 1, 3).reshape(peers, own_rows, 4 * cols),
                logits.transpose(2, 0, 1, 3).reshape(peers, own_rows, logit_cols),
                jnp.zeros((peers, own_rows, LANES - logit_cols), low),
            ],
            axis=2,
        )
    )
    mix_here = gather_dp(mix_rows[:, : 4 * cols])
    logit_here = gather_dp_small(mix_rows[:, 4 * cols :]).reshape(width, LANES)
    normed, norm_back = jax.vjp(rms_scale, inputs, norm_gain)
    normed_all = gather_seq(normed.astype(low))
    in_pieces = mlp_in_weight.reshape(own_rows, 2, peers, local_units).transpose(2, 0, 1, 3)
    in_rows = to_columns(
        after(in_pieces.reshape(peers, own_rows, 2 * local_units), mix_rows)
    )
    down_rows = to_columns(
        after(mlp_out_weight.reshape(own_rows, peers, local_units).transpose(1, 0, 2), mix_rows)
    )
    out_rows = lax.ppermute(after(out_weight, mix_rows), both, row_pairs(False))
    mix_here, in_rows, down_rows, out_rows = lax.optimization_barrier(
        (mix_here, in_rows, down_rows, out_rows)
    )
    out_here = gather_dp(out_rows)
    in_here = gather_dp(in_rows)
    down_here = gather_dp(down_rows)

    projected = dot32(normed_all, mix_here).astype(low).reshape(peers, micro, seq_rows, -1)
    logit_pre = dot32(normed_all, logit_here).astype(low).reshape(peers, micro, seq_rows, LANES)
    conv_here = lax.dynamic_index_in_dim(
        conv_weight.reshape(taps, 3, peers, cols), here, 2, keepdims=False
    ).reshape(taps, 3 * cols)
    rates_here = lax.dynamic_slice_in_dim(decay_rate, here * local_heads, local_heads)
    rate_lanes = jnp.pad(rates_here, (0, LANES - local_heads)).reshape(1, LANES)
    gain_row = out_gain.reshape(1, LANES)
    places = gather_places()
    mixed_rows, *kept = heads_forward(
        places, projected, logit_pre, conv_here, rate_lanes, gain_row, local_heads
    )
    mixed_low = mixed_rows.reshape(-1, cols)
    hidden = inputs + scatter_seq(dot32(mixed_low, out_here))

    second, second_back = jax.vjp(rms_scale, hidden, mlp_gain)
    second_all = gather_seq(second.astype(low))
    cotangent = valid * grad_out.reshape(-1, width).astype(f32)
    cot_all = gather_seq(after(cotangent.astype(low), second_all))
    gate_up = dot32(second_all, in_here).astype(low)
    activated, swiglu_back = jax.vjp(swiglu, gate_up.astype(f32))
    activated_low = activated.astype(low)
    (grad_gate_up,) = swiglu_back(dot32(cot_all, down_here))
    grad_gate_low = grad_gate_up.astype(low)
    grad_second = scatter_seq(dot_t(grad_gate_low, in_here))
    grad_hidden_norm, grad_mlp_gain = second_back(grad_second)
    grad_hidden = cotangent + grad_hidden_norm
    branch_all = gather_seq(grad_hidden.astype(low))
    grad_in = columns_back(t_dot(second_all, grad_gate_low))
    grad_down = columns_back(t_dot(cot_all, activated_low))

    grad_mixed = dot_t(branch_all, out_here).reshape(peers, micro, seq_rows, cols)
    grad_out_own = lax.ppermute(
        lax.psum_scatter(
            t_dot(mixed_low, branch_all).astype(low), "dp", scatter_dimension=0, tiled=True
        ),
        both,
        row_pairs(True),
    )
    grad_projected, grad_logits, grad_conv, rate_sums, gain_sums = heads_backward(
        places, grad_mixed, projected, logit_pre, conv_here, rate_lanes, gain_row, kept, local_heads
    )
    grad_projected = grad_projected.reshape(-1, 4 * cols)
    grad_logits = grad_logits.reshape(-1, LANES)
    grad_normed = scatter_seq(
        dot_t(grad_projected, mix_here) + dot_t(grad_logits, logit_here)
    )
    grad_inputs_norm, grad_norm_gain = norm_back(grad_normed)
    grad_tokens = grad_hidden + grad_inputs_norm
    grad_mix = columns_back(t_dot(normed_all, grad_projected))
    grad_mix_main = grad_mix.reshape(own_rows, peers, 4, cols).transpose(0, 2, 1, 3)
    logit_terms = t_dot(grad_logits[:, :logit_cols], normed_all)
    logit_terms = logit_terms.reshape(logit_cols, groups * peers, own_rows).transpose(1, 0, 2)
    logit_terms = lax.all_to_all(logit_terms, both, split_axis=0, concat_axis=0, tiled=True)
    logit_terms = logit_terms.reshape(groups, peers, 2, local_heads, own_rows).sum(0)
    grad_mix_logits = logit_terms.transpose(3, 1, 0, 2).reshape(own_rows, 2 * heads)

    feed_out = scatter_seq(dot_t(after(activated_low, grad_projected), down_here))
    result = (valid * (hidden + feed_out)).astype(low)

    conv_terms = lax.dynamic_update_slice(
        jnp.zeros((taps, 3, peers, cols), f32),
        grad_conv.reshape(taps, 3, 1, cols),
        (0, 0, here, 0),
    )
    rate_terms = lax.dynamic_update_slice(
        jnp.zeros((LANES,), f32), rate_sums[0, :local_heads], (here * local_heads,)
    )
    sizes = [width, width, LANES, LANES, taps * 3 * width]
    summed = sum_all(
        jnp.concatenate(
            [
                grad_norm_gain,
                grad_mlp_gain,
                gain_sums[0],
                rate_terms,
                conv_terms.reshape(-1),
            ]
        ).reshape(-1, LANES)
    ).reshape(-1)
    ends = [sum(sizes[: i + 1]) for i in range(len(sizes))]
    sums = [summed[end - size : end] for end, size in zip(ends, sizes)]
    return (
        result.reshape(tokens.shape),
        grad_tokens.reshape(tokens.shape),
        sums[0],
        jnp.concatenate(
            [grad_mix_main.reshape(own_rows, 4 * width).astype(f32), grad_mix_logits], axis=1
        ),
        sums[4].reshape(taps, 3 * width),
        sums[3][:heads],
        sums[2],
        grad_out_own.astype(f32),
        sums[1],
        grad_in.reshape(own_rows, peers, 2, local_units)
        .transpose(0, 2, 1, 3)
        .reshape(own_rows, 2 * units)
        .astype(f32),
        grad_down.reshape(own_rows, units).astype(f32),
    )


def solution(mesh):
    in_specs = (
        P("dp", "seq", None),
        P("dp"),
        P(),
        P(("dp", "seq"), None),
        P(),
        P(),
        P(),
        P(("dp", "seq"), None),
        P(),
        P(("dp", "seq"), None),
        P(("dp", "seq"), None),
        P("dp", "seq", None),
    )
    out_specs = (
        P("dp", "seq", None),
        P("dp", "seq", None),
        P(),
        P(("dp", "seq"), None),
        P(),
        P(),
        P(),
        P(("dp", "seq"), None),
        P(),
        P(("dp", "seq"), None),
        P(("dp", "seq"), None),
    )
    return jax.shard_map(shards, mesh=mesh, in_specs=in_specs, out_specs=out_specs, check_vma=False)
```

time: 3700 us -> 752 us (0.20)
  waiting for transfers between devices: 2690 us -> 275 us
  matrix products: 498 us -> 94.2 us
  other arithmetic: 196 us -> 48.9 us
  starting transfers between devices: 46.8 us -> 121 us
  Pallas kernels: 0 us -> 54.4 us
  blocking collectives: 45.9 us -> 0 us
  local copies, waits for them, and re-layouts: 177 us -> 134 us
    reduce_scatter x2 -> x4, waiting for transfers between devices: 2180 us -> 40.2 us  [the longest x3 40.2 us: columns_back(): lax.psum_scatter(term.astype(low), 'dp', scatter_dimension=0, tiled=True)]
    dot_general x565 -> x15, matrix products: 498 us -> 94.2 us  [the longest x5 34.1 us: t_dot(): lax.dot_general(left, right, (((0,), (0,)), ((), ())), preferred_element_...]
    all_gather x4, waiting for transfers between devices: 446 us -> 51.3 us  [gather_dp(): return lax.all_gather(rows_here, 'dp', axis=0, tiled=True)]
    ppermute x2 -> x49, waiting for transfers between devices: 0.01 us -> 159 us  [the longest x47 159 us: swap(): lax.ppermute(value, axis, [(i, i ^ bit) for i in range(lax.axis_size(axis...]
    concatenate x2 -> x15, other arithmetic: 112 us -> 11.3 us  [the longest x4 4.13 us: gather_seq(): top_y = swap(jnp.concatenate([top, top_x]), 'seq', 4)]
    ppermute x2 -> x49, starting transfers between devices: 3.75 us -> 92.9 us  [the longest x47 87.7 us: swap(): lax.ppermute(value, axis, [(i, i ^ bit) for i in range(lax.axis_size(axis...]
    pallas_call x0 -> x2, Pallas kernels: none -> 54.4 us  [the longest x1 32.3 us: heads_backward(): pl.pallas_call(partial(backward_kernel, local_heads), out_shape=(shape((b...]
    psum x1 -> x0, blocking collectives: 45.9 us -> none  [shards(): lax.psum((grad_norm_gain, grad_conv, rate_terms, grad_out_gain, grad_mlp_...]
  transfers between devices with their start and end apart: 21 -> 64, of which waited for: 15 -> 35; matrix products, arithmetic and copies ran while one was open for 12% -> 29% of each run, Pallas kernels for 0% -> 7%
where the time goes in v1:
time: 752 us; the launch traced here: 744 us
  waiting for transfers between devices  275 us (37%)
  local copies, waits for them, and re-layouts  134 us (18%)
  starting transfers between devices  121 us (16%)
  matrix products  94.2 us (13%)
  Pallas kernels  54.4 us (7%)
  other arithmetic  48.9 us (7%)
  between operations  15.9 us (2%)
    ppermute x47, waiting for transfers between devices, swap(): lax.ppermute(value, axis, [(i, i ^ bit) for i in range(lax.axis_size(axis...  159 us
    ppermute x47, starting transfers between devices, swap(): lax.ppermute(value, axis, [(i, i ^ bit) for i in range(lax.axis_size(axis...  87.7 us
    unnamed x158, local copies, waits for them, and re-layouts  55.2 us
    all_gather x4, waiting for transfers between devices, gather_dp(): return lax.all_gather(rows_here, 'dp', axis=0, tiled=True)  51.3 us
    reduce_scatter x3, waiting for transfers between devices, columns_back(): lax.psum_scatter(term.astype(low), 'dp', scatter_dimension=0, tiled=True)  40.2 us
    dot_general x5, matrix products, t_dot(): lax.dot_general(left, right, (((0,), (0,)), ((), ())), preferred_element_...  34.1 us
    dot_general x5, matrix products, dot32(): return jnp.dot(left, right, preferred_element_type=f32)  33.6 us
    pallas_call x1, Pallas kernels, heads_backward(): pl.pallas_call(partial(backward_kernel, local_heads), out_shape=(shape((b...  32.3 us
  transfers between devices with their start and end apart: 64, of which 35 were waited for; matrix products, arithmetic and copies ran while one was open for 29% of the time, Pallas kernels for 7%

profile of v1, /device:TPU:0, one launch (start us, length us, event | category | flops | bytes accessed | tf_op | source)
XLA Modules:
  0.0 743.7 jit_solution(14833224357953581017)
XLA Ops:
  12.2 5.2 all-to-all-start
  19.5 14.7 %all-to-all-done = bf16[8,64,1152]{2,1,0:T(8,128)(2,1)S(1)} async-done(((bf16[8,64,1152]{2,1,0:T(8,128)(2,1)}), bf16[8,64,1152]{2,1,0:T(8,128)(2,1)S(1)}, u32[]{:S(2)}, u32[]{:S(2)}) %all-to-all-start) | async-done | bytes 1179680 | tf_op jit(solution)/shard_map/all_to_all | solution.py:601
  37.5 7.1 collective-permute-done.1
  62.6 8.7 %collective-permute-done.3 = bf16[128,2048]{1,0:T(8,128)(2,1)S(1)} collective-permute-done((bf16[128,2048]{1,0:T(8,128)(2,1)S(1)}, bf16[128,2048]{1,0:T(8,128)(2,1)S(1)}, u32[]{:S(2)}, u32[]{:S(2)}) %collective-permute-start.3) | collective-permute-done | bytes 524320 | tf_op jit(solution)/shard_map/ppermute | solution.py:532
  82.1 9.4 %all-to-all-done.2 = bf16[8,64,704]{2,1,0:T(8,128)(2,1)S(1)} async-done(((bf16[8,64,704]{2,1,0:T(8,128)(2,1)}), bf16[8,64,704]{2,1,0:T(8,128)(2,1)S(1)}, u32[]{:S(2)}, u32[]{:S(2)}) %all-to-all-start.2) | async-done | bytes 720928 | tf_op jit(solution)/shard_map/all_to_all | solution.py:601
  105.7 26.5 %collective-permute-done.7 = bf16[2,512,128]{2,1,0:T(8,128)(2,1)S(1)} collective-permute-done((bf16[2,512,128]{2,1,0:T(8,128)(2,1)S(1)}, bf16[2,512,128]{2,1,0:T(8,128)(2,1)S(1)}, u32[]{:S(2)}, u32[]{:S(2)}) %collective-permute-start.7) | collective-permute-done | bytes 262176 | tf_op jit(solution)/shard_map/ppermute | solution.py:532
  141.3 5.7 convolution_convert_fusion.8
  147.0 22.1 %heads_forward.1 = (bf16[8,2,64,256]{3,2,1,0:T(8,128)(2,1)S(1)}, bf16[8,2,64,256]{3,2,1,0:T(8,128)(2,1)S(1)}, bf16[8,2,64,768]{3,2,1,0:T(8,128)(2,1)}, f32[8,2,6...) custom-call(s32[8]{0:T(128)S(1)} %fusion.36.perm, ...), custom_call_target="tpu_custom_call" | custom-call | tf_op jit(solution)/shard_map/heads_forward/pallas_call | solution.py:464
  182.2 6.2 collective-permute-start.11
  188.5 8.0 %collective-permute-done.9 = bf16[2,64,2048]{2,1,0:T(8,128)(2,1)} collective-permute-done((bf16[2,64,2048]{2,1,0:T(8,128)(2,1)}, bf16[2,64,2048]{2,1,0:T(8,128)(2,1)}, u32[]{:S(2)}, u32[]{:S(2)}) %collective-permute-start.9) | collective-permute-done | bytes 524320 | tf_op jit(solution)/shard_map/ppermute | solution.py:532
  229.9 7.1 collective-permute-done.15
  257.7 6.4 collective-permute-done.19
  271.6 7.2 collective-permute-done.20
  293.4 11.7 %fusion = f32[1024,1408]{1,0:T(8,128)} fusion(bf16[1024,2048]{1,0:T(8,128)(2,1)} %constant_dynamic-update-slice_fusion.10, bf16[2048,1408]{1,0:T(8,128)(2,1)} %all-gather.9.cloned.1.call-done), kind=kOutput, calls=%fused_computation.10 | convolution fusion | flops 5908463616 | bytes 15728640 | tf_op jit(solution)/shard_map/dot_general | solution.py:623
  308.2 48.5 %all-gather.11.cloned.1.call-done = bf16[2048,704]{1,0:T(8,128)(2,1)} async-done(((bf16[512,704]{1,0:T(8,128)(2,1)}), bf16[2048,704]{1,0:T(8,128)(2,1)}) %all-gather.11.cloned.1.call-update) | async-done | bytes 2883600 | tf_op jit(solution)/shard_map/all_gather | solution.py:606
  356.6 10.2 %fusion.23 = (f32[1024,704]{1,0:T(8,128)S(1)}, f32[1024,704]{1,0:T(8,128)S(1)}, bf16[1024,704]{1,0:T(8,128)(2,1)}) fusion(f32[1024,1408]{1,0:T(8,128)} %fusion, bf16[1024,2048]{1,0:T(8,128)(2,1)} %constant_dynamic-update-slice_fusion.17, bf16[2048,704]{1,0:T(8,128)(2,1)} %all-gather.11.cloned.1.call-done), kind=kOutput, calls=%fused_computation.106 | convolution fusion | flops 2962882560 | bytes 20054016 | tf_op jit(solution)/shard_map/dot_general | solution.py:623
  366.8 11.3 %convolution_convert_fusion.2 = bf16[1024,2048]{1,0:T(8,128)(2,1)S(1)} fusion(bf16[2048,1408]{1,0:T(8,128)(2,1)} %all-gather.9.cloned.1.call-done, f32[1024,704]{1,0:T(8,128)S(1)} %get-tuple-element.60, f32[1024,704]{1,0:T(8,128)S(1)} %get-tuple-element.59), kind=kOutput, calls=%fused_computation.11 | convolution fusion | flops 5910560768 | bytes 15728640 | tf_op jit(solution)/shard_map/dot_general | solution.py:627
  387.2 11.0 %collective-permute-done.24 = bf16[2,64,2048]{2,1,0:T(8,128)(2,1)S(1)} collective-permute-done((bf16[2,64,2048]{2,1,0:T(8,128)(2,1)S(1)}, bf16[2,64,2048]{2,1,0:T(8,128)(2,1)S(1)}, u32[]{:S(2)}, u32[]{:S(2)}) %collective-permute-start.24) | collective-permute-done | bytes 524320 | tf_op jit(solution)/shard_map/ppermute | solution.py:532
  413.9 7.0 convolution_convert_fusion.6
  424.2 6.3 collective-permute-done.28
  455.1 12.5 %convolution_convert_fusion = bf16[2048,1408]{1,0:T(8,128)(2,1)} fusion(bf16[1024,2048]{1,0:T(8,128)(2,1)} %constant_dynamic-update-slice_fusion.10, f32[1024,704]{1,0:T(8,128)} %copy-done.51, f32[1024,704]{1,0:T(8,128)} %copy-done.50), kind=kOutput, calls=%fused_computation.2 | convolution fusion | flops 5911347200 | bytes 15728640 | tf_op jit(solution)/shard_map/dot_general | solution.py:631
  473.4 32.3 %heads_backward.1 = (bf16[8,2,64,1024]{3,2,1,0:T(8,128)(2,1)}, bf16[8,2,64,128]{3,2,1,0:T(8,128)(2,1)S(1)}, f32[4,768]{1,0:T(4,128)S(1)}, f32[1,128]{1,0:T(1,128)S(1)}, f32[1,128]{1,0:T(1,128)S(1)}) custom-call(s32[8]{0:T(128)S(1)} %fusion.36.perm, f32[8,2,64,256]{3,2,1,0:T(8,128)S(1)} %bitcast.211, bf16[8,2,64,1024]{3,2,1,0:T(8,128)(2,1)} %bitcast.227, ...), custom_call_target="tpu_custom_call" | custom-call | tf_op jit(solution)/shard_map/heads_backward/pallas_call | solution.py:500
  512.9 6.5 add_convert_fusion
  535.1 9.5 %convolution_convert_fusion.5 = bf16[2048,1024]{1,0:T(8,128)(2,1)} fusion(bf16[1024,2048]{1,0:T(8,128)(2,1)} %constant_dynamic-update-slice_fusion.3, bf16[1024,1024]{1,0:T(8,128)(2,1)} %bitcast.255), kind=kOutput, calls=%fused_computation.14 | convolution fusion | flops 4297064448 | bytes 10485760 | tf_op jit(solution)/shard_map/dot_general | solution.py:631
  557.2 5.2 fusion.44
  579.7 6.6 collective-permute-done.39
  589.0 15.2 %collective-permute-start.42 = (bf16[64,2048]{1,0:T(8,128)(2,1)S(1)}, bf16[64,2048]{1,0:T(8,128)(2,1)S(1)}, u32[]{:S(2)}, u32[]{:S(2)}) collective-permute-start(bf16[64,2048]{1,0:T(8,128)(2,1)S(1)} %fusion.31), channel_id=1, source_target_pairs={{0,2},{1,3},{2,0},{3,1},{4,6},{5,7},{6,4},{7,5},{8,10},{9,11},{10,... | collective-permute-start | bytes 786440 | tf_op jit(solution)/shard_map/ppermute | solution.py:532
  609.1 15.2 %collective-permute-start.43 = (f32[226,128]{1,0:T(8,128)S(1)}, f32[226,128]{1,0:T(8,128)S(1)}, u32[]{:S(2)}, u32[]{:S(2)}) collective-permute-start(f32[226,128]{1,0:T(8,128)S(1)} %bitcast.244), channel_id=1, source_target_pairs={{0,8},{8,0},{16,24},{24,16},{1,9},{9,1},{17,25},{25,17},{2,10},{10... | collective-permute-start | bytes 347144 | tf_op jit(solution)/shard_map/ppermute | solution.py:532
  627.8 5.4 collective-permute-start.44
  646.1 13.7 %collective-permute-done.46 = f32[226,128]{1,0:T(8,128)S(1)} collective-permute-done((f32[226,128]{1,0:T(8,128)S(1)}, f32[226,128]{1,0:T(8,128)S(1)}, u32[]{:S(2)}, u32[]{:S(2)}) %collective-permute-start.46) | collective-permute-done | bytes 115744 | tf_op jit(solution)/shard_map/ppermute | solution.py:532
  665.2 40.2 %reduce-scatter.5.cloned.1.call-done = bf16[512,1024]{1,0:T(8,128)(2,1)} async-done(((bf16[2048,1024]{1,0:T(8,128)(2,1)}), bf16[512,1024]{1,0:T(8,128)(2,1)}) %reduce-scatter.5.cloned.1.call-update) | async-done | bytes 1048592 | tf_op jit(solution)/shard_map/reduce_scatter | solution.py:611
  717.3 5.5 copy.89
  (428 shorter events, 320.0 us)
Async XLA Ops:
  12.2 22.0 %all-to-all-start = ((bf16[8,64,1152]{2,1,0:T(8,128)(2,1)}), bf16[8,64,1152]{2,1,0:T(8,128)(2,1)S(1)}, u32[]{:S(2)}, u32[]{:S(2)}) async-start(bf16[8,64,1152]{2,1,0:T(8,128)(2,1)} %concatenate.100), calls=%async_computation | async-start | bytes 2359296 | tf_op jit(solution)/shard_map/all_to_all | solution.py:601
  17.4 115.9 %all-gather.5.cloned.1.call-start = ((), (), s32[]{:S(2)}) async-start(), calls=%async_computation.11 | async-start | bytes 5242880 | tf_op jit(solution)/shard_map/all_gather | solution.py:606
  36.1 21.5 %collective-permute-start = (bf16[64,2048]{1,0:T(8,128)(2,1)}, bf16[64,2048]{1,0:T(8,128)(2,1)}, u32[]{:S(2)}, u32[]{:S(2)}) collective-permute-start(bf16[64,2048]{1,0:T(8,128)(2,1)} %get-tuple-element.111), channel_id=1, source_target_pairs={{0,2},{1,3},{2,0},{3,1},{4,6},{5,7},{6,4},{7,5},{8,10},{9,11},{10,... | collective-permute-start | bytes 786440 | tf_op jit(solution)/shard_map/ppermute | solution.py:532
  75.4 58.1 %collective-permute-start.4 = (bf16[512,2048]{1,0:T(8,128)(2,1)}, bf16[512,2048]{1,0:T(8,128)(2,1)}, u32[]{:S(2)}, u32[]{:S(2)}) collective-permute-start(bf16[512,2048]{1,0:T(8,128)(2,1)} %get-tuple-element.106), channel_id=1, source_target_pairs={{0,1},{1,0},{2,3},{3,2},{4,5},{5,4},{6,7},{7,6},{8,9},{9,8},{10,11... | collective-permute-start | bytes 6291464 | tf_op jit(solution)/shard_map/ppermute | solution.py:532
  80.4 17.4 %collective-permute-start.6 = (bf16[1,512,128]{2,1,0:T(8,128)(2,1)S(1)}, bf16[1,512,128]{2,1,0:T(8,128)(2,1)S(1)}, u32[]{:S(2)}, u32[]{:S(2)}) collective-permute-start(bf16[1,512,128]{2,1,0:T(8,128)(2,1)S(1)} %slice_bitcast_fusion.8), channel_id=1, source_target_pairs={{0,8},{8,0},{16,24},{24,16},{1,9},{9,1},{17,25},{25,17},{2,10},{10... | collective-permute-start | bytes 393224 | tf_op jit(solution)/shard_map/ppermute | solution.py:532
  92.4 40.8 %all-to-all-start.1 = ((bf16[8,64,1408]{2,1,0:T(8,128)(2,1)}), bf16[8,64,1408]{2,1,0:T(8,128)(2,1)S(1)}, u32[]{:S(2)}, u32[]{:S(2)}) async-start(bf16[8,64,1408]{2,1,0:T(8,128)(2,1)} %reshape.376), calls=%async_computation.1 | async-start | bytes 2883584 | tf_op jit(solution)/shard_map/all_to_all | solution.py:601
  96.0 74.1 %all-gather.7.cloned.1.call-start = ((), (), s32[]{:S(2)}) async-start(), calls=%async_computation.12 | async-start | bytes 1310720 | tf_op jit(solution)/shard_map/all_gather | solution.py:606
  97.9 34.3 %collective-permute-start.7 = (bf16[2,512,128]{2,1,0:T(8,128)(2,1)S(1)}, bf16[2,512,128]{2,1,0:T(8,128)(2,1)S(1)}, u32[]{:S(2)}, u32[]{:S(2)}) collective-permute-start(bf16[2,512,128]{2,1,0:T(8,128)(2,1)S(1)} %pad_maximum_fusion.14), channel_id=1, source_target_pairs={{0,16},{8,24},{16,0},{24,8},{1,17},{9,25},{17,1},{25,9},{2,18},{10... | collective-permute-start | bytes 786440 | tf_op jit(solution)/shard_map/ppermute | solution.py:532
  102.1 31.2 %collective-permute-start.5 = (bf16[64,2048]{1,0:T(8,128)(2,1)}, bf16[64,2048]{1,0:T(8,128)(2,1)}, u32[]{:S(2)}, u32[]{:S(2)}) collective-permute-start(bf16[64,2048]{1,0:T(8,128)(2,1)} %param.19), channel_id=1, source_target_pairs={{0,0},{4,1},{8,2},{12,3},{16,4},{20,5},{24,6},{28,7},{1,8},{5,9},{... | collective-permute-start | bytes 786440 | tf_op jit(solution)/shard_map/ppermute | solution.py:688
  133.3 160.1 %all-gather.9.cloned.1.call-start = ((), (), s32[]{:S(2)}) async-start(), calls=%async_computation.13 | async-start | bytes 7208960 | tf_op jit(solution)/shard_map/all_gather | solution.py:606
  182.2 18.8 %collective-permute-start.11 = (bf16[2,64,2048]{2,1,0:T(8,128)(2,1)}, bf16[2,64,2048]{2,1,0:T(8,128)(2,1)}, u32[]{:S(2)}, u32[]{:S(2)}) collective-permute-start(bf16[2,64,2048]{2,1,0:T(8,128)(2,1)} %slice.412), channel_id=1, source_target_pairs={{0,4},{1,5},{2,6},{3,7},{4,0},{5,1},{6,2},{7,3},{8,12},{9,13},{10,... | collective-permute-start | bytes 1572872 | tf_op jit(solution)/shard_map/ppermute | solution.py:532
  188.5 168.1 %all-gather.11.cloned.1.call-start = ((), (), s32[]{:S(2)}) async-start(), calls=%async_computation.14 | async-start | bytes 3932160 | tf_op jit(solution)/shard_map/all_gather | solution.py:606
  256.2 272.7 %reduce-scatter.11.cloned.1.call-start = ((), (), s32[]{:S(2)}) async-start(), calls=%async_computation.18 | async-start | bytes 3604480 | tf_op jit(solution)/shard_map/reduce_scatter | solution.py:611
  286.8 18.3 %collective-permute-start.22 = (bf16[512,2048]{1,0:T(8,128)(2,1)}, bf16[512,2048]{1,0:T(8,128)(2,1)}, u32[]{:S(2)}, u32[]{:S(2)}) collective-permute-start(bf16[512,2048]{1,0:T(8,128)(2,1)} %get-tuple-element.94), channel_id=1, source_target_pairs={{0,1},{1,0},{2,3},{3,2},{4,5},{5,4},{6,7},{7,6},{8,9},{9,8},{10,11... | collective-permute-start | bytes 6291464 | tf_op jit(solution)/shard_map/ppermute | solution.py:532
  420.9 146.7 %reduce-scatter.7.cloned.1.call-start = ((), (), s32[]{:S(2)}) async-start(), calls=%async_computation.16 | async-start | bytes 1310720 | tf_op jit(solution)/shard_map/reduce_scatter | solution.py:729
  455.0 179.1 %reduce-scatter.9.cloned.1.call-start = ((), (), s32[]{:S(2)}) async-start(), calls=%async_computation.17 | async-start | bytes 7208960 | tf_op jit(solution)/shard_map/reduce_scatter | solution.py:611
  507.3 23.8 %all-to-all-start.4 = ((f32[32,1,256]{2,1,0:T(1,128)}), f32[32,1,256]{2,1,0:T(1,128)S(1)}, u32[]{:S(2)}, u32[]{:S(2)}) async-start(f32[32,1,256]{2,1,0:T(1,128)} %reshape.420), calls=%async_computation.5 | async-start | bytes 65536 | tf_op jit(solution)/shard_map/all_to_all | solution.py:749
  521.8 35.4 %collective-permute-start.38 = (bf16[4,128,2048]{2,1,0:T(8,128)(2,1)}, bf16[4,128,2048]{2,1,0:T(8,128)(2,1)}, u32[]{:S(2)}, u32[]{:S(2)}) collective-permute-start(bf16[4,128,2048]{2,1,0:T(8,128)(2,1)} %bitcast.47), channel_id=1, source_target_pairs={{0,1},{1,0},{2,3},{3,2},{4,5},{5,4},{6,7},{7,6},{8,9},{9,8},{10,11... | collective-permute-start | bytes 6291464 | tf_op jit(solution)/shard_map/ppermute | solution.py:532
  528.7 40.6 %collective-permute-start.33 = (bf16[4,128,2048]{2,1,0:T(8,128)(2,1)}, bf16[4,128,2048]{2,1,0:T(8,128)(2,1)}, u32[]{:S(2)}, u32[]{:S(2)}) collective-permute-start(bf16[4,128,2048]{2,1,0:T(8,128)(2,1)} %bitcast.38), channel_id=1, source_target_pairs={{0,1},{1,0},{2,3},{3,2},{4,5},{5,4},{6,7},{7,6},{8,9},{9,8},{10,11... | collective-permute-start | bytes 6291464 | tf_op jit(solution)/shard_map/ppermute | solution.py:532
  531.1 21.1 %all-to-all-start.6 = ((bf16[8,64,704]{2,1,0:T(8,128)(2,1)}), bf16[8,64,704]{2,1,0:T(8,128)(2,1)S(1)}, u32[]{:S(2)}, u32[]{:S(2)}) async-start(bf16[8,64,704]{2,1,0:T(8,128)(2,1)} %bitcast.71), calls=%async_computation.10 | async-start | bytes 1572864 | tf_op jit(solution)/shard_map/all_to_all | solution.py:613
  535.0 170.3 %reduce-scatter.5.cloned.1.call-start = ((), (), s32[]{:S(2)}) async-start(), calls=%async_computation.15 | async-start | bytes 5242880 | tf_op jit(solution)/shard_map/reduce_scatter | solution.py:611
  564.2 22.2 %collective-permute-start.39 = (bf16[2,64,2048]{2,1,0:T(8,128)(2,1)}, bf16[2,64,2048]{2,1,0:T(8,128)(2,1)S(1)}, u32[]{:S(2)}, u32[]{:S(2)}) collective-permute-start(bf16[2,64,2048]{2,1,0:T(8,128)(2,1)} %slice.378), channel_id=1, source_target_pairs={{0,2},{1,3},{2,0},{3,1},{4,6},{5,7},{6,4},{7,5},{8,10},{9,11},{10,... | collective-permute-start | bytes 1572872 | tf_op jit(solution)/shard_map/ppermute | solution.py:532
  566.2 20.2 %collective-permute-start.41 = (bf16[2,64,2048]{2,1,0:T(8,128)(2,1)}, bf16[2,64,2048]{2,1,0:T(8,128)(2,1)}, u32[]{:S(2)}, u32[]{:S(2)}) collective-permute-start(bf16[2,64,2048]{2,1,0:T(8,128)(2,1)} %slice.457), channel_id=1, source_target_pairs={{0,4},{1,5},{2,6},{3,7},{4,0},{5,1},{6,2},{7,3},{8,12},{9,13},{10,... | collective-permute-start | bytes 1572872 | tf_op jit(solution)/shard_map/ppermute | solution.py:532
  571.9 32.2 %collective-permute-start.34 = (bf16[2,64,2048]{2,1,0:T(8,128)(2,1)S(1)}, bf16[2,64,2048]{2,1,0:T(8,128)(2,1)S(1)}, u32[]{:S(2)}, u32[]{:S(2)}) collective-permute-start(bf16[2,64,2048]{2,1,0:T(8,128)(2,1)S(1)} %slice.366), channel_id=1, source_target_pairs={{0,2},{1,3},{2,0},{3,1},{4,6},{5,7},{6,4},{7,5},{8,10},{9,11},{10,... | collective-permute-start | bytes 1572872 | tf_op jit(solution)/shard_map/ppermute | solution.py:532
  575.3 28.8 %collective-permute-start.36 = (bf16[2,64,2048]{2,1,0:T(8,128)(2,1)S(1)}, bf16[2,64,2048]{2,1,0:T(8,128)(2,1)S(1)}, u32[]{:S(2)}, u32[]{:S(2)}) collective-permute-start(bf16[2,64,2048]{2,1,0:T(8,128)(2,1)S(1)} %slice.448), channel_id=1, source_target_pairs={{0,4},{1,5},{2,6},{3,7},{4,0},{5,1},{6,2},{7,3},{8,12},{9,13},{10,... | collective-permute-start | bytes 1572872 | tf_op jit(solution)/shard_map/ppermute | solution.py:532
  587.8 17.4 %collective-permute-start.40 = (bf16[64,2048]{1,0:T(8,128)(2,1)S(1)}, bf16[64,2048]{1,0:T(8,128)(2,1)S(1)}, u32[]{:S(2)}, u32[]{:S(2)}) collective-permute-start(bf16[64,2048]{1,0:T(8,128)(2,1)S(1)} %fusion.30), channel_id=1, source_target_pairs={{0,4},{1,5},{2,6},{3,7},{4,0},{5,1},{6,2},{7,3},{8,12},{9,13},{10,... | collective-permute-start | bytes 786440 | tf_op jit(solution)/shard_map/ppermute | solution.py:532
  589.0 19.5 %collective-permute-start.42 = (bf16[64,2048]{1,0:T(8,128)(2,1)S(1)}, bf16[64,2048]{1,0:T(8,128)(2,1)S(1)}, u32[]{:S(2)}, u32[]{:S(2)}) collective-permute-start(bf16[64,2048]{1,0:T(8,128)(2,1)S(1)} %fusion.31), channel_id=1, source_target_pairs={{0,2},{1,3},{2,0},{3,1},{4,6},{5,7},{6,4},{7,5},{8,10},{9,11},{10,... | collective-permute-start | bytes 786440 | tf_op jit(solution)/shard_map/ppermute | solution.py:532
  604.5 19.8 %collective-permute-start.35 = (bf16[64,2048]{1,0:T(8,128)(2,1)S(1)}, bf16[64,2048]{1,0:T(8,128)(2,1)S(1)}, u32[]{:S(2)}, u32[]{:S(2)}) collective-permute-start(bf16[64,2048]{1,0:T(8,128)(2,1)S(1)} %fusion.28), channel_id=1, source_target_pairs={{0,4},{1,5},{2,6},{3,7},{4,0},{5,1},{6,2},{7,3},{8,12},{9,13},{10,... | collective-permute-start | bytes 786440 | tf_op jit(solution)/shard_map/ppermute | solution.py:532
  605.2 28.1 %collective-permute-start.37 = (bf16[64,2048]{1,0:T(8,128)(2,1)S(1)}, bf16[64,2048]{1,0:T(8,128)(2,1)S(1)}, u32[]{:S(2)}, u32[]{:S(2)}) collective-permute-start(bf16[64,2048]{1,0:T(8,128)(2,1)S(1)} %fusion.29), channel_id=1, source_target_pairs={{0,2},{1,3},{2,0},{3,1},{4,6},{5,7},{6,4},{7,5},{8,10},{9,11},{10,... | collective-permute-start | bytes 786440 | tf_op jit(solution)/shard_map/ppermute | solution.py:532
  609.1 18.0 %collective-permute-start.43 = (f32[226,128]{1,0:T(8,128)S(1)}, f32[226,128]{1,0:T(8,128)S(1)}, u32[]{:S(2)}, u32[]{:S(2)}) collective-permute-start(f32[226,128]{1,0:T(8,128)S(1)} %bitcast.244), channel_id=1, source_target_pairs={{0,8},{8,0},{16,24},{24,16},{1,9},{9,1},{17,25},{25,17},{2,10},{10... | collective-permute-start | bytes 347144 | tf_op jit(solution)/shard_map/ppermute | solution.py:532
  634.1 31.1 %all-to-all-start.5 = ((bf16[8,64,1408]{2,1,0:T(8,128)(2,1)}), bf16[8,64,1408]{2,1,0:T(8,128)(2,1)}, u32[]{:S(2)}, u32[]{:S(2)}) async-start(bf16[8,64,1408]{2,1,0:T(8,128)(2,1)} %bitcast.242), calls=%async_computation.8 | async-start | bytes 2883584 | tf_op jit(solution)/shard_map/all_to_all | solution.py:613
  705.4 22.1 %all-to-all-start.3 = ((bf16[8,64,1024]{2,1,0:T(8,128)(2,1)}), bf16[8,64,1024]{2,1,0:T(8,128)(2,1)}, u32[]{:S(2)}, u32[]{:S(2)}) async-start(bf16[8,64,1024]{2,1,0:T(8,128)(2,1)} %bitcast.243), calls=%async_computation.4 | async-start | bytes 2097152 | tf_op jit(solution)/shard_map/all_to_all | solution.py:613
  (87 other events, 884.7 us)
Sparse Core Ops, SparseCore 0:
  35.5 96.8 all-gather.4
  134.0 29.5 all-gather.6
  188.6 104.7 all-gather.8
  294.8 61.7 all-gather.10
  421.0 53.9 reduce-scatter.10
  477.8 26.9 reduce-scatter.6
  507.2 118.0 reduce-scatter.8
  627.7 77.6 reduce-scatter.4

commit v2 on v1

--- a/solution.py
+++ b/solution.py
@@ -94,10 +94,10 @@
     return inverses
 
 
-def fill_taps(ext, slot, m, proj, pos, prev, first, qkv):
+def fill_taps(ext, slot, proj, pos, prev, first, qkv):
     rows = proj.shape[2]
-    ext[slot, 8 : 8 + rows, :] = proj[pos, m, :, :qkv].astype(f32)
-    tail = proj[prev, m, rows - 16 :, :qkv].astype(f32)[8:]
+    ext[slot, 8 : 8 + rows, :] = proj[*pos, :, :qkv].astype(f32)
+    tail = proj[*prev, rows - 16 :, :qkv].astype(f32)[8:]
     ext[slot, 0:8, :] = jnp.where(first, 0.0, tail)
 
 
@@ -111,9 +111,9 @@
 
 def forward_kernel(
     local_heads,
+    blocks,
     perm,
     proj,
-    logit,
     conv,
     rates,
     gain,
@@ -132,7 +132,7 @@
     keys_t,
     state,
 ):
-    blocks, micro, rows, _ = proj.shape
+    _, micro, rows, _ = proj.shape
     cols = local_heads * LANES
     qkv = 3 * cols
     row, col = grid_of(rows)
@@ -144,13 +144,13 @@
         work = []
         for part in range(PAIR):
             b = i * PAIR + part
-            pos, prev = perm[b], perm[jnp.maximum(b - 1, 0)]
             for m in range(micro):
                 slot = part * micro + m
-                fill_taps(ext, slot, m, proj, pos, prev, b == 0, qkv)
+                pos, prev = (perm[b], m), (perm[jnp.maximum(b - 1, 0)], m)
+                fill_taps(ext, slot, proj, pos, prev, b == 0, qkv)
                 conv_out = conv_rows(ext, slot, conv, rows)
                 act = conv_out * jax.nn.sigmoid(conv_out)
-                logits = logit[pos, m].astype(f32)
+                logits = proj[*pos, :, 4 * cols :].astype(f32)
                 decay = -rates[...] * softplus(logits)
                 strength = jax.nn.sigmoid(logits)
                 total = mm_exact(upto, decay)
@@ -199,7 +199,6 @@
     state[...] = jnp.zeros_like(state)
 
     def step(b, carry):
-        pos = perm[b]
         growth = [jnp.exp(gates[b, m]) for m in range(micro)]
         chains = [(m, h, m * local_heads + h) for m in range(micro) for h in range(local_heads)]
         now = [state[p] for _, _, p in chains]
@@ -221,11 +220,11 @@
             out = out.astype(low)
             heads_out[b, m, :, h * LANES : (h + 1) * LANES] = out
             out = out.astype(f32)
-            gate = proj[pos, m, :, 3 * cols + h * LANES : 3 * cols + (h + 1) * LANES].astype(f32)
+            pos = (perm[b], m)
+            gate = proj[*pos, :, 3 * cols + h * LANES : 3 * cols + (h + 1) * LANES].astype(f32)
             normed = out * lax.rsqrt(jnp.mean(out * out, axis=1, keepdims=True) + eps_norm) * gain[...]
-            mixed[pos, m, :, h * LANES : (h + 1) * LANES] = (
-                normed * (gate * jax.nn.sigmoid(gate))
-            ).astype(low)
+            done = (normed * (gate * jax.nn.sigmoid(gate))).astype(low)
+            mixed[*pos, :, h * LANES : (h + 1) * LANES] = done
         return carry
 
     lax.fori_loop(0, blocks, step, 0)
@@ -233,10 +232,10 @@
 
 def backward_kernel(
     local_heads,
+    blocks,
     perm,
     grad_mixed,
     proj,
-    logit,
     conv,
     rates,
     gain,
@@ -248,7 +247,6 @@
     fresh,
     states,
     grad_proj,
-    grad_logit,
     grad_conv,
     grad_rates,
     grad_gain,
@@ -263,7 +261,7 @@
     grad_states,
     grad_state,
 ):
-    blocks, micro, rows, _ = proj.shape
+    _, micro, rows, _ = proj.shape
     cols = local_heads * LANES
     qkv = 3 * cols
     taps = conv.shape[0]
@@ -279,9 +277,9 @@
     grad_state[...] = jnp.zeros_like(grad_state)
 
     def prepare(b, carry):
-        pos = perm[b]
         work = []
         for m in range(micro):
+            pos = (perm[b], m)
             total = gates[b, m]
             growth = jnp.exp(total)
             total_t = total.T
@@ -289,15 +287,15 @@
                 p = m * local_heads + h
                 here = slice(h * LANES, (h + 1) * LANES)
                 out = heads_out[b, m, :, here].astype(f32)
-                gate = proj[pos, m, :, 3 * cols + h * LANES : 3 * cols + (h + 1) * LANES].astype(f32)
-                dmixed = grad_mixed[pos, m, :, here].astype(f32)
+                gate = proj[*pos, :, 3 * cols + h * LANES : 3 * cols + (h + 1) * LANES].astype(f32)
+                dmixed = grad_mixed[*pos, :, here].astype(f32)
                 root = lax.rsqrt(jnp.mean(out * out, axis=1, keepdims=True) + eps_norm)
                 unit = out * root
                 sig = jax.nn.sigmoid(gate)
                 dnormed = dmixed * (gate * sig)
-                grad_proj[pos, m, :, 3 * cols + h * LANES : 3 * cols + (h + 1) * LANES] = (
-                    dmixed * (unit * gain[...]) * (sig * (1.0 + gate * (1.0 - sig)))
-                ).astype(low)
+                dgate = dmixed * (unit * gain[...]) * (sig * (1.0 + gate * (1.0 - sig)))
+                at = slice(3 * cols + h * LANES, 3 * cols + (h + 1) * LANES)
+                grad_proj[*pos, :, at] = dgate.astype(low)
                 grad_gain[...] += jnp.sum(dnormed * unit, axis=0, keepdims=True)
                 dunit = dnormed * gain[...]
                 dout = root * (dunit - unit * jnp.mean(unit * dunit, axis=1, keepdims=True))
@@ -340,7 +338,6 @@
 
     def finish(i, carry):
         b = blocks - 1 - i
-        pos, prev = perm[b], perm[jnp.maximum(b - 1, 0)]
         work = []
         for m in range(micro):
             total = gates[b, m]
@@ -385,7 +382,8 @@
         dk = [fine(dscores[n].T, queries[n]) for n in number]
         dk_same = [fine(dbelow[n] + dbelow[n].T, keys[n]) for n in number]
         for m in range(micro):
-            fill_taps(ext, m, m, proj, pos, prev, b == 0, qkv)
+            pos, prev = (perm[b], m), (perm[jnp.maximum(b - 1, 0)], m)
+            fill_taps(ext, m, proj, pos, prev, b == 0, qkv)
             conv_out = conv_rows(ext, m, conv, rows)
             sig = jax.nn.sigmoid(conv_out)
             act = conv_out * sig
@@ -428,11 +426,11 @@
             du = conv[taps - 1 : taps, :] * dconv
             for j in range(taps - 1):
                 du = du + conv[j : j + 1, :] * dext[m, taps - 1 - j : taps - 1 - j + rows, :]
-            grad_proj[pos, m, :, :qkv] = du.astype(low)
+            grad_proj[*pos, :, :qkv] = du.astype(low)
             for j in range(taps):
                 term = dconv * ext[m, 9 - taps + j : 9 - taps + j + rows, :]
                 conv_sum[j] += jnp.sum(term.reshape(rows // 8, 8, qkv), axis=0)
-            logits = logit[pos, m].astype(f32)
+            logits = proj[*pos, :, 4 * cols :].astype(f32)
             ddecay = mm_exact(upto_t, dtotal)
             strength = gates[b, m]
             dlogit = jnp.where(
@@ -440,7 +438,8 @@
                 -rates[...] * jax.nn.sigmoid(logits) * ddecay,
                 strength * (1.0 - strength) * dstrength,
             )
-            grad_logit[pos, m] = jnp.where(lane < 2 * local_heads, dlogit, 0.0).astype(low)
+            dlogit = jnp.where(lane < 2 * local_heads, dlogit, 0.0).astype(low)
+            grad_proj[*pos, :, 4 * cols :] = dlogit
             grad_rates[...] -= jnp.sum(softplus(logits) * ddecay, axis=0, keepdims=True)
         return carry
 
@@ -453,7 +452,7 @@
     return pl.BlockSpec(memory_space=pltpu.VMEM)
 
 
-def heads_forward(perm, proj, logit, conv, rates, gain, local_heads):
+def heads_forward(perm, proj, conv, rates, gain, local_heads):
     blocks, micro, rows, _ = proj.shape
     cols = local_heads * LANES
     chains = micro * local_heads
@@ -462,7 +461,7 @@
         return jax.ShapeDtypeStruct(dims, kind)
 
     return pl.pallas_call(
-        partial(forward_kernel, local_heads),
+        partial(forward_kernel, local_heads, perm.shape[0]),
         out_shape=(
             shape((blocks, micro, rows, cols), low),
             shape((blocks, micro, rows, cols), low),
@@ -473,7 +472,7 @@
             shape((blocks, chains, rows, LANES), f32),
             shape((blocks, chains, LANES, LANES), f32),
         ),
-        in_specs=[pl.BlockSpec(memory_space=pltpu.SMEM)] + [in_vmem()] * 5,
+        in_specs=[pl.BlockSpec(memory_space=pltpu.SMEM)] + [in_vmem()] * 4,
         out_specs=(in_vmem(),) * 8,
         scratch_shapes=[
             pltpu.VMEM((PAIR * micro, rows + 8, 3 * cols), f32),
@@ -485,10 +484,10 @@
         ],
         compiler_params=pltpu.CompilerParams(vmem_limit_bytes=50 * 1024 * 1024),
         name="heads_forward",
-    )(perm, proj, logit, conv, rates, gain)
-
-
-def heads_backward(perm, grad_mixed, proj, logit, conv, rates, gain, kept, local_heads):
+    )(perm, proj, conv, rates, gain)
+
+
+def heads_backward(perm, grad_mixed, proj, conv, rates, gain, kept, local_heads):
     blocks, micro, rows, wide = proj.shape
     cols = local_heads * LANES
     chains = micro * local_heads
@@ -498,16 +497,15 @@
         return jax.ShapeDtypeStruct(dims, kind)
 
     return pl.pallas_call(
-        partial(backward_kernel, local_heads),
+        partial(backward_kernel, local_heads, perm.shape[0]),
         out_shape=(
             shape((blocks, micro, rows, wide), low),
-            shape((blocks, micro, rows, LANES), low),
             shape((taps, 3 * cols), f32),
             shape((1, LANES), f32),
             shape((1, LANES), f32),
         ),
-        in_specs=[pl.BlockSpec(memory_space=pltpu.SMEM)] + [in_vmem()] * 13,
-        out_specs=(in_vmem(),) * 5,
+        in_specs=[pl.BlockSpec(memory_space=pltpu.SMEM)] + [in_vmem()] * 12,
+        out_specs=(in_vmem(),) * 4,
         scratch_shapes=[
             pltpu.VMEM((micro, rows + 8, 3 * cols), f32),
             pltpu.VMEM((micro, rows + 8, 3 * cols), f32),
@@ -522,7 +520,7 @@
         ],
         compiler_params=pltpu.CompilerParams(vmem_limit_bytes=50 * 1024 * 1024),
         name="heads_backward",
-    )(perm, grad_mixed, proj, logit, conv, rates, gain, *kept)
+    )(perm, grad_mixed, proj, conv, rates, gain, *kept)
 
 
 both = ("dp", "seq")
@@ -532,8 +530,8 @@
     return lax.ppermute(value, axis, [(i, i ^ bit) for i in range(lax.axis_size(axis))])
 
 
-def after(value, *others):
-    return lax.optimization_barrier((value, *others))[0]
+def tie(*values):
+    return lax.optimization_barrier(values)
 
 
 def gather_places():
@@ -559,12 +557,13 @@
     return jnp.concatenate([near, swap(near, "seq", 1)])
 
 
-def scatter_seq(partial_rows):
+def scatter_seq(partial_rows, beside=None):
     peers = lax.axis_size("seq")
     if peers != 8:
-        return lax.psum_scatter(
+        total = lax.psum_scatter(
             partial_rows.astype(low), "seq", scatter_dimension=0, tiled=True
         ).astype(f32)
+        return total if beside is None else (total, beside)
     terms = partial_rows.astype(low).reshape(peers, -1, partial_rows.shape[-1])
     half = terms.shape[1] // 2
     near = terms[:4].astype(f32) + swap(terms[4:], "seq", 1).astype(f32)
@@ -573,9 +572,12 @@
     bottom_y = swap(bottom[2:], "seq", 4)
     top = near[0::2, :half] + top_x.astype(f32)
     bottom = near[:2, half:] + bottom_y.astype(f32)
+    if beside is not None:
+        top, bottom, beside = tie(top, bottom, beside)
     top_y = swap(top[1].astype(low), "seq", 4)
     bottom_x = swap(bottom[1].astype(low), "seq", 2)
-    return jnp.concatenate([top[0] + top_y.astype(f32), bottom[0] + bottom_x.astype(f32)])
+    total = jnp.concatenate([top[0] + top_y.astype(f32), bottom[0] + bottom_x.astype(f32)])
+    return total if beside is None else (total, beside)
 
 
 def sum_all(value):
@@ -587,16 +589,6 @@
     return value
 
 
-def gather_dp_small(value):
-    groups = lax.axis_size("dp")
-    parts, bit = value[None], 1
-    while bit < groups:
-        parts = jnp.concatenate([parts, swap(parts, "dp", bit)])
-        bit *= 2
-    places = jnp.arange(groups, dtype=jnp.int32) ^ lax.axis_index("dp").astype(jnp.int32)
-    return jnp.take(parts, places, axis=0)
-
-
 def to_columns(pieces):
     rows_here = lax.all_to_all(pieces, "seq", split_axis=0, concat_axis=0, tiled=True)
     return rows_here.reshape(-1, pieces.shape[-1])
@@ -606,11 +598,51 @@
     return lax.all_gather(rows_here, "dp", axis=0, tiled=True)
 
 
-def columns_back(term):
-    peers = lax.axis_size("seq")
-    own = lax.psum_scatter(term.astype(low), "dp", scatter_dimension=0, tiled=True)
-    own = own.reshape(peers, own.shape[0] // peers, own.shape[1])
-    return lax.all_to_all(own, "seq", split_axis=0, concat_axis=0, tiled=True).transpose(1, 0, 2)
+def sum_dp(term):
+    return lax.psum_scatter(term.astype(low), "dp", scatter_dimension=0, tiled=True)
+
+
+def to_owners(own):
+    pieces = own.reshape(lax.axis_size("seq"), -1, own.shape[1])
+    return lax.all_to_all(pieces, "seq", split_axis=0, concat_axis=0, tiled=True)
+
+
+def widen(columns):
+    extra = -columns.shape[-1] % LANES
+    return jnp.pad(columns, [(0, 0)] * (columns.ndim - 1) + [(0, extra)])
+
+
+def assemble_kernel(local_heads, pieces, whole):
+    peers, _, wide = pieces.shape
+    cols = (wide - LANES) // 4
+    width = cols * peers
+    logits = []
+    for part in range(5):
+        for j in range(peers):
+            from_here = slice(part * cols, min((part + 1) * cols, wide))
+            total = pieces[j, :, from_here].astype(f32)
+            if part < 4:
+                whole[:, part * width + j * cols : part * width + (j + 1) * cols] = total
+            else:
+                logits.append(total)
+    for kind in range(2):
+        here = slice(kind * local_heads, (kind + 1) * local_heads)
+        for j in range(peers):
+            at = 4 * width + kind * local_heads * peers + j * local_heads
+            whole[:, at : at + local_heads] = logits[j][:, here]
+
+
+def assemble(pieces, local_heads):
+    peers, rows, wide = pieces.shape
+    total = (wide - LANES) * peers + 2 * local_heads * peers
+    return pl.pallas_call(
+        partial(assemble_kernel, local_heads),
+        out_shape=jax.ShapeDtypeStruct((rows, total), f32),
+        in_specs=[in_vmem()],
+        out_specs=in_vmem(),
+        compiler_params=pltpu.CompilerParams(vmem_limit_bytes=30 * 1024 * 1024),
+        name="assemble",
+    )(pieces)
 
 
 def row_pairs(inverse):
@@ -653,7 +685,7 @@
     local_heads = heads // peers
     taps = conv_weight.shape[0]
     units = mlp_out_weight.shape[1]
-    local_units = units // peers
+    own_units = units // peers
     own_rows = mix_weight.shape[0]
     cols = width // peers
     logit_cols = 2 * local_heads
@@ -662,39 +694,36 @@
     valid = (positions < lengths[:, None]).astype(f32).reshape(-1, 1)
     inputs = tokens.reshape(-1, width).astype(f32)
 
-    main = mix_weight[:, : 4 * width].reshape(own_rows, 4, peers, cols)
+    out_rows = lax.ppermute(out_weight, both, row_pairs(False))
+    main = mix_weight[:, : 4 * width].reshape(own_rows, 4, peers, cols).transpose(2, 0, 1, 3)
     logits = mix_weight[:, 4 * width :].reshape(own_rows, 2, peers, local_heads)
+    logits = logits.transpose(2, 0, 1, 3).reshape(peers, own_rows, logit_cols)
     mix_rows = to_columns(
-        jnp.concatenate(
-            [
-                main.transpose(2, 0, 1, 3).reshape(peers, own_rows, 4 * cols),
-                logits.transpose(2, 0, 1, 3).reshape(peers, own_rows, logit_cols),
-                jnp.zeros((peers, own_rows, LANES - logit_cols), low),
-            ],
-            axis=2,
-        )
-    )
-    mix_here = gather_dp(mix_rows[:, : 4 * cols])
-    logit_here = gather_dp_small(mix_rows[:, 4 * cols :]).reshape(width, LANES)
+        jnp.concatenate([main.reshape(peers, own_rows, 4 * cols), widen(logits)], axis=2)
+    )
+    wide_cols = mix_rows.shape[1]
     normed, norm_back = jax.vjp(rms_scale, inputs, norm_gain)
-    normed_all = gather_seq(normed.astype(low))
-    in_pieces = mlp_in_weight.reshape(own_rows, 2, peers, local_units).transpose(2, 0, 1, 3)
-    in_rows = to_columns(
-        after(in_pieces.reshape(peers, own_rows, 2 * local_units), mix_rows)
-    )
-    down_rows = to_columns(
-        after(mlp_out_weight.reshape(own_rows, peers, local_units).transpose(1, 0, 2), mix_rows)
-    )
-    out_rows = lax.ppermute(after(out_weight, mix_rows), both, row_pairs(False))
-    mix_here, in_rows, down_rows, out_rows = lax.optimization_barrier(
-        (mix_here, in_rows, down_rows, out_rows)
-    )
-    out_here = gather_dp(out_rows)
-    in_here = gather_dp(in_rows)
-    down_here = gather_dp(down_rows)
+    mix_rows, normed_low, mlp_in_rows, mlp_out_rows = tie(
+        mix_rows, normed.astype(low), mlp_in_weight, mlp_out_weight
+    )
+    mixer_here = gather_dp(
+        jnp.concatenate([mix_rows, out_rows.reshape(mix_rows.shape[0], -1)], axis=1)
+    )
+    normed_all = gather_seq(normed_low)
+    gate_up = mlp_in_rows.reshape(own_rows, 2, peers, own_units).transpose(2, 0, 1, 3)
+    down = mlp_out_rows.reshape(own_rows, peers, 1, own_units).transpose(1, 0, 2, 3)
+    mlp_pieces = jnp.concatenate([gate_up, down], axis=2).reshape(peers, own_rows, 3 * own_units)
+    mlp_rows = to_columns(mlp_pieces)
+    cotangent = valid * grad_out.reshape(-1, width).astype(f32)
+    mixer_here, mlp_rows, normed_all, cot_low = tie(
+        mixer_here, mlp_rows, normed_all, cotangent.astype(low)
+    )
+    in_here = gather_dp(mlp_rows[:, : 2 * own_units])
+    down_here = gather_dp(mlp_rows[:, 2 * own_units :])
+    mix_here = mixer_here[:, :wide_cols]
+    out_here = mixer_here[:, wide_cols:].reshape(-1, width)
 
     projected = dot32(normed_all, mix_here).astype(low).reshape(peers, micro, seq_rows, -1)
-    logit_pre = dot32(normed_all, logit_here).astype(low).reshape(peers, micro, seq_rows, LANES)
     conv_here = lax.dynamic_index_in_dim(
         conv_weight.reshape(taps, 3, peers, cols), here, 2, keepdims=False
     ).reshape(taps, 3 * cols)
@@ -702,55 +731,63 @@
     rate_lanes = jnp.pad(rates_here, (0, LANES - local_heads)).reshape(1, LANES)
     gain_row = out_gain.reshape(1, LANES)
     places = gather_places()
-    mixed_rows, *kept = heads_forward(
-        places, projected, logit_pre, conv_here, rate_lanes, gain_row, local_heads
-    )
-    mixed_low = mixed_rows.reshape(-1, cols)
-    hidden = inputs + scatter_seq(dot32(mixed_low, out_here))
+    mixed, *kept = heads_forward(
+        places, projected, conv_here, rate_lanes, gain_row, local_heads
+    )
+    mixed, cot_low = tie(mixed, cot_low)
+    mixed_low = mixed.reshape(-1, cols)
+    branch, in_here = scatter_seq(dot32(mixed_low, out_here), in_here)
+    hidden = inputs + branch
 
     second, second_back = jax.vjp(rms_scale, hidden, mlp_gain)
     second_all = gather_seq(second.astype(low))
-    cotangent = valid * grad_out.reshape(-1, width).astype(f32)
-    cot_all = gather_seq(after(cotangent.astype(low), second_all))
+    cot_all = gather_seq(cot_low)
     gate_up = dot32(second_all, in_here).astype(low)
     activated, swiglu_back = jax.vjp(swiglu, gate_up.astype(f32))
     activated_low = activated.astype(low)
+    activated_low, down_here = tie(activated_low, down_here)
+    grad_down_term = t_dot(cot_all, activated_low).astype(low)
+    cot_all, grad_down_term = tie(cot_all, grad_down_term)
     (grad_gate_up,) = swiglu_back(dot32(cot_all, down_here))
     grad_gate_low = grad_gate_up.astype(low)
     grad_second = scatter_seq(dot_t(grad_gate_low, in_here))
     grad_hidden_norm, grad_mlp_gain = second_back(grad_second)
     grad_hidden = cotangent + grad_hidden_norm
     branch_all = gather_seq(grad_hidden.astype(low))
-    grad_in = columns_back(t_dot(second_all, grad_gate_low))
-    grad_down = columns_back(t_dot(cot_all, activated_low))
+    grad_down = sum_dp(grad_down_term)
+    grad_in = sum_dp(t_dot(second_all, grad_gate_low))
 
     grad_mixed = dot_t(branch_all, out_here).reshape(peers, micro, seq_rows, cols)
+    grad_mixed, grad_down = tie(grad_mixed, grad_down)
+    grad_out_term = t_dot(mixed_low, branch_all).astype(low)
+    grad_projected, grad_conv, rate_sums, gain_sums = (
+        heads_backward(
+            places,
+            grad_mixed,
+            projected,
+            conv_here,
+            rate_lanes,
+            gain_row,
+            kept,
+            local_heads,
+        )
+    )
+    grad_projected = grad_projected.reshape(-1, wide_cols)
+    grad_mix_term = t_dot(normed_all, grad_projected).astype(low)
+    grad_mix_term, grad_projected, activated_low = tie(
+        grad_mix_term, grad_projected, activated_low
+    )
+    mixer_own = sum_dp(
+        jnp.concatenate([grad_mix_term, grad_out_term.reshape(width, -1)], axis=1)
+    )
+    grad_mix = to_owners(mixer_own[:, :wide_cols])
     grad_out_own = lax.ppermute(
-        lax.psum_scatter(
-            t_dot(mixed_low, branch_all).astype(low), "dp", scatter_dimension=0, tiled=True
-        ),
-        both,
-        row_pairs(True),
-    )
-    grad_projected, grad_logits, grad_conv, rate_sums, gain_sums = heads_backward(
-        places, grad_mixed, projected, logit_pre, conv_here, rate_lanes, gain_row, kept, local_heads
-    )
-    grad_projected = grad_projected.reshape(-1, 4 * cols)
-    grad_logits = grad_logits.reshape(-1, LANES)
-    grad_normed = scatter_seq(
-        dot_t(grad_projected, mix_here) + dot_t(grad_logits, logit_here)
-    )
+        mixer_own[:, wide_cols:].reshape(own_rows, width), both, row_pairs(True)
+    )
+    grad_normed = scatter_seq(dot_t(grad_projected, mix_here))
     grad_inputs_norm, grad_norm_gain = norm_back(grad_normed)
     grad_tokens = grad_hidden + grad_inputs_norm
-    grad_mix = columns_back(t_dot(normed_all, grad_projected))
-    grad_mix_main = grad_mix.reshape(own_rows, peers, 4, cols).transpose(0, 2, 1, 3)
-    logit_terms = t_dot(grad_logits[:, :logit_cols], normed_all)
-    logit_terms = logit_terms.reshape(logit_cols, groups * peers, own_rows).transpose(1, 0, 2)
-    logit_terms = lax.all_to_all(logit_terms, both, split_axis=0, concat_axis=0, tiled=True)
-    logit_terms = logit_terms.reshape(groups, peers, 2, local_heads, own_rows).sum(0)
-    grad_mix_logits = logit_terms.transpose(3, 1, 0, 2).reshape(own_rows, 2 * heads)
-
-    feed_out = scatter_seq(dot_t(after(activated_low, grad_projected), down_here))
+    feed_out = scatter_seq(dot_t(activated_low, down_here))
     result = (valid * (hidden + feed_out)).astype(low)
 
     conv_terms = lax.dynamic_update_slice(
@@ -775,22 +812,19 @@
     ).reshape(-1)
     ends = [sum(sizes[: i + 1]) for i in range(len(sizes))]
     sums = [summed[end - size : end] for end, size in zip(ends, sizes)]
+    grad_in = to_owners(grad_in).reshape(peers, own_rows, 2, own_units).transpose(1, 2, 0, 3)
+    grad_down = to_owners(grad_down).transpose(1, 0, 2)
     return (
         result.reshape(tokens.shape),
         grad_tokens.reshape(tokens.shape),
         sums[0],
-        jnp.concatenate(
-            [grad_mix_main.reshape(own_rows, 4 * width).astype(f32), grad_mix_logits], axis=1
-        ),
+        assemble(grad_mix, local_heads),
         sums[4].reshape(taps, 3 * width),
         sums[3][:heads],
         sums[2],
         grad_out_own.astype(f32),
         sums[1],
-        grad_in.reshape(own_rows, peers, 2, local_units)
-        .transpose(0, 2, 1, 3)
-        .reshape(own_rows, 2 * units)
-        .astype(f32),
+        grad_in.reshape(own_rows, 2 * units).astype(f32),
         grad_down.reshape(own_rows, units).astype(f32),
     )
 

time: 752 us -> 650 us (0.86)
  starting transfers between devices: 121 us -> 65.2 us
  waiting for transfers between devices: 275 us -> 242 us
  local copies, waits for them, and re-layouts: 134 us -> 120 us
  matrix products: 94.2 us -> 82.2 us
    ppermute x47 -> x45, starting transfers between devices: 87.7 us -> 41.5 us  [swap(): lax.ppermute(value, axis, [(i, i ^ bit) for i in range(lax.axis_size(axis...]
    reduce_scatter x4 -> x3, waiting for transfers between devices: 40.2 us -> 9.01 us  [sum_dp(): lax.psum_scatter(term.astype(low), 'dp', scatter_dimension=0, tiled=True)]
    ppermute x47 -> x45, waiting for transfers between devices: 159 us -> 130 us  [swap(): lax.ppermute(value, axis, [(i, i ^ bit) for i in range(lax.axis_size(axis...]
    unnamed x158 -> x167, local copies, waits for them, and re-layouts: 55.2 us -> 32.2 us
    all_to_all x3 -> x2, waiting for transfers between devices: 24.1 us -> 38.8 us  [to_columns(): lax.all_to_all(pieces, 'seq', split_axis=0, concat_axis=0, tiled=True)]
    all_to_all x4 -> x3, waiting for transfers between devices: 0.01 us -> 11.6 us  [to_owners(): lax.all_to_all(pieces, 'seq', split_axis=0, concat_axis=0, tiled=True)]
    concatenate x3 -> x4, other arithmetic: 1.55 us -> 12.9 us  [the longest x1 5.27 us: shards(): jnp.concatenate([gate_up, down], axis=2)]
    slice x2 -> x6, local copies, waits for them, and re-layouts: 2.45 us -> 11.5 us  [the longest x1 2.57 us: shards(): in_here = gather_dp(mlp_rows[:, :2 * own_units])]
  transfers between devices with their start and end apart: 64 -> 58, of which waited for: 35 -> 42; matrix products, arithmetic and copies ran while one was open for 29% -> 37% of each run, Pallas kernels for 7% -> 9%
where the time goes in v2:
time: 650 us; the launch traced here: 637 us
  waiting for transfers between devices  242 us (37%)
  local copies, waits for them, and re-layouts  120 us (18%)
  matrix products  82.2 us (13%)
  starting transfers between devices  65.2 us (10%)
  Pallas kernels  56.3 us (9%)
  other arithmetic  55.2 us (8%)
  between operations  15.6 us (2%)
    ppermute x45, waiting for transfers between devices, swap(): lax.ppermute(value, axis, [(i, i ^ bit) for i in range(lax.axis_size(axis...  130 us
    all_gather x3, waiting for transfers between devices, gather_dp(): return lax.all_gather(rows_here, 'dp', axis=0, tiled=True)  52.9 us
    ppermute x45, starting transfers between devices, swap(): lax.ppermute(value, axis, [(i, i ^ bit) for i in range(lax.axis_size(axis...  41.5 us
    all_to_all x2, waiting for transfers between devices, to_columns(): lax.all_to_all(pieces, 'seq', split_axis=0, concat_axis=0, tiled=True)  38.8 us
    pallas_call x1, Pallas kernels, heads_backward(): pl.pallas_call(partial(backward_kernel, local_heads, perm.shape[0]), out_...  32.2 us
    unnamed x167, local copies, waits for them, and re-layouts  32.2 us
    dot_general x4, matrix products, dot32(): return jnp.dot(left, right, preferred_element_type=f32)  28.7 us
    dot_general x4, matrix products, t_dot(): lax.dot_general(left, right, (((0,), (0,)), ((), ())), preferred_element_...  27.5 us
  transfers between devices with their start and end apart: 58, of which 42 were waited for; matrix products, arithmetic and copies ran while one was open for 37% of the time, Pallas kernels for 9%

profile of v2, /device:TPU:0, one launch (start us, length us, event | category | flops | bytes accessed | tf_op | source)
XLA Modules:
  0.0 637.3 jit_solution(4948152233306842859)
XLA Ops:
  14.2 5.2 all-to-all-start
  21.0 17.9 %all-to-all-done = bf16[8,64,1152]{2,1,0:T(8,128)(2,1)S(1)} async-done(((bf16[8,64,1152]{2,1,0:T(8,128)(2,1)}), bf16[8,64,1152]{2,1,0:T(8,128)(2,1)S(1)}, u32[]{:S(2)}, u32[]{:S(2)}) %all-to-all-start) | async-done | bytes 1179680 | tf_op jit(solution)/shard_map/all_to_all | solution.py:593
  63.7 8.9 %collective-permute-done.4 = bf16[128,2048]{1,0:T(8,128)(2,1)S(1)} collective-permute-done((bf16[128,2048]{1,0:T(8,128)(2,1)S(1)}, bf16[128,2048]{1,0:T(8,128)(2,1)S(1)}, u32[]{:S(2)}, u32[]{:S(2)}) %collective-permute-start.4) | collective-permute-done | bytes 524320 | tf_op jit(solution)/shard_map/ppermute | solution.py:530
  75.6 5.3 pad_maximum_fusion.1
  80.9 6.9 %reshape.311 = bf16[8,64,2112]{2,1,0:T(8,128)(2,1)} reshape(bf16[8,64,3,704]{3,2,1,0:T(4,128)(2,1)} %pad_maximum_fusion.1) | data formatting | bytes 4325376 | tf_op jit(solution)/shard_map/reshape | solution.py:715
  99.4 21.0 %all-to-all-done.1 = bf16[8,64,2112]{2,1,0:T(8,128)(2,1)} async-done(((bf16[8,64,2112]{2,1,0:T(8,128)(2,1)}), bf16[8,64,2112]{2,1,0:T(8,128)(2,1)}, u32[]{:S(2)}, u32[]{:S(2)}) %all-to-all-start.1) | async-done | bytes 2162720 | tf_op jit(solution)/shard_map/all_to_all | solution.py:593
  120.4 29.0 %all-gather.4.cloned.1.call-done = bf16[2048,1408]{1,0:T(8,128)(2,1)} async-done(((bf16[512,1408]{1,0:T(8,128)(2,1)}), bf16[2048,1408]{1,0:T(8,128)(2,1)}) %all-gather.4.cloned.1.call-update) | async-done | bytes 5767184 | tf_op jit(solution)/shard_map/all_gather | solution.py:598
  154.7 10.1 %fusion.5 = bf16[1024,1152]{1,0:T(8,128)(2,1)} fusion(bf16[1024,2048]{1,0:T(8,128)(2,1)} %constant_dynamic-update-slice_fusion.3, bf16[2048,1408]{1,0:T(8,128)(2,1)} %all-gather.4.cloned.1.call-done), kind=kOutput, calls=%fused_computation.15 | convolution fusion | flops 4833017856 | bytes 11272192 | tf_op jit(solution)/shard_map/dot_general | solution.py:655
  164.8 22.6 %heads_forward.1 = (bf16[8,2,64,256]{3,2,1,0:T(8,128)(2,1)S(1)}, bf16[8,2,64,256]{3,2,1,0:T(8,128)(2,1)S(1)}, bf16[8,2,64,768]{3,2,1,0:T(8,128)(2,1)}, f32[8,2,6...) custom-call(s32[8]{0:T(128)S(1)} %fusion.46.perm, ...), custom_call_target="tpu_custom_call" | custom-call | tf_op jit(solution)/shard_map/heads_forward/pallas_call | solution.py:463
  212.1 7.1 %collective-permute-done.18 = bf16[128,2048]{1,0:T(8,128)(2,1)S(1)} collective-permute-done((bf16[128,2048]{1,0:T(8,128)(2,1)}, bf16[128,2048]{1,0:T(8,128)(2,1)S(1)}, u32[]{:S(2)}, u32[]{:S(2)}) %collective-permute-start.18) | collective-permute-done | bytes 524320 | tf_op jit(solution)/shard_map/ppermute | solution.py:530
  230.8 8.6 %collective-permute-done.8 = bf16[2,64,2048]{2,1,0:T(8,128)(2,1)S(1)} collective-permute-done((bf16[2,64,2048]{2,1,0:T(8,128)(2,1)S(1)}, bf16[2,64,2048]{2,1,0:T(8,128)(2,1)S(1)}, u32[]{:S(2)}, u32[]{:S(2)}) %collective-permute-start.8) | collective-permute-done | bytes 524320 | tf_op jit(solution)/shard_map/ppermute | solution.py:530
  241.6 15.5 %all-gather.6.cloned.1.call-done = bf16[2048,1408]{1,0:T(8,128)(2,1)} async-done(((bf16[512,1408]{1,0:T(8,128)(2,1)}), bf16[2048,1408]{1,0:T(8,128)(2,1)}) %all-gather.6.cloned.1.call-update) | async-done | bytes 5767184 | tf_op jit(solution)/shard_map/all_gather | solution.py:598
  286.3 9.3 %collective-permute-done.13 = bf16[128,2048]{1,0:T(8,128)(2,1)S(1)} collective-permute-done((bf16[128,2048]{1,0:T(8,128)(2,1)S(1)}, bf16[128,2048]{1,0:T(8,128)(2,1)S(1)}, u32[]{:S(2)}, u32[]{:S(2)}) %collective-permute-start.13) | collective-permute-done | bytes 524320 | tf_op jit(solution)/shard_map/ppermute | solution.py:530
  300.6 6.6 %fusion.4 = f32[1024,1408]{1,0:T(8,128)S(1)} fusion(bf16[1024,2048]{1,0:T(8,128)(2,1)S(1)} %constant_dynamic-update-slice_fusion.10, bf16[2048,1408]{1,0:T(8,128)(2,1)S(1)} %bitcast.198), kind=kOutput, calls=%fused_computation.14 | convolution fusion | flops 5908463616 | bytes 15728640 | tf_op jit(solution)/shard_map/dot_general | solution.py:655
  312.0 8.5 %all-gather.8.cloned.1.call-done = bf16[2048,704]{1,0:T(8,128)(2,1)} async-done(((bf16[512,704]{1,0:T(8,128)(2,1)}), bf16[2048,704]{1,0:T(8,128)(2,1)}) %all-gather.8.cloned.1.call-update) | async-done | bytes 2883600 | tf_op jit(solution)/shard_map/all_gather | solution.py:598
  320.5 7.5 %convolution_convert_fusion.6 = bf16[2048,704]{0,1:T(8,128)(2,1)} fusion(bf16[1024,2048]{1,0:T(8,128)(2,1)} %copy-done.42, bf16[1024,704]{1,0:T(8,128)(2,1)} %multiply_convert_fusion), kind=kOutput, calls=%fused_computation.20 | convolution fusion | flops 2954231808 | bytes 8519680 | tf_op jit(solution)/shard_map/dot_general | solution.py:663
  328.2 9.5 %fusion.35 = (f32[1024,704]{1,0:T(8,128)S(1)}, f32[1024,704]{1,0:T(8,128)S(1)}) fusion(f32[1024,1408]{1,0:T(8,128)} %copy-done.20, bf16[1024,2048]{1,0:T(8,128)(2,1)} %copy-done.42, bf16[2048,704]{1,0:T(8,128)(2,1)} %all-gather.8.cloned.1.call-done), kind=kOutput, calls=%fused_computation.108 | convolution fusion | flops 2961440768 | bytes 18612224 | tf_op jit(solution)/shard_map/dot_general | solution.py:655
  337.7 8.8 %convolution_convert_fusion.3 = bf16[1024,2048]{1,0:T(8,128)(2,1)S(1)} fusion(bf16[2048,1408]{1,0:T(8,128)(2,1)} %all-gather.6.cloned.1.call-done, f32[1024,704]{1,0:T(8,128)S(1)} %get-tuple-element.84, f32[1024,704]{1,0:T(8,128)S(1)} %get-tuple-element.83), kind=kOutput, calls=%fused_computation.17 | convolution fusion | flops 5910560768 | bytes 15728640 | tf_op jit(solution)/shard_map/dot_general | solution.py:659
  358.8 9.0 %convolution_convert_fusion.1 = bf16[2048,1408]{1,0:T(8,128)(2,1)} fusion(bf16[1024,2048]{1,0:T(8,128)(2,1)S(1)} %copy-done.44, f32[1024,704]{1,0:T(8,128)S(1)} %get-tuple-element.84, f32[1024,704]{1,0:T(8,128)S(1)} %get-tuple-element.83), kind=kOutput, calls=%fused_computation.1 | convolution fusion | flops 5911347200 | bytes 15728640 | tf_op jit(solution)/shard_map/dot_general | solution.py:663
  375.7 5.0 collective-permute-done.25
  397.3 8.6 %collective-permute-done.28 = bf16[128,2048]{1,0:T(8,128)(2,1)S(1)} collective-permute-done((bf16[128,2048]{1,0:T(8,128)(2,1)S(1)}, bf16[128,2048]{1,0:T(8,128)(2,1)S(1)}, u32[]{:S(2)}, u32[]{:S(2)}) %collective-permute-start.28) | collective-permute-done | bytes 524320 | tf_op jit(solution)/shard_map/ppermute | solution.py:530
  424.9 32.2 %heads_backward.1 = (bf16[8,2,64,1152]{3,2,1,0:T(8,128)(2,1)}, f32[4,768]{1,0:T(4,128)S(1)}, f32[1,128]{1,0:T(1,128)S(1)}, f32[1,128]{1,0:T(1,128)S(1)}) custom-call(s32[8]{0:T(128)S(1)} %fusion.46.perm, f32[8,2,64,256]{3,2,1,0:T(8,128)S(1)} %fusion.24.grad_mixed, bf16[8,2,64,1152]{3,2,1,0:T(8,128)(2,1)} %bitcast.172, f32[4,768]{1,0:T(4,128)S(1)} %bitcast.166, ...), custom_call_target="tpu_custom_call" | custom-call | tf_op jit(solution)/shard_map/heads_backward/pallas_call | solution.py:499
  457.2 9.8 %convolution_convert_fusion = bf16[2048,1152]{1,0:T(8,128)(2,1)} fusion(bf16[1024,2048]{1,0:T(8,128)(2,1)} %constant_dynamic-update-slice_fusion.3, bf16[1024,1152]{1,0:T(8,128)(2,1)} %bitcast.199), kind=kOutput, calls=%fused_computation | convolution fusion | flops 4834197504 | bytes 11272192 | tf_op jit(solution)/shard_map/dot_general | solution.py:663
  468.7 5.2 pad_maximum_fusion
  474.0 9.6 %fusion.8 = bf16[1024,2048]{1,0:T(8,128)(2,1)} fusion(bf16[1024,1152]{1,0:T(8,128)(2,1)} %bitcast.200, bf16[2048,1408]{1,0:T(8,128)(2,1)} %all-gather.4.cloned.1.call-done), kind=kOutput, calls=%fused_computation.16 | convolution fusion | flops 4833935360 | bytes 11272192 | tf_op jit(solution)/shard_map/dot_general | solution.py:659
  500.6 11.6 %all-to-all-done.4 = bf16[8,64,704]{2,1,0:T(8,128)(2,1)S(1)} async-done(((bf16[8,64,704]{2,1,0:T(8,128)(2,1)}), bf16[8,64,704]{2,1,0:T(8,128)(2,1)S(1)}, u32[]{:S(2)}, u32[]{:S(2)}) %all-to-all-start.4) | async-done | bytes 720928 | tf_op jit(solution)/shard_map/all_to_all | solution.py:607
  527.5 8.0 %collective-permute-done.37 = bf16[2,64,2048]{2,1,0:T(8,128)(2,1)S(1)} collective-permute-done((bf16[2,64,2048]{2,1,0:T(8,128)(2,1)S(1)}, bf16[2,64,2048]{2,1,0:T(8,128)(2,1)S(1)}, u32[]{:S(2)}, u32[]{:S(2)}) %collective-permute-start.37) | collective-permute-done | bytes 524320 | tf_op jit(solution)/shard_map/ppermute | solution.py:530
  538.6 8.2 %collective-permute-done.32 = bf16[2,64,2048]{2,1,0:T(8,128)(2,1)S(1)} collective-permute-done((bf16[2,64,2048]{2,1,0:T(8,128)(2,1)S(1)}, bf16[2,64,2048]{2,1,0:T(8,128)(2,1)S(1)}, u32[]{:S(2)}, u32[]{:S(2)}) %collective-permute-start.32) | collective-permute-done | bytes 524320 | tf_op jit(solution)/shard_map/ppermute | solution.py:530
  564.3 15.8 %collective-permute-done.42 = f32[226,128]{1,0:T(8,128)S(1)} collective-permute-done((f32[226,128]{1,0:T(8,128)S(1)}, f32[226,128]{1,0:T(8,128)S(1)}, u32[]{:S(2)}, u32[]{:S(2)}) %collective-permute-start.42) | collective-permute-done | bytes 115744 | tf_op jit(solution)/shard_map/ppermute | solution.py:530
  588.4 9.0 %reduce-scatter.6.cloned.1.call-done = bf16[512,1408]{1,0:T(8,128)(2,1)} async-done(((bf16[2048,1408]{1,0:T(8,128)(2,1)}), bf16[512,1408]{1,0:T(8,128)(2,1)}) %reduce-scatter.6.cloned.1.call-update) | async-done | bytes 1441808 | tf_op jit(solution)/shard_map/reduce_scatter | solution.py:602
  612.3 5.4 reshape.339
  617.7 5.4 copy.63
  (412 shorter events, 270.6 us)
Async XLA Ops:
  14.2 24.7 %all-to-all-start = ((bf16[8,64,1152]{2,1,0:T(8,128)(2,1)}), bf16[8,64,1152]{2,1,0:T(8,128)(2,1)S(1)}, u32[]{:S(2)}, u32[]{:S(2)}) async-start(bf16[8,64,1152]{2,1,0:T(8,128)(2,1)} %fusion.15), calls=%async_computation | async-start | bytes 2359296 | tf_op jit(solution)/shard_map/all_to_all | solution.py:593
  19.3 130.0 %all-gather.4.cloned.1.call-start = ((), (), s32[]{:S(2)}) async-start(), calls=%async_computation.8 | async-start | bytes 7208960 | tf_op jit(solution)/shard_map/all_gather | solution.py:598
  42.7 16.3 %collective-permute-start.1 = (bf16[64,2048]{1,0:T(8,128)(2,1)}, bf16[64,2048]{1,0:T(8,128)(2,1)S(1)}, u32[]{:S(2)}, u32[]{:S(2)}) collective-permute-start(bf16[64,2048]{1,0:T(8,128)(2,1)} %get-tuple-element.134), channel_id=1, source_target_pairs={{0,2},{1,3},{2,0},{3,1},{4,6},{5,7},{6,4},{7,5},{8,10},{9,11},{10,... | collective-permute-start | bytes 786440 | tf_op jit(solution)/shard_map/ppermute | solution.py:530
  75.6 20.6 %collective-permute-start.5 = (bf16[512,2048]{1,0:T(8,128)(2,1)}, bf16[512,2048]{1,0:T(8,128)(2,1)}, u32[]{:S(2)}, u32[]{:S(2)}) collective-permute-start(bf16[512,2048]{1,0:T(8,128)(2,1)} %get-tuple-element.129), channel_id=1, source_target_pairs={{0,1},{1,0},{2,3},{3,2},{4,5},{5,4},{6,7},{7,6},{8,9},{9,8},{10,11... | collective-permute-start | bytes 6291464 | tf_op jit(solution)/shard_map/ppermute | solution.py:530
  87.8 32.6 %all-to-all-start.1 = ((bf16[8,64,2112]{2,1,0:T(8,128)(2,1)}), bf16[8,64,2112]{2,1,0:T(8,128)(2,1)}, u32[]{:S(2)}, u32[]{:S(2)}) async-start(bf16[8,64,2112]{2,1,0:T(8,128)(2,1)} %reshape.311), calls=%async_computation.1 | async-start | bytes 4456448 | tf_op jit(solution)/shard_map/all_to_all | solution.py:593
  92.3 164.8 %all-gather.6.cloned.1.call-start = ((), (), s32[]{:S(2)}) async-start(), calls=%async_computation.9 | async-start | bytes 7208960 | tf_op jit(solution)/shard_map/all_gather | solution.py:598
  151.9 168.6 %all-gather.8.cloned.1.call-start = ((), (), s32[]{:S(2)}) async-start(), calls=%async_computation.10 | async-start | bytes 3932160 | tf_op jit(solution)/shard_map/all_gather | solution.py:598
  199.1 25.2 %collective-permute-start.6 = (bf16[4,128,2048]{2,1,0:T(8,128)(2,1)}, bf16[4,128,2048]{2,1,0:T(8,128)(2,1)}, u32[]{:S(2)}, u32[]{:S(2)}) collective-permute-start(bf16[4,128,2048]{2,1,0:T(8,128)(2,1)} %bitcast.17), channel_id=1, source_target_pairs={{0,1},{1,0},{2,3},{3,2},{4,5},{5,4},{6,7},{7,6},{8,9},{9,8},{10,11... | collective-permute-start | bytes 6291464 | tf_op jit(solution)/shard_map/ppermute | solution.py:530
  201.7 17.5 %collective-permute-start.18 = (bf16[128,2048]{1,0:T(8,128)(2,1)}, bf16[128,2048]{1,0:T(8,128)(2,1)S(1)}, u32[]{:S(2)}, u32[]{:S(2)}) collective-permute-start(bf16[128,2048]{1,0:T(8,128)(2,1)} %pad_maximum_fusion.11), channel_id=1, source_target_pairs={{0,2},{1,3},{2,0},{3,1},{4,6},{5,7},{6,4},{7,5},{8,10},{9,11},{10,... | collective-permute-start | bytes 1572872 | tf_op jit(solution)/shard_map/ppermute | solution.py:530
  206.3 217.5 %reduce-scatter.4.cloned.1.call-start = ((), (), s32[]{:S(2)}) async-start(), calls=%async_computation.11 | async-start | bytes 3604480 | tf_op jit(solution)/shard_map/reduce_scatter | solution.py:602
  209.6 13.2 %collective-permute-start.19 = (bf16[128,2048]{1,0:T(8,128)(2,1)S(1)}, bf16[128,2048]{1,0:T(8,128)(2,1)S(1)}, u32[]{:S(2)}, u32[]{:S(2)}) collective-permute-start(bf16[128,2048]{1,0:T(8,128)(2,1)S(1)} %pad_maximum_fusion.12), channel_id=1, source_target_pairs={{0,4},{1,5},{2,6},{3,7},{4,0},{5,1},{6,2},{7,3},{8,12},{9,13},{10,... | collective-permute-start | bytes 1572872 | tf_op jit(solution)/shard_map/ppermute | solution.py:530
  230.8 65.6 %collective-permute-start.20 = (bf16[512,2048]{1,0:T(8,128)(2,1)}, bf16[512,2048]{1,0:T(8,128)(2,1)}, u32[]{:S(2)}, u32[]{:S(2)}) collective-permute-start(bf16[512,2048]{1,0:T(8,128)(2,1)} %get-tuple-element.123), channel_id=1, source_target_pairs={{0,1},{1,0},{2,3},{3,2},{4,5},{5,4},{6,7},{7,6},{8,9},{9,8},{10,11... | collective-permute-start | bytes 6291464 | tf_op jit(solution)/shard_map/ppermute | solution.py:530
  281.8 13.8 %collective-permute-start.13 = (bf16[128,2048]{1,0:T(8,128)(2,1)S(1)}, bf16[128,2048]{1,0:T(8,128)(2,1)S(1)}, u32[]{:S(2)}, u32[]{:S(2)}) collective-permute-start(bf16[128,2048]{1,0:T(8,128)(2,1)S(1)} %pad_maximum_fusion.9), channel_id=1, source_target_pairs={{0,2},{1,3},{2,0},{3,1},{4,6},{5,7},{6,4},{7,5},{8,10},{9,11},{10,... | collective-permute-start | bytes 1572872 | tf_op jit(solution)/shard_map/ppermute | solution.py:530
  328.0 228.0 %reduce-scatter.8.cloned.1.call-start = ((), (), s32[]{:S(2)}) async-start(), calls=%async_computation.13 | async-start | bytes 7208960 | tf_op jit(solution)/shard_map/reduce_scatter | solution.py:602
  356.1 14.3 %collective-permute-start.22 = (bf16[2,64,2048]{2,1,0:T(8,128)(2,1)}, bf16[2,64,2048]{2,1,0:T(8,128)(2,1)}, u32[]{:S(2)}, u32[]{:S(2)}) collective-permute-start(bf16[2,64,2048]{2,1,0:T(8,128)(2,1)} %slice.359), channel_id=1, source_target_pairs={{0,2},{1,3},{2,0},{3,1},{4,6},{5,7},{6,4},{7,5},{8,10},{9,11},{10,... | collective-permute-start | bytes 1572872 | tf_op jit(solution)/shard_map/ppermute | solution.py:530
  357.3 14.0 %collective-permute-start.24 = (bf16[2,64,2048]{2,1,0:T(8,128)(2,1)}, bf16[2,64,2048]{2,1,0:T(8,128)(2,1)}, u32[]{:S(2)}, u32[]{:S(2)}) collective-permute-start(bf16[2,64,2048]{2,1,0:T(8,128)(2,1)} %slice.437), channel_id=1, source_target_pairs={{0,4},{1,5},{2,6},{3,7},{4,0},{5,1},{6,2},{7,3},{8,12},{9,13},{10,... | collective-permute-start | bytes 1572872 | tf_op jit(solution)/shard_map/ppermute | solution.py:530
  367.8 229.5 %reduce-scatter.6.cloned.1.call-start = ((), (), s32[]{:S(2)}) async-start(), calls=%async_computation.12 | async-start | bytes 7208960 | tf_op jit(solution)/shard_map/reduce_scatter | solution.py:602
  488.6 28.7 %collective-permute-start.36 = (bf16[4,128,2048]{2,1,0:T(8,128)(2,1)}, bf16[4,128,2048]{2,1,0:T(8,128)(2,1)}, u32[]{:S(2)}, u32[]{:S(2)}) collective-permute-start(bf16[4,128,2048]{2,1,0:T(8,128)(2,1)} %bitcast.41), channel_id=1, source_target_pairs={{0,1},{1,0},{2,3},{3,2},{4,5},{5,4},{6,7},{7,6},{8,9},{9,8},{10,11... | collective-permute-start | bytes 6291464 | tf_op jit(solution)/shard_map/ppermute | solution.py:530
  494.9 26.9 %collective-permute-start.31 = (bf16[4,128,2048]{2,1,0:T(8,128)(2,1)}, bf16[4,128,2048]{2,1,0:T(8,128)(2,1)}, u32[]{:S(2)}, u32[]{:S(2)}) collective-permute-start(bf16[4,128,2048]{2,1,0:T(8,128)(2,1)} %bitcast.34), channel_id=1, source_target_pairs={{0,1},{1,0},{2,3},{3,2},{4,5},{5,4},{6,7},{7,6},{8,9},{9,8},{10,11... | collective-permute-start | bytes 6291464 | tf_op jit(solution)/shard_map/ppermute | solution.py:530
  496.1 16.1 %all-to-all-start.4 = ((bf16[8,64,704]{2,1,0:T(8,128)(2,1)}), bf16[8,64,704]{2,1,0:T(8,128)(2,1)S(1)}, u32[]{:S(2)}, u32[]{:S(2)}) async-start(bf16[8,64,704]{2,1,0:T(8,128)(2,1)} %bitcast.58), calls=%async_computation.7 | async-start | bytes 1572864 | tf_op jit(solution)/shard_map/all_to_all | solution.py:607
  520.6 14.9 %collective-permute-start.37 = (bf16[2,64,2048]{2,1,0:T(8,128)(2,1)S(1)}, bf16[2,64,2048]{2,1,0:T(8,128)(2,1)S(1)}, u32[]{:S(2)}, u32[]{:S(2)}) collective-permute-start(bf16[2,64,2048]{2,1,0:T(8,128)(2,1)S(1)} %slice.389), channel_id=1, source_target_pairs={{0,2},{1,3},{2,0},{3,1},{4,6},{5,7},{6,4},{7,5},{8,10},{9,11},{10,... | collective-permute-start | bytes 1572872 | tf_op jit(solution)/shard_map/ppermute | solution.py:530
  521.1 14.8 %collective-permute-start.39 = (bf16[2,64,2048]{2,1,0:T(8,128)(2,1)S(1)}, bf16[2,64,2048]{2,1,0:T(8,128)(2,1)S(1)}, u32[]{:S(2)}, u32[]{:S(2)}) collective-permute-start(bf16[2,64,2048]{2,1,0:T(8,128)(2,1)S(1)} %slice.461), channel_id=1, source_target_pairs={{0,4},{1,5},{2,6},{3,7},{4,0},{5,1},{6,2},{7,3},{8,12},{9,13},{10,... | collective-permute-start | bytes 1572872 | tf_op jit(solution)/shard_map/ppermute | solution.py:530
  524.5 22.3 %collective-permute-start.32 = (bf16[2,64,2048]{2,1,0:T(8,128)(2,1)S(1)}, bf16[2,64,2048]{2,1,0:T(8,128)(2,1)S(1)}, u32[]{:S(2)}, u32[]{:S(2)}) collective-permute-start(bf16[2,64,2048]{2,1,0:T(8,128)(2,1)S(1)} %slice.377), channel_id=1, source_target_pairs={{0,2},{1,3},{2,0},{3,1},{4,6},{5,7},{6,4},{7,5},{8,10},{9,11},{10,... | collective-permute-start | bytes 1572872 | tf_op jit(solution)/shard_map/ppermute | solution.py:530
  526.0 21.2 %collective-permute-start.34 = (bf16[2,64,2048]{2,1,0:T(8,128)(2,1)S(1)}, bf16[2,64,2048]{2,1,0:T(8,128)(2,1)S(1)}, u32[]{:S(2)}, u32[]{:S(2)}) collective-permute-start(bf16[2,64,2048]{2,1,0:T(8,128)(2,1)S(1)} %slice.452), channel_id=1, source_target_pairs={{0,4},{1,5},{2,6},{3,7},{4,0},{5,1},{6,2},{7,3},{8,12},{9,13},{10,... | collective-permute-start | bytes 1572872 | tf_op jit(solution)/shard_map/ppermute | solution.py:530
  536.3 15.9 %collective-permute-start.40 = (bf16[64,2048]{1,0:T(8,128)(2,1)S(1)}, bf16[64,2048]{1,0:T(8,128)(2,1)S(1)}, u32[]{:S(2)}, u32[]{:S(2)}) collective-permute-start(bf16[64,2048]{1,0:T(8,128)(2,1)S(1)} %fusion.43), channel_id=1, source_target_pairs={{0,2},{1,3},{2,0},{3,1},{4,6},{5,7},{6,4},{7,5},{8,10},{9,11},{10,... | collective-permute-start | bytes 786440 | tf_op jit(solution)/shard_map/ppermute | solution.py:530
  538.0 14.8 %collective-permute-start.38 = (bf16[64,2048]{1,0:T(8,128)(2,1)S(1)}, bf16[64,2048]{1,0:T(8,128)(2,1)S(1)}, u32[]{:S(2)}, u32[]{:S(2)}) collective-permute-start(bf16[64,2048]{1,0:T(8,128)(2,1)S(1)} %fusion.42), channel_id=1, source_target_pairs={{0,4},{1,5},{2,6},{3,7},{4,0},{5,1},{6,2},{7,3},{8,12},{9,13},{10,... | collective-permute-start | bytes 786440 | tf_op jit(solution)/shard_map/ppermute | solution.py:530
  550.0 14.3 %collective-permute-start.33 = (bf16[64,2048]{1,0:T(8,128)(2,1)}, bf16[64,2048]{1,0:T(8,128)(2,1)S(1)}, u32[]{:S(2)}, u32[]{:S(2)}) collective-permute-start(bf16[64,2048]{1,0:T(8,128)(2,1)} %fusion.40), channel_id=1, source_target_pairs={{0,4},{1,5},{2,6},{3,7},{4,0},{5,1},{6,2},{7,3},{8,12},{9,13},{10,... | collective-permute-start | bytes 786440 | tf_op jit(solution)/shard_map/ppermute | solution.py:530
  556.0 43.7 %all-to-all-start.3 = ((bf16[8,64,1408]{2,1,0:T(8,128)(2,1)}), bf16[8,64,1408]{2,1,0:T(8,128)(2,1)}, u32[]{:S(2)}, u32[]{:S(2)}) async-start(bf16[8,64,1408]{2,1,0:T(8,128)(2,1)} %bitcast.190), calls=%async_computation.6 | async-start | bytes 2883584 | tf_op jit(solution)/shard_map/all_to_all | solution.py:607
  563.7 16.4 %collective-permute-start.42 = (f32[226,128]{1,0:T(8,128)S(1)}, f32[226,128]{1,0:T(8,128)S(1)}, u32[]{:S(2)}, u32[]{:S(2)}) collective-permute-start(f32[226,128]{1,0:T(8,128)S(1)} %bitcast_add_fusion.3), channel_id=1, source_target_pairs={{0,16},{8,24},{16,0},{24,8},{1,17},{9,25},{17,1},{25,9},{2,18},{10... | collective-permute-start | bytes 347144 | tf_op jit(solution)/shard_map/ppermute | solution.py:530
  587.0 20.2 %collective-permute-start.45 = (f32[226,128]{1,0:T(8,128)S(1)}, f32[226,128]{1,0:T(8,128)}, u32[]{:S(2)}, u32[]{:S(2)}) collective-permute-start(f32[226,128]{1,0:T(8,128)S(1)} %add.213), channel_id=1, source_target_pairs={{0,4},{1,5},{2,6},{3,7},{4,0},{5,1},{6,2},{7,3},{8,12},{9,13},{10,... | collective-permute-start | bytes 347144 | tf_op jit(solution)/shard_map/ppermute | solution.py:530
  599.7 29.0 %all-to-all-start.2 = ((bf16[8,64,1152]{2,1,0:T(8,128)(2,1)}), bf16[8,64,1152]{2,1,0:T(8,128)(2,1)S(1)}, u32[]{:S(2)}, u32[]{:S(2)}) async-start(bf16[8,64,1152]{2,1,0:T(8,128)(2,1)} %bitcast.181), calls=%async_computation.4 | async-start | bytes 2359296 | tf_op jit(solution)/shard_map/all_to_all | solution.py:607
  609.8 18.0 %collective-permute-start.46 = (bf16[64,2048]{1,0:T(8,128)(2,1)S(1)}, bf16[64,2048]{1,0:T(8,128)(2,1)S(1)}, u32[]{:S(2)}, u32[]{:S(2)}) collective-permute-start(bf16[64,2048]{1,0:T(8,128)(2,1)S(1)} %reshape.327), channel_id=1, source_target_pairs={{0,0},{1,4},{2,8},{3,12},{4,16},{5,20},{6,24},{7,28},{8,1},{9,5},{... | collective-permute-start | bytes 786440 | tf_op jit(solution)/shard_map/ppermute | solution.py:784
  (87 other events, 1061.3 us)
Sparse Core Ops, SparseCore 0:
  40.2 109.0 all-gather.3
  152.1 104.9 all-gather.5
  258.7 61.7 all-gather.7
  328.1 54.8 reduce-scatter.3
  385.1 102.0 reduce-scatter.7
  489.4 107.8 reduce-scatter.5

commit v3 on v2

--- a/solution.py
+++ b/solution.py
@@ -582,10 +582,12 @@
 
 def sum_all(value):
     for axis in both:
-        bit = 1
-        while bit < lax.axis_size(axis):
-            value = value + swap(value, axis, bit)
-            bit *= 2
+        size, bit = lax.axis_size(axis), 1
+        if size.bit_length() % 2 == 0:
+            value, bit = value + swap(value, axis, 1), 2
+        while bit < size:
+            one, two, three = (swap(value, axis, k * bit) for k in (1, 2, 3))
+            value, bit = (value + one) + (two + three), 4 * bit
     return value
 
 
@@ -645,10 +647,52 @@
     )(pieces)
 
 
-def row_pairs(inverse):
+def hop(step, back):
     groups, peers = lax.axis_size("dp"), lax.axis_size("seq")
-    pairs = [(j * groups + d, d * peers + j) for d in range(groups) for j in range(peers)]
-    return [(b, a) for a, b in pairs] if inverse else pairs
+    ratio = peers // groups
+    pairs = [(s, (s + step) % groups * ratio + s // groups) for s in range(peers)]
+    return [(b, a) for a, b in pairs] if back else pairs
+
+
+def pick(parts, index):
+    return lax.dynamic_index_in_dim(parts, index, 0, keepdims=False)
+
+
+def out_rows_near(rows):
+    return jnp.stack([rows] + [swap(rows, "dp", k) for k in range(1, lax.axis_size("dp"))])
+
+
+def out_rows_here(parts):
+    groups, ratio = lax.axis_size("dp"), lax.axis_size("seq") // lax.axis_size("dp")
+    place, here = lax.axis_index("dp"), lax.axis_index("seq")
+    got = jnp.stack(
+        [
+            lax.ppermute(pick(parts, (here + t) % groups ^ place), "seq", hop(t, False))
+            for t in range(groups)
+        ]
+    )
+    return jnp.concatenate([pick(got, (here // ratio - e) % groups) for e in range(groups)])
+
+
+def out_rows_sent(term):
+    groups, ratio = lax.axis_size("dp"), lax.axis_size("seq") // lax.axis_size("dp")
+    here = lax.axis_index("seq")
+    parts = term.reshape(groups, -1, term.shape[1])
+    got = jnp.stack(
+        [
+            lax.ppermute(pick(parts, (here // ratio - t) % groups), "seq", hop(t, True))
+            for t in range(groups)
+        ]
+    )
+    return jnp.stack([pick(got, (z - here) % groups) for z in range(groups)])
+
+
+def out_rows_sum(parts):
+    place = lax.axis_index("dp")
+    total = pick(parts, place).astype(f32)
+    for k in range(1, lax.axis_size("dp")):
+        total = total + swap(pick(parts, place ^ k), "dp", k).astype(f32)
+    return total
 
 
 def dot32(left, right):
@@ -694,7 +738,7 @@
     valid = (positions < lengths[:, None]).astype(f32).reshape(-1, 1)
     inputs = tokens.reshape(-1, width).astype(f32)
 
-    out_rows = lax.ppermute(out_weight, both, row_pairs(False))
+    out_parts = out_rows_near(out_weight)
     main = mix_weight[:, : 4 * width].reshape(own_rows, 4, peers, cols).transpose(2, 0, 1, 3)
     logits = mix_weight[:, 4 * width :].reshape(own_rows, 2, peers, local_heads)
     logits = logits.transpose(2, 0, 1, 3).reshape(peers, own_rows, logit_cols)
@@ -703,25 +747,22 @@
     )
     wide_cols = mix_rows.shape[1]
     normed, norm_back = jax.vjp(rms_scale, inputs, norm_gain)
-    mix_rows, normed_low, mlp_in_rows, mlp_out_rows = tie(
-        mix_rows, normed.astype(low), mlp_in_weight, mlp_out_weight
-    )
-    mixer_here = gather_dp(
-        jnp.concatenate([mix_rows, out_rows.reshape(mix_rows.shape[0], -1)], axis=1)
-    )
+    gate_up = mlp_in_weight.reshape(own_rows, 2, peers, own_units).transpose(2, 0, 1, 3)
+    down = mlp_out_weight.reshape(own_rows, peers, 1, own_units).transpose(1, 0, 2, 3)
+    mlp_pieces = jnp.concatenate([gate_up, down], axis=2).reshape(peers, own_rows, 3 * own_units)
+    mix_rows, normed_low, mlp_pieces, out_parts = tie(
+        mix_rows, normed.astype(low), mlp_pieces, out_parts
+    )
+    mix_here = gather_dp(mix_rows)
     normed_all = gather_seq(normed_low)
-    gate_up = mlp_in_rows.reshape(own_rows, 2, peers, own_units).transpose(2, 0, 1, 3)
-    down = mlp_out_rows.reshape(own_rows, peers, 1, own_units).transpose(1, 0, 2, 3)
-    mlp_pieces = jnp.concatenate([gate_up, down], axis=2).reshape(peers, own_rows, 3 * own_units)
     mlp_rows = to_columns(mlp_pieces)
     cotangent = valid * grad_out.reshape(-1, width).astype(f32)
-    mixer_here, mlp_rows, normed_all, cot_low = tie(
-        mixer_here, mlp_rows, normed_all, cotangent.astype(low)
-    )
+    mix_here, out_parts, mlp_rows, normed_all, cot_low = tie(
+        mix_here, out_parts, mlp_rows, normed_all, cotangent.astype(low)
+    )
+    out_here = out_rows_here(out_parts)
     in_here = gather_dp(mlp_rows[:, : 2 * own_units])
     down_here = gather_dp(mlp_rows[:, 2 * own_units :])
-    mix_here = mixer_here[:, :wide_cols]
-    out_here = mixer_here[:, wide_cols:].reshape(-1, width)
 
     projected = dot32(normed_all, mix_here).astype(low).reshape(peers, micro, seq_rows, -1)
     conv_here = lax.dynamic_index_in_dim(
@@ -745,18 +786,19 @@
     gate_up = dot32(second_all, in_here).astype(low)
     activated, swiglu_back = jax.vjp(swiglu, gate_up.astype(f32))
     activated_low = activated.astype(low)
-    activated_low, down_here = tie(activated_low, down_here)
     grad_down_term = t_dot(cot_all, activated_low).astype(low)
-    cot_all, grad_down_term = tie(cot_all, grad_down_term)
+    cot_all, grad_down_term, down_here = tie(cot_all, grad_down_term, down_here)
     (grad_gate_up,) = swiglu_back(dot32(cot_all, down_here))
     grad_gate_low = grad_gate_up.astype(low)
     grad_second = scatter_seq(dot_t(grad_gate_low, in_here))
     grad_hidden_norm, grad_mlp_gain = second_back(grad_second)
     grad_hidden = cotangent + grad_hidden_norm
-    branch_all = gather_seq(grad_hidden.astype(low))
+    branch_low = grad_hidden.astype(low)
+    branch_all = gather_seq(branch_low)
     grad_down = sum_dp(grad_down_term)
     grad_in = sum_dp(t_dot(second_all, grad_gate_low))
 
+    branch_all, activated_low = tie(branch_all, activated_low)
     grad_mixed = dot_t(branch_all, out_here).reshape(peers, micro, seq_rows, cols)
     grad_mixed, grad_down = tie(grad_mixed, grad_down)
     grad_out_term = t_dot(mixed_low, branch_all).astype(low)
@@ -774,17 +816,11 @@
     )
     grad_projected = grad_projected.reshape(-1, wide_cols)
     grad_mix_term = t_dot(normed_all, grad_projected).astype(low)
-    grad_mix_term, grad_projected, activated_low = tie(
-        grad_mix_term, grad_projected, activated_low
-    )
-    mixer_own = sum_dp(
-        jnp.concatenate([grad_mix_term, grad_out_term.reshape(width, -1)], axis=1)
-    )
-    grad_mix = to_owners(mixer_own[:, :wide_cols])
-    grad_out_own = lax.ppermute(
-        mixer_own[:, wide_cols:].reshape(own_rows, width), both, row_pairs(True)
-    )
-    grad_normed = scatter_seq(dot_t(grad_projected, mix_here))
+    grad_mix_term, grad_projected = tie(grad_mix_term, grad_projected)
+    mix_own = sum_dp(grad_mix_term)
+    out_parts = out_rows_sent(grad_out_term)
+    grad_normed, grad_in = scatter_seq(dot_t(grad_projected, mix_here), to_owners(grad_in))
+    grad_down = to_owners(grad_down)
     grad_inputs_norm, grad_norm_gain = norm_back(grad_normed)
     grad_tokens = grad_hidden + grad_inputs_norm
     feed_out = scatter_seq(dot_t(activated_low, down_here))
@@ -810,10 +846,16 @@
             ]
         ).reshape(-1, LANES)
     ).reshape(-1)
+    mix_own, out_parts, summed, grad_in, grad_down = tie(
+        mix_own, out_parts, summed, grad_in, grad_down
+    )
+    grad_mix = to_owners(mix_own)
+    grad_out_own = out_rows_sum(out_parts)
+    grad_in = grad_in.reshape(peers, own_rows, 2, own_units).transpose(1, 2, 0, 3)
+    grad_in = grad_in.reshape(own_rows, 2 * units).astype(f32)
+    grad_down = grad_down.transpose(1, 0, 2).reshape(own_rows, units).astype(f32)
     ends = [sum(sizes[: i + 1]) for i in range(len(sizes))]
     sums = [summed[end - size : end] for end, size in zip(ends, sizes)]
-    grad_in = to_owners(grad_in).reshape(peers, own_rows, 2, own_units).transpose(1, 2, 0, 3)
-    grad_down = to_owners(grad_down).transpose(1, 0, 2)
     return (
         result.reshape(tokens.shape),
         grad_tokens.reshape(tokens.shape),
@@ -822,10 +864,10 @@
         sums[4].reshape(taps, 3 * width),
         sums[3][:heads],
         sums[2],
-        grad_out_own.astype(f32),
+        grad_out_own,
         sums[1],
-        grad_in.reshape(own_rows, 2 * units).astype(f32),
-        grad_down.reshape(own_rows, units).astype(f32),
+        grad_in,
+        grad_down,
     )
 
 

time: 650 us -> 633 us (0.974)
  starting transfers between devices: 65.2 us -> 99.9 us
  waiting for transfers between devices: 242 us -> 214 us
  local copies, waits for them, and re-layouts: 120 us -> 104 us
  matrix products: 82.2 us -> 75.2 us
    ppermute x45 -> x53, starting transfers between devices: 41.5 us -> 60.7 us  [swap(): lax.ppermute(value, axis, [(i, i ^ bit) for i in range(lax.axis_size(axis...]
    all_to_all x2, waiting for transfers between devices: 38.8 us -> 21 us  [to_columns(): lax.all_to_all(pieces, 'seq', split_axis=0, concat_axis=0, tiled=True)]
    ppermute x2 -> x8, starting transfers between devices: 1.35 us -> 17.5 us  [the longest x4 8.99 us: out_rows_here(): lax.ppermute(pick(parts, (here + t) % groups ^ place), 'seq', hop(t, False))]
    ppermute x2 -> x8, waiting for transfers between devices: 0.01 us -> 9.06 us  [the longest x4 5.19 us: out_rows_sent(): lax.ppermute(pick(parts, (here // ratio - t) % groups), 'seq', hop(t, True))]
    all_gather x3, waiting for transfers between devices: 52.9 us -> 43.9 us  [gather_dp(): return lax.all_gather(rows_here, 'dp', axis=0, tiled=True)]
    reduce_scatter x3, waiting for transfers between devices: 9.01 us -> 0.04 us  [sum_dp(): lax.psum_scatter(term.astype(low), 'dp', scatter_dimension=0, tiled=True)]
    unnamed x167 -> x195, local copies, waits for them, and re-layouts: 32.2 us -> 25.5 us
    ppermute x45 -> x53, waiting for transfers between devices: 130 us -> 125 us  [swap(): lax.ppermute(value, axis, [(i, i ^ bit) for i in range(lax.axis_size(axis...]
  transfers between devices with their start and end apart: 58 -> 72, of which waited for: 42 -> 42; matrix products, arithmetic and copies ran while one was open for 37% -> 36% of each run, Pallas kernels for 9% -> 9%
where the time goes in v3:
time: 633 us; the launch traced here: 623 us
  waiting for transfers between devices  214 us (34%)
  local copies, waits for them, and re-layouts  104 us (16%)
  starting transfers between devices  99.9 us (16%)
  matrix products  75.2 us (12%)
  other arithmetic  57.1 us (9%)
  Pallas kernels  56.5 us (9%)
  between operations  16.1 us (3%)
    ppermute x53, waiting for transfers between devices, swap(): lax.ppermute(value, axis, [(i, i ^ bit) for i in range(lax.axis_size(axis...  125 us
    ppermute x53, starting transfers between devices, swap(): lax.ppermute(value, axis, [(i, i ^ bit) for i in range(lax.axis_size(axis...  60.7 us
    all_gather x3, waiting for transfers between devices, gather_dp(): return lax.all_gather(rows_here, 'dp', axis=0, tiled=True)  43.9 us
    pallas_call x1, Pallas kernels, heads_backward(): pl.pallas_call(partial(backward_kernel, local_heads, perm.shape[0]), out_...  32.4 us
    dot_general x4, matrix products, dot32(): return jnp.dot(left, right, preferred_element_type=f32)  26.9 us
    unnamed x195, local copies, waits for them, and re-layouts  25.5 us
    dot_general x4, matrix products, t_dot(): lax.dot_general(left, right, (((0,), (0,)), ((), ())), preferred_element_...  24.3 us
    dot_general x4, matrix products, dot_t(): lax.dot_general(left, right, (((1,), (1,)), ((), ())), preferred_element_...  24 us
  transfers between devices with their start and end apart: 72, of which 42 were waited for; matrix products, arithmetic and copies ran while one was open for 36% of the time, Pallas kernels for 9%

profile of v3, /device:TPU:0, one launch (start us, length us, event | category | flops | bytes accessed | tf_op | source)
XLA Modules:
  0.0 622.6 jit_solution(2573033642142871185)
XLA Ops:
  7.2 5.1 collective-permute-start.2
  33.2 5.2 pad_maximum_fusion
  38.4 6.9 %reshape.299 = bf16[8,64,2112]{2,1,0:T(8,128)(2,1)} reshape(bf16[8,64,3,704]{3,2,1,0:T(4,128)(2,1)} %pad_maximum_fusion) | data formatting | bytes 4325376 | tf_op jit(solution)/shard_map/reshape | solution.py:752
  52.2 5.2 collective-permute-done.4
  62.8 8.3 %collective-permute-done.5 = bf16[128,2048]{1,0:T(8,128)(2,1)S(1)} collective-permute-done((bf16[128,2048]{1,0:T(8,128)(2,1)S(1)}, bf16[128,2048]{1,0:T(8,128)(2,1)S(1)}, u32[]{:S(2)}, u32[]{:S(2)}) %collective-permute-start.5) | collective-permute-done | bytes 524320 | tf_op jit(solution)/shard_map/ppermute | solution.py:530
  87.9 21.0 %all-to-all-done.1 = bf16[8,64,2112]{2,1,0:T(8,128)(2,1)} async-done(((bf16[8,64,2112]{2,1,0:T(8,128)(2,1)}), bf16[8,64,2112]{2,1,0:T(8,128)(2,1)}, u32[]{:S(2)}, u32[]{:S(2)}) %all-to-all-start.1) | async-done | bytes 2162720 | tf_op jit(solution)/shard_map/all_to_all | solution.py:595
  108.9 31.0 %all-gather.4.cloned.1.call-done = bf16[2048,1152]{1,0:T(8,128)(2,1)} async-done(((bf16[512,1152]{1,0:T(8,128)(2,1)}), bf16[2048,1152]{1,0:T(8,128)(2,1)}) %all-gather.4.cloned.1.call-update) | async-done | bytes 4718608 | tf_op jit(solution)/shard_map/all_gather | solution.py:600
  143.1 9.8 %convolution_convert_fusion.6 = bf16[1024,1152]{1,0:T(8,128)(2,1)} fusion(bf16[1024,2048]{1,0:T(8,128)(2,1)} %constant_dynamic-update-slice_fusion.3, bf16[2048,1152]{1,0:T(8,128)(2,1)} %all-gather.4.cloned.1.call-done), kind=kOutput, calls=%fused_computation.13 | convolution fusion | flops 4833017856 | bytes 11272192 | tf_op jit(solution)/shard_map/dot_general | solution.py:699
  152.9 22.6 %heads_forward.1 = (bf16[8,2,64,256]{3,2,1,0:T(8,128)(2,1)S(1)}, bf16[8,2,64,256]{3,2,1,0:T(8,128)(2,1)S(1)}, bf16[8,2,64,768]{3,2,1,0:T(8,128)(2,1)}, f32[8,2,6...) custom-call(s32[8]{0:T(128)S(1)} %fusion.35.perm, ...), custom_call_target="tpu_custom_call" | custom-call | tf_op jit(solution)/shard_map/heads_forward/pallas_call | solution.py:463
  214.1 5.2 collective-permute-done.25
  228.3 8.3 %collective-permute-done.14 = bf16[2,64,2048]{2,1,0:T(8,128)(2,1)S(1)} collective-permute-done((bf16[2,64,2048]{2,1,0:T(8,128)(2,1)S(1)}, bf16[2,64,2048]{2,1,0:T(8,128)(2,1)S(1)}, u32[]{:S(2)}, u32[]{:S(2)}) %collective-permute-start.14) | collective-permute-done | bytes 524320 | tf_op jit(solution)/shard_map/ppermute | solution.py:530
  239.8 8.0 %all-gather.6.cloned.1.call-done = bf16[2048,1408]{1,0:T(8,128)(2,1)} async-done(((bf16[512,1408]{1,0:T(8,128)(2,1)}), bf16[2048,1408]{1,0:T(8,128)(2,1)}) %all-gather.6.cloned.1.call-update) | async-done | bytes 5767184 | tf_op jit(solution)/shard_map/all_gather | solution.py:600
  277.0 9.3 %collective-permute-done.19 = bf16[128,2048]{1,0:T(8,128)(2,1)S(1)} collective-permute-done((bf16[128,2048]{1,0:T(8,128)(2,1)S(1)}, bf16[128,2048]{1,0:T(8,128)(2,1)S(1)}, u32[]{:S(2)}, u32[]{:S(2)}) %collective-permute-start.19) | collective-permute-done | bytes 524320 | tf_op jit(solution)/shard_map/ppermute | solution.py:530
  291.4 6.6 %fusion = f32[1024,1408]{1,0:T(8,128)S(1)} fusion(bf16[1024,2048]{1,0:T(8,128)(2,1)S(1)} %constant_dynamic-update-slice_fusion.10, bf16[2048,1408]{1,0:T(8,128)(2,1)S(1)} %bitcast.242), kind=kOutput, calls=%fused_computation.9 | convolution fusion | flops 5908463616 | bytes 15728640 | tf_op jit(solution)/shard_map/dot_general | solution.py:699
  306.3 4.9 all-gather.8.cloned.1.call-done
  311.5 9.1 %fusion.23 = (f32[1024,704]{1,0:T(8,128)S(1)}, f32[1024,704]{1,0:T(8,128)S(1)}) fusion(f32[1024,1408]{1,0:T(8,128)} %copy-done.18, bf16[1024,2048]{1,0:T(8,128)(2,1)} %copy-done.55, bf16[2048,704]{1,0:T(8,128)(2,1)} %all-gather.8.cloned.1.call-done), kind=kOutput, calls=%fused_computation.106 | convolution fusion | flops 2961440768 | bytes 18612224 | tf_op jit(solution)/shard_map/dot_general | solution.py:699
  320.6 8.8 %convolution_convert_fusion.4 = bf16[1024,2048]{1,0:T(8,128)(2,1)S(1)} fusion(bf16[2048,1408]{1,0:T(8,128)(2,1)} %all-gather.6.cloned.1.call-done, f32[1024,704]{1,0:T(8,128)S(1)} %get-tuple-element.102, f32[1024,704]{1,0:T(8,128)S(1)} %get-tuple-element.101), kind=kOutput, calls=%fused_computation.11 | convolution fusion | flops 5910560768 | bytes 15728640 | tf_op jit(solution)/shard_map/dot_general | solution.py:703
  342.0 8.9 %convolution_convert_fusion.1 = bf16[2048,1408]{1,0:T(8,128)(2,1)} fusion(bf16[1024,2048]{1,0:T(8,128)(2,1)S(1)} %copy-done.57, f32[1024,704]{1,0:T(8,128)S(1)} %get-tuple-element.102, f32[1024,704]{1,0:T(8,128)S(1)} %get-tuple-element.101), kind=kOutput, calls=%fused_computation.1 | convolution fusion | flops 5911347200 | bytes 15728640 | tf_op jit(solution)/shard_map/dot_general | solution.py:707
  358.9 5.1 collective-permute-done.31
  378.8 9.3 %collective-permute-done.34 = bf16[128,2048]{1,0:T(8,128)(2,1)S(1)} collective-permute-done((bf16[128,2048]{1,0:T(8,128)(2,1)S(1)}, bf16[128,2048]{1,0:T(8,128)(2,1)S(1)}, u32[]{:S(2)}, u32[]{:S(2)}) %collective-permute-start.34) | collective-permute-done | bytes 524320 | tf_op jit(solution)/shard_map/ppermute | solution.py:530
  396.1 32.4 %heads_backward.1 = (bf16[8,2,64,1152]{3,2,1,0:T(8,128)(2,1)}, f32[4,768]{1,0:T(4,128)S(1)}, f32[1,128]{1,0:T(1,128)S(1)}, f32[1,128]{1,0:T(1,128)S(1)}) custom-call(s32[8]{0:T(128)S(1)} %fusion.35.perm, f32[8,2,64,256]{3,2,1,0:T(8,128)S(1)} %bitcast.195, bf16[8,2,64,1152]{3,2,1,0:T(8,128)(2,1)} %bitcast.205, f32[4,768]{1,0:T(4,128)S(1)} %bitcast.197, ...), custom_call_target="tpu_custom_call" | custom-call | tf_op jit(solution)/shard_map/heads_backward/pallas_call | solution.py:499
  428.4 9.7 %convolution_convert_fusion = bf16[2048,1152]{1,0:T(8,128)(2,1)} fusion(bf16[1024,2048]{1,0:T(8,128)(2,1)} %constant_dynamic-update-slice_fusion.3, bf16[1024,1152]{1,0:T(8,128)(2,1)} %bitcast.243), kind=kOutput, calls=%fused_computation | convolution fusion | flops 4834197504 | bytes 11272192 | tf_op jit(solution)/shard_map/dot_general | solution.py:707
  438.1 5.6 convolution_convert_fusion.7
  448.1 8.3 %convolution_convert_fusion.3 = bf16[1024,2048]{1,0:T(8,128)(2,1)S(1)} fusion(bf16[1024,1152]{1,0:T(8,128)(2,1)S(1)} %bitcast.244, bf16[2048,1152]{1,0:T(8,128)(2,1)} %all-gather.4.cloned.1.call-done), kind=kOutput, calls=%fused_computation.10 | convolution fusion | flops 4833935360 | bytes 11272192 | tf_op jit(solution)/shard_map/dot_general | solution.py:703
  501.4 4.6 all-to-all-start.2
  505.9 4.6 collective-permute-done.44
  517.0 14.4 %all-to-all-done.2 = bf16[8,64,1408]{2,1,0:T(8,128)(2,1)S(1)} async-done(((bf16[8,64,1408]{2,1,0:T(8,128)(2,1)}), bf16[8,64,1408]{2,1,0:T(8,128)(2,1)S(1)}, u32[]{:S(2)}, u32[]{:S(2)}) %all-to-all-start.2) | async-done | bytes 1441824 | tf_op jit(solution)/shard_map/all_to_all | solution.py:609
  541.3 11.5 %collective-permute-done.46 = bf16[64,2048]{1,0:T(8,128)(2,1)S(1)} collective-permute-done((bf16[64,2048]{1,0:T(8,128)(2,1)S(1)}, bf16[64,2048]{1,0:T(8,128)(2,1)S(1)}, u32[]{:S(2)}, u32[]{:S(2)}) %collective-permute-start.46) | collective-permute-done | bytes 262176 | tf_op jit(solution)/shard_map/ppermute | solution.py:530
  559.5 8.8 %collective-permute-done.52 = f32[226,128]{1,0:T(8,128)S(1)} collective-permute-done((f32[226,128]{1,0:T(8,128)S(1)}, f32[226,128]{1,0:T(8,128)S(1)}, u32[]{:S(2)}, u32[]{:S(2)}) %collective-permute-start.52) | collective-permute-done | bytes 115744 | tf_op jit(solution)/shard_map/ppermute | solution.py:530
  591.2 5.3 reshape.328
  596.4 5.4 copy.62
  601.8 4.7 reshape.326
  (465 shorter events, 292.8 us)
Async XLA Ops:
  7.2 38.3 %collective-permute-start.2 = (bf16[64,2048]{1,0:T(8,128)(2,1)}, bf16[64,2048]{1,0:T(8,128)(2,1)S(1)}, u32[]{:S(2)}, u32[]{:S(2)}) collective-permute-start(bf16[64,2048]{1,0:T(8,128)(2,1)} %param.19), channel_id=1, source_target_pairs={{0,24},{8,16},{16,8},{24,0},{1,25},{9,17},{17,9},{25,1},{2,26},{10... | collective-permute-start | bytes 786440 | tf_op jit(solution)/shard_map/ppermute | solution.py:530
  12.3 33.2 %collective-permute-start.1 = (bf16[64,2048]{1,0:T(8,128)(2,1)}, bf16[64,2048]{1,0:T(8,128)(2,1)S(1)}, u32[]{:S(2)}, u32[]{:S(2)}) collective-permute-start(bf16[64,2048]{1,0:T(8,128)(2,1)} %param.19), channel_id=1, source_target_pairs={{0,16},{8,24},{16,0},{24,8},{1,17},{9,25},{17,1},{25,9},{2,18},{10... | collective-permute-start | bytes 786440 | tf_op jit(solution)/shard_map/ppermute | solution.py:530
  12.3 33.2 %collective-permute-start = (bf16[64,2048]{1,0:T(8,128)(2,1)}, bf16[64,2048]{1,0:T(8,128)(2,1)}, u32[]{:S(2)}, u32[]{:S(2)}) collective-permute-start(bf16[64,2048]{1,0:T(8,128)(2,1)} %param.19), channel_id=1, source_target_pairs={{0,8},{8,0},{16,24},{24,16},{1,9},{9,1},{17,25},{25,17},{2,10},{10... | collective-permute-start | bytes 786440 | tf_op jit(solution)/shard_map/ppermute | solution.py:530
  17.8 29.8 %all-to-all-start = ((bf16[8,64,1152]{2,1,0:T(8,128)(2,1)}), bf16[8,64,1152]{2,1,0:T(8,128)(2,1)S(1)}, u32[]{:S(2)}, u32[]{:S(2)}) async-start(bf16[8,64,1152]{2,1,0:T(8,128)(2,1)} %fusion.5), calls=%async_computation | async-start | bytes 2359296 | tf_op jit(solution)/shard_map/all_to_all | solution.py:595
  21.7 118.2 %all-gather.4.cloned.1.call-start = ((), (), s32[]{:S(2)}) async-start(), calls=%async_computation.8 | async-start | bytes 5898240 | tf_op jit(solution)/shard_map/all_gather | solution.py:600
  76.5 32.4 %all-to-all-start.1 = ((bf16[8,64,2112]{2,1,0:T(8,128)(2,1)}), bf16[8,64,2112]{2,1,0:T(8,128)(2,1)}, u32[]{:S(2)}, u32[]{:S(2)}) async-start(bf16[8,64,2112]{2,1,0:T(8,128)(2,1)} %reshape.299), calls=%async_computation.1 | async-start | bytes 4456448 | tf_op jit(solution)/shard_map/all_to_all | solution.py:595
  80.9 167.0 %all-gather.6.cloned.1.call-start = ((), (), s32[]{:S(2)}) async-start(), calls=%async_computation.9 | async-start | bytes 7208960 | tf_op jit(solution)/shard_map/all_gather | solution.py:600
  142.5 168.7 %all-gather.8.cloned.1.call-start = ((), (), s32[]{:S(2)}) async-start(), calls=%async_computation.10 | async-start | bytes 3932160 | tf_op jit(solution)/shard_map/all_gather | solution.py:600
  185.4 18.8 %collective-permute-start.22 = (bf16[64,2048]{1,0:T(8,128)(2,1)}, bf16[64,2048]{1,0:T(8,128)(2,1)}, u32[]{:S(2)}, u32[]{:S(2)}) collective-permute-start(bf16[64,2048]{1,0:T(8,128)(2,1)} %get-tuple-element.165), channel_id=1, source_target_pairs={{0,2},{1,3},{2,0},{3,1},{4,6},{5,7},{6,4},{7,5},{8,10},{9,11},{10,... | collective-permute-start | bytes 786440 | tf_op jit(solution)/shard_map/ppermute | solution.py:530
  195.9 24.8 %collective-permute-start.12 = (bf16[4,128,2048]{2,1,0:T(8,128)(2,1)}, bf16[4,128,2048]{2,1,0:T(8,128)(2,1)}, u32[]{:S(2)}, u32[]{:S(2)}) collective-permute-start(bf16[4,128,2048]{2,1,0:T(8,128)(2,1)} %bitcast.33), channel_id=1, source_target_pairs={{0,1},{1,0},{2,3},{3,2},{4,5},{5,4},{6,7},{7,6},{8,9},{9,8},{10,11... | collective-permute-start | bytes 6291464 | tf_op jit(solution)/shard_map/ppermute | solution.py:530
  199.3 14.0 %collective-permute-start.24 = (bf16[128,2048]{1,0:T(8,128)(2,1)}, bf16[128,2048]{1,0:T(8,128)(2,1)S(1)}, u32[]{:S(2)}, u32[]{:S(2)}) collective-permute-start(bf16[128,2048]{1,0:T(8,128)(2,1)} %pad_maximum_fusion.14), channel_id=1, source_target_pairs={{0,2},{1,3},{2,0},{3,1},{4,6},{5,7},{6,4},{7,5},{8,10},{9,11},{10,... | collective-permute-start | bytes 1572872 | tf_op jit(solution)/shard_map/ppermute | solution.py:530
  203.7 192.3 %reduce-scatter.4.cloned.1.call-start = ((), (), s32[]{:S(2)}) async-start(), calls=%async_computation.11 | async-start | bytes 3604480 | tf_op jit(solution)/shard_map/reduce_scatter | solution.py:604
  228.3 58.8 %collective-permute-start.26 = (bf16[512,2048]{1,0:T(8,128)(2,1)}, bf16[512,2048]{1,0:T(8,128)(2,1)}, u32[]{:S(2)}, u32[]{:S(2)}) collective-permute-start(bf16[512,2048]{1,0:T(8,128)(2,1)} %get-tuple-element.160), channel_id=1, source_target_pairs={{0,1},{1,0},{2,3},{3,2},{4,5},{5,4},{6,7},{7,6},{8,9},{9,8},{10,11... | collective-permute-start | bytes 6291464 | tf_op jit(solution)/shard_map/ppermute | solution.py:530
  311.3 190.1 %reduce-scatter.6.cloned.1.call-start = ((), (), s32[]{:S(2)}) async-start(), calls=%async_computation.12 | async-start | bytes 7208960 | tf_op jit(solution)/shard_map/reduce_scatter | solution.py:604
  339.0 14.3 %collective-permute-start.28 = (bf16[2,64,2048]{2,1,0:T(8,128)(2,1)}, bf16[2,64,2048]{2,1,0:T(8,128)(2,1)}, u32[]{:S(2)}, u32[]{:S(2)}) collective-permute-start(bf16[2,64,2048]{2,1,0:T(8,128)(2,1)} %slice.331), channel_id=1, source_target_pairs={{0,2},{1,3},{2,0},{3,1},{4,6},{5,7},{6,4},{7,5},{8,10},{9,11},{10,... | collective-permute-start | bytes 1572872 | tf_op jit(solution)/shard_map/ppermute | solution.py:530
  340.5 14.0 %collective-permute-start.30 = (bf16[2,64,2048]{2,1,0:T(8,128)(2,1)}, bf16[2,64,2048]{2,1,0:T(8,128)(2,1)}, u32[]{:S(2)}, u32[]{:S(2)}) collective-permute-start(bf16[2,64,2048]{2,1,0:T(8,128)(2,1)} %slice.403), channel_id=1, source_target_pairs={{0,4},{1,5},{2,6},{3,7},{4,0},{5,1},{6,2},{7,3},{8,12},{9,13},{10,... | collective-permute-start | bytes 1572872 | tf_op jit(solution)/shard_map/ppermute | solution.py:530
  350.9 228.0 %reduce-scatter.8.cloned.1.call-start = ((), (), s32[]{:S(2)}) async-start(), calls=%async_computation.13 | async-start | bytes 5898240 | tf_op jit(solution)/shard_map/reduce_scatter | solution.py:604
  445.6 32.1 %collective-permute-start.37 = (bf16[4,128,2048]{2,1,0:T(8,128)(2,1)}, bf16[4,128,2048]{2,1,0:T(8,128)(2,1)}, u32[]{:S(2)}, u32[]{:S(2)}) collective-permute-start(bf16[4,128,2048]{2,1,0:T(8,128)(2,1)} %bitcast.47), channel_id=1, source_target_pairs={{0,1},{1,0},{2,3},{3,2},{4,5},{5,4},{6,7},{7,6},{8,9},{9,8},{10,11... | collective-permute-start | bytes 6291464 | tf_op jit(solution)/shard_map/ppermute | solution.py:530
  462.1 22.5 %collective-permute-start.42 = (bf16[4,128,2048]{2,1,0:T(8,128)(2,1)}, bf16[4,128,2048]{2,1,0:T(8,128)(2,1)}, u32[]{:S(2)}, u32[]{:S(2)}) collective-permute-start(bf16[4,128,2048]{2,1,0:T(8,128)(2,1)} %bitcast.56), channel_id=1, source_target_pairs={{0,1},{1,0},{2,3},{3,2},{4,5},{5,4},{6,7},{7,6},{8,9},{9,8},{10,11... | collective-permute-start | bytes 6291464 | tf_op jit(solution)/shard_map/ppermute | solution.py:530
  480.7 16.1 %collective-permute-start.38 = (bf16[2,64,2048]{2,1,0:T(8,128)(2,1)S(1)}, bf16[2,64,2048]{2,1,0:T(8,128)(2,1)S(1)}, u32[]{:S(2)}, u32[]{:S(2)}) collective-permute-start(bf16[2,64,2048]{2,1,0:T(8,128)(2,1)S(1)} %slice.349), channel_id=1, source_target_pairs={{0,2},{1,3},{2,0},{3,1},{4,6},{5,7},{6,4},{7,5},{8,10},{9,11},{10,... | collective-permute-start | bytes 1572872 | tf_op jit(solution)/shard_map/ppermute | solution.py:530
  484.5 14.8 %collective-permute-start.40 = (bf16[2,64,2048]{2,1,0:T(8,128)(2,1)S(1)}, bf16[2,64,2048]{2,1,0:T(8,128)(2,1)S(1)}, u32[]{:S(2)}, u32[]{:S(2)}) collective-permute-start(bf16[2,64,2048]{2,1,0:T(8,128)(2,1)S(1)} %slice.418), channel_id=1, source_target_pairs={{0,4},{1,5},{2,6},{3,7},{4,0},{5,1},{6,2},{7,3},{8,12},{9,13},{10,... | collective-permute-start | bytes 1572872 | tf_op jit(solution)/shard_map/ppermute | solution.py:530
  490.0 20.6 %collective-permute-start.44 = (bf16[2,64,2048]{2,1,0:T(8,128)(2,1)}, bf16[2,64,2048]{2,1,0:T(8,128)(2,1)S(1)}, u32[]{:S(2)}, u32[]{:S(2)}) collective-permute-start(bf16[2,64,2048]{2,1,0:T(8,128)(2,1)} %slice.425), channel_id=1, source_target_pairs={{0,4},{1,5},{2,6},{3,7},{4,0},{5,1},{6,2},{7,3},{8,12},{9,13},{10,... | collective-permute-start | bytes 1572872 | tf_op jit(solution)/shard_map/ppermute | solution.py:530
  492.9 17.7 %collective-permute-start.43 = (bf16[2,64,2048]{2,1,0:T(8,128)(2,1)}, bf16[2,64,2048]{2,1,0:T(8,128)(2,1)}, u32[]{:S(2)}, u32[]{:S(2)}) collective-permute-start(bf16[2,64,2048]{2,1,0:T(8,128)(2,1)} %slice.361), channel_id=1, source_target_pairs={{0,2},{1,3},{2,0},{3,1},{4,6},{5,7},{6,4},{7,5},{8,10},{9,11},{10,... | collective-permute-start | bytes 1572872 | tf_op jit(solution)/shard_map/ppermute | solution.py:530
  501.4 14.8 %collective-permute-start.39 = (bf16[64,2048]{1,0:T(8,128)(2,1)}, bf16[64,2048]{1,0:T(8,128)(2,1)S(1)}, u32[]{:S(2)}, u32[]{:S(2)}) collective-permute-start(bf16[64,2048]{1,0:T(8,128)(2,1)} %fusion.28), channel_id=1, source_target_pairs={{0,4},{1,5},{2,6},{3,7},{4,0},{5,1},{6,2},{7,3},{8,12},{9,13},{10,... | collective-permute-start | bytes 786440 | tf_op jit(solution)/shard_map/ppermute | solution.py:530
  501.4 30.0 %all-to-all-start.2 = ((bf16[8,64,1408]{2,1,0:T(8,128)(2,1)}), bf16[8,64,1408]{2,1,0:T(8,128)(2,1)S(1)}, u32[]{:S(2)}, u32[]{:S(2)}) async-start(bf16[8,64,1408]{2,1,0:T(8,128)(2,1)} %bitcast.223), calls=%async_computation.4 | async-start | bytes 2883584 | tf_op jit(solution)/shard_map/all_to_all | solution.py:609
  531.4 47.5 %all-to-all-start.3 = ((bf16[8,64,704]{2,1,0:T(8,128)(2,1)}), bf16[8,64,704]{2,1,0:T(8,128)(2,1)}, u32[]{:S(2)}, u32[]{:S(2)}) async-start(bf16[8,64,704]{2,1,0:T(8,128)(2,1)} %bitcast.221), calls=%async_computation.6 | async-start | bytes 1572864 | tf_op jit(solution)/shard_map/all_to_all | solution.py:609
  536.8 16.1 %collective-permute-start.46 = (bf16[64,2048]{1,0:T(8,128)(2,1)S(1)}, bf16[64,2048]{1,0:T(8,128)(2,1)S(1)}, u32[]{:S(2)}, u32[]{:S(2)}) collective-permute-start(bf16[64,2048]{1,0:T(8,128)(2,1)S(1)} %fusion.31), channel_id=1, source_target_pairs={{0,2},{1,3},{2,0},{3,1},{4,6},{5,7},{6,4},{7,5},{8,10},{9,11},{10,... | collective-permute-start | bytes 786440 | tf_op jit(solution)/shard_map/ppermute | solution.py:530
  539.8 14.2 %collective-permute-start.45 = (bf16[64,2048]{1,0:T(8,128)(2,1)S(1)}, bf16[64,2048]{1,0:T(8,128)(2,1)S(1)}, u32[]{:S(2)}, u32[]{:S(2)}) collective-permute-start(bf16[64,2048]{1,0:T(8,128)(2,1)S(1)} %fusion.30), channel_id=1, source_target_pairs={{0,4},{1,5},{2,6},{3,7},{4,0},{5,1},{6,2},{7,3},{8,12},{9,13},{10,... | collective-permute-start | bytes 786440 | tf_op jit(solution)/shard_map/ppermute | solution.py:530
  578.9 35.1 %all-to-all-start.4 = ((bf16[8,64,1152]{2,1,0:T(8,128)(2,1)}), bf16[8,64,1152]{2,1,0:T(8,128)(2,1)S(1)}, u32[]{:S(2)}, u32[]{:S(2)}) async-start(bf16[8,64,1152]{2,1,0:T(8,128)(2,1)} %bitcast.224), calls=%async_computation.7 | async-start | bytes 2359296 | tf_op jit(solution)/shard_map/all_to_all | solution.py:609
  583.6 28.4 %collective-permute-start.60 = (bf16[64,2048]{1,0:T(8,128)(2,1)}, bf16[64,2048]{1,0:T(8,128)(2,1)S(1)}, u32[]{:S(2)}, u32[]{:S(2)}) collective-permute-start(bf16[64,2048]{1,0:T(8,128)(2,1)} %get-tuple-element.130), channel_id=1, source_target_pairs={{0,24},{8,16},{16,8},{24,0},{1,25},{9,17},{17,9},{25,1},{2,26},{10... | collective-permute-start | bytes 786440 | tf_op jit(solution)/shard_map/ppermute | solution.py:530
  585.7 26.3 %collective-permute-start.59 = (bf16[64,2048]{1,0:T(8,128)(2,1)}, bf16[64,2048]{1,0:T(8,128)(2,1)}, u32[]{:S(2)}, u32[]{:S(2)}) collective-permute-start(bf16[64,2048]{1,0:T(8,128)(2,1)} %get-tuple-element.131), channel_id=1, source_target_pairs={{0,16},{8,24},{16,0},{24,8},{1,17},{9,25},{17,1},{25,9},{2,18},{10... | collective-permute-start | bytes 786440 | tf_op jit(solution)/shard_map/ppermute | solution.py:530
  588.2 23.9 %collective-permute-start.58 = (bf16[64,2048]{1,0:T(8,128)(2,1)S(1)}, bf16[64,2048]{1,0:T(8,128)(2,1)}, u32[]{:S(2)}, u32[]{:S(2)}) collective-permute-start(bf16[64,2048]{1,0:T(8,128)(2,1)S(1)} %get-tuple-element.129), channel_id=1, source_target_pairs={{0,8},{8,0},{16,24},{24,16},{1,9},{9,1},{17,25},{25,17},{2,10},{10... | collective-permute-start | bytes 786440 | tf_op jit(solution)/shard_map/ppermute | solution.py:530
  (115 other events, 1441.1 us)
Sparse Core Ops, SparseCore 0:
  48.8 91.0 all-gather.3
  142.6 105.1 all-gather.5
  249.4 61.7 all-gather.7
  314.0 54.8 reduce-scatter.3
  371.0 102.0 reduce-scatter.5
  475.3 86.0 reduce-scatter.7

commit v4 on v3

--- a/solution.py
+++ b/solution.py
@@ -563,7 +563,7 @@
         total = lax.psum_scatter(
             partial_rows.astype(low), "seq", scatter_dimension=0, tiled=True
         ).astype(f32)
-        return total if beside is None else (total, beside)
+        return total if beside is None else (total, *beside)
     terms = partial_rows.astype(low).reshape(peers, -1, partial_rows.shape[-1])
     half = terms.shape[1] // 2
     near = terms[:4].astype(f32) + swap(terms[4:], "seq", 1).astype(f32)
@@ -573,11 +573,11 @@
     top = near[0::2, :half] + top_x.astype(f32)
     bottom = near[:2, half:] + bottom_y.astype(f32)
     if beside is not None:
-        top, bottom, beside = tie(top, bottom, beside)
+        top, bottom, *beside = tie(top, bottom, *beside)
     top_y = swap(top[1].astype(low), "seq", 4)
     bottom_x = swap(bottom[1].astype(low), "seq", 2)
     total = jnp.concatenate([top[0] + top_y.astype(f32), bottom[0] + bottom_x.astype(f32)])
-    return total if beside is None else (total, beside)
+    return total if beside is None else (total, *beside)
 
 
 def sum_all(value):
@@ -644,6 +644,42 @@
         out_specs=in_vmem(),
         compiler_params=pltpu.CompilerParams(vmem_limit_bytes=30 * 1024 * 1024),
         name="assemble",
+    )(pieces)
+
+
+def order_kernel(units, pieces, whole):
+    peers, rows, _ = pieces.shape
+    wide = units + LANES // 2
+    middle = lax.broadcasted_iota(jnp.int32, (rows, LANES), 1) < LANES // 2
+    for kind in range(2):
+        for j in range(0, peers, 2):
+            if kind == 0:
+                one = pieces[j, :, :wide].astype(f32)
+                two = pltpu.roll(pieces[j + 1, :, :wide].astype(f32), LANES // 2, axis=1)
+            else:
+                start = 2 * units - wide
+                one = pltpu.roll(pieces[j, :, start:].astype(f32), wide - LANES // 2, axis=1)
+                two = pieces[j + 1, :, start:].astype(f32)
+            at = (kind * peers + j) * units
+            whole[:, at : at + wide - LANES] = one[:, : wide - LANES]
+            at = at + wide - LANES
+            whole[:, at : at + LANES] = jnp.where(middle, one[:, wide - LANES :], two[:, :LANES])
+            at = at + LANES
+            whole[:, at : at + wide - LANES] = two[:, LANES:]
+
+
+def order_units(pieces, units):
+    peers, rows, _ = pieces.shape
+    if units % LANES != LANES // 2 or peers % 2 != 0:
+        whole = pieces.reshape(peers, rows, 2, units).transpose(1, 2, 0, 3)
+        return whole.reshape(rows, 2 * units * peers).astype(f32)
+    return pl.pallas_call(
+        partial(order_kernel, units),
+        out_shape=jax.ShapeDtypeStruct((rows, 2 * units * peers), f32),
+        in_specs=[in_vmem()],
+        out_specs=in_vmem(),
+        compiler_params=pltpu.CompilerParams(vmem_limit_bytes=30 * 1024 * 1024),
+        name="order_units",
     )(pieces)
 
 
@@ -738,7 +774,6 @@
     valid = (positions < lengths[:, None]).astype(f32).reshape(-1, 1)
     inputs = tokens.reshape(-1, width).astype(f32)
 
-    out_parts = out_rows_near(out_weight)
     main = mix_weight[:, : 4 * width].reshape(own_rows, 4, peers, cols).transpose(2, 0, 1, 3)
     logits = mix_weight[:, 4 * width :].reshape(own_rows, 2, peers, local_heads)
     logits = logits.transpose(2, 0, 1, 3).reshape(peers, own_rows, logit_cols)
@@ -747,12 +782,14 @@
     )
     wide_cols = mix_rows.shape[1]
     normed, norm_back = jax.vjp(rms_scale, inputs, norm_gain)
-    gate_up = mlp_in_weight.reshape(own_rows, 2, peers, own_units).transpose(2, 0, 1, 3)
-    down = mlp_out_weight.reshape(own_rows, peers, 1, own_units).transpose(1, 0, 2, 3)
+    normed_low, out_mine = tie(normed.astype(low), out_weight)
+    out_parts = out_rows_near(out_mine)
+    mix_rows, normed_low, mlp_in_rows, mlp_out_rows, out_parts = tie(
+        mix_rows, normed_low, mlp_in_weight, mlp_out_weight, out_parts
+    )
+    gate_up = mlp_in_rows.reshape(own_rows, 2, peers, own_units).transpose(2, 0, 1, 3)
+    down = mlp_out_rows.reshape(own_rows, peers, 1, own_units).transpose(1, 0, 2, 3)
     mlp_pieces = jnp.concatenate([gate_up, down], axis=2).reshape(peers, own_rows, 3 * own_units)
-    mix_rows, normed_low, mlp_pieces, out_parts = tie(
-        mix_rows, normed.astype(low), mlp_pieces, out_parts
-    )
     mix_here = gather_dp(mix_rows)
     normed_all = gather_seq(normed_low)
     mlp_rows = to_columns(mlp_pieces)
@@ -777,7 +814,7 @@
     )
     mixed, cot_low = tie(mixed, cot_low)
     mixed_low = mixed.reshape(-1, cols)
-    branch, in_here = scatter_seq(dot32(mixed_low, out_here), in_here)
+    branch, in_here = scatter_seq(dot32(mixed_low, out_here), (in_here,))
     hidden = inputs + branch
 
     second, second_back = jax.vjp(rms_scale, hidden, mlp_gain)
@@ -801,7 +838,6 @@
     branch_all, activated_low = tie(branch_all, activated_low)
     grad_mixed = dot_t(branch_all, out_here).reshape(peers, micro, seq_rows, cols)
     grad_mixed, grad_down = tie(grad_mixed, grad_down)
-    grad_out_term = t_dot(mixed_low, branch_all).astype(low)
     grad_projected, grad_conv, rate_sums, gain_sums = (
         heads_backward(
             places,
@@ -818,9 +854,11 @@
     grad_mix_term = t_dot(normed_all, grad_projected).astype(low)
     grad_mix_term, grad_projected = tie(grad_mix_term, grad_projected)
     mix_own = sum_dp(grad_mix_term)
-    out_parts = out_rows_sent(grad_out_term)
-    grad_normed, grad_in = scatter_seq(dot_t(grad_projected, mix_here), to_owners(grad_in))
+    grad_normed, grad_in, mixed_low = scatter_seq(
+        dot_t(grad_projected, mix_here), (to_owners(grad_in), mixed_low)
+    )
     grad_down = to_owners(grad_down)
+    out_parts = out_rows_sent(t_dot(mixed_low, branch_all).astype(low))
     grad_inputs_norm, grad_norm_gain = norm_back(grad_normed)
     grad_tokens = grad_hidden + grad_inputs_norm
     feed_out = scatter_seq(dot_t(activated_low, down_here))
@@ -851,8 +889,7 @@
     )
     grad_mix = to_owners(mix_own)
     grad_out_own = out_rows_sum(out_parts)
-    grad_in = grad_in.reshape(peers, own_rows, 2, own_units).transpose(1, 2, 0, 3)
-    grad_in = grad_in.reshape(own_rows, 2 * units).astype(f32)
+    grad_in = order_units(grad_in, own_units)
     grad_down = grad_down.transpose(1, 0, 2).reshape(own_rows, units).astype(f32)
     ends = [sum(sizes[: i + 1]) for i in range(len(sizes))]
     sums = [summed[end - size : end] for end, size in zip(ends, sizes)]

time: 633 us -> 618 us (0.976)
  local copies, waits for them, and re-layouts: 104 us -> 86.6 us
    ppermute x53, waiting for transfers between devices: 125 us -> 155 us  [swap(): lax.ppermute(value, axis, [(i, i ^ bit) for i in range(lax.axis_size(axis...]
    all_gather x3, waiting for transfers between devices: 43.9 us -> 20.8 us  [gather_dp(): return lax.all_gather(rows_here, 'dp', axis=0, tiled=True)]
    convert_element_type x3 -> x0, local copies, waits for them, and re-layouts: 15.4 us -> none  [shards(): grad_in = grad_in.reshape(own_rows, 2 * units).astype(f32)]
    unnamed x195 -> x189, local copies, waits for them, and re-layouts: 25.5 us -> 24.9 us
  transfers between devices with their start and end apart: 72 -> 72, of which waited for: 42 -> 47; matrix products, arithmetic and copies ran while one was open for 36% -> 33% of each run, Pallas kernels for 9% -> 9%
where the time goes in v4:
time: 618 us; the launch traced here: 609 us
  waiting for transfers between devices  216 us (35%)
  starting transfers between devices  99.2 us (16%)
  local copies, waits for them, and re-layouts  86.6 us (14%)
  matrix products  77.5 us (13%)
  Pallas kernels  58.2 us (9%)
  other arithmetic  55.1 us (9%)
  between operations  16.1 us (3%)
    ppermute x53, waiting for transfers between devices, swap(): lax.ppermute(value, axis, [(i, i ^ bit) for i in range(lax.axis_size(axis...  155 us
    ppermute x53, starting transfers between devices, swap(): lax.ppermute(value, axis, [(i, i ^ bit) for i in range(lax.axis_size(axis...  60.9 us
    pallas_call x1, Pallas kernels, heads_backward(): pl.pallas_call(partial(backward_kernel, local_heads, perm.shape[0]), out_...  32.1 us
    dot_general x4, matrix products, dot32(): return jnp.dot(left, right, preferred_element_type=f32)  26.9 us
    dot_general x4, matrix products, t_dot(): lax.dot_general(left, right, (((0,), (0,)), ((), ())), preferred_element_...  26.7 us
    unnamed x189, local copies, waits for them, and re-layouts  24.9 us
    dot_general x4, matrix products, dot_t(): lax.dot_general(left, right, (((1,), (1,)), ((), ())), preferred_element_...  24 us
    pallas_call x1, Pallas kernels, heads_forward(): pl.pallas_call(partial(forward_kernel, local_heads, perm.shape[0]), out_s...  22.6 us
  transfers between devices with their start and end apart: 72, of which 47 were waited for; matrix products, arithmetic and copies ran while one was open for 33% of the time, Pallas kernels for 9%

profile of v4, /device:TPU:0, one launch (start us, length us, event | category | flops | bytes accessed | tf_op | source)
XLA Modules:
  0.0 609.2 jit_solution(2873292117544051875)
XLA Ops:
  12.1 5.2 all-to-all-start
  22.3 6.7 %collective-permute-done.2 = bf16[64,2048]{1,0:T(8,128)(2,1)S(1)} collective-permute-done((bf16[64,2048]{1,0:T(8,128)(2,1)S(1)}, bf16[64,2048]{1,0:T(8,128)(2,1)S(1)}, u32[]{:S(2)}, u32[]{:S(2)}) %collective-permute-start.2) | collective-permute-done | bytes 262176 | tf_op jit(solution)/shard_map/ppermute | solution.py:530
  29.0 15.5 %collective-permute-done.1 = bf16[64,2048]{1,0:T(8,128)(2,1)S(1)} collective-permute-done((bf16[64,2048]{1,0:T(8,128)(2,1)S(1)}, bf16[64,2048]{1,0:T(8,128)(2,1)S(1)}, u32[]{:S(2)}, u32[]{:S(2)}) %collective-permute-start.1) | collective-permute-done | bytes 262176 | tf_op jit(solution)/shard_map/ppermute | solution.py:530
  50.0 4.6 collective-permute-done.4
  72.1 8.9 %collective-permute-done.6 = bf16[128,2048]{1,0:T(8,128)(2,1)S(1)} collective-permute-done((bf16[128,2048]{1,0:T(8,128)(2,1)S(1)}, bf16[128,2048]{1,0:T(8,128)(2,1)S(1)}, u32[]{:S(2)}, u32[]{:S(2)}) %collective-permute-start.6) | collective-permute-done | bytes 524320 | tf_op jit(solution)/shard_map/ppermute | solution.py:530
  84.0 5.1 pad_maximum_fusion
  89.1 6.9 %reshape.293 = bf16[8,64,2112]{2,1,0:T(8,128)(2,1)} reshape(bf16[8,64,3,704]{3,2,1,0:T(4,128)(2,1)} %pad_maximum_fusion) | data formatting | bytes 4325376 | tf_op jit(solution)/shard_map/reshape | solution.py:792
  96.0 4.5 all-to-all-start.1
  107.6 21.0 %all-to-all-done.1 = bf16[8,64,2112]{2,1,0:T(8,128)(2,1)} async-done(((bf16[8,64,2112]{2,1,0:T(8,128)(2,1)}), bf16[8,64,2112]{2,1,0:T(8,128)(2,1)}, u32[]{:S(2)}, u32[]{:S(2)}) %all-to-all-start.1) | async-done | bytes 2162720 | tf_op jit(solution)/shard_map/all_to_all | solution.py:595
  128.6 7.8 %all-gather.4.cloned.1.call-done = bf16[2048,1152]{1,0:T(8,128)(2,1)} async-done(((bf16[512,1152]{1,0:T(8,128)(2,1)}), bf16[2048,1152]{1,0:T(8,128)(2,1)}) %all-gather.4.cloned.1.call-update) | async-done | bytes 4718608 | tf_op jit(solution)/shard_map/all_gather | solution.py:600
  139.8 9.8 %convolution_convert_fusion.6 = bf16[1024,1152]{1,0:T(8,128)(2,1)} fusion(bf16[1024,2048]{1,0:T(8,128)(2,1)} %constant_dynamic-update-slice_fusion.3, bf16[2048,1152]{1,0:T(8,128)(2,1)} %all-gather.4.cloned.1.call-done), kind=kOutput, calls=%fused_computation.13 | convolution fusion | flops 4833017856 | bytes 11272192 | tf_op jit(solution)/shard_map/dot_general | solution.py:735
  149.7 22.6 %heads_forward.1 = (bf16[8,2,64,256]{3,2,1,0:T(8,128)(2,1)S(1)}, bf16[8,2,64,256]{3,2,1,0:T(8,128)(2,1)S(1)}, bf16[8,2,64,768]{3,2,1,0:T(8,128)(2,1)}, f32[8,2,6...) custom-call(s32[8]{0:T(128)S(1)} %fusion.35.perm, ...), custom_call_target="tpu_custom_call" | custom-call | tf_op jit(solution)/shard_map/heads_forward/pallas_call | solution.py:463
  205.4 4.6 collective-permute-done.24
  210.8 5.0 collective-permute-done.25
  224.9 8.2 %collective-permute-done.14 = bf16[2,64,2048]{2,1,0:T(8,128)(2,1)S(1)} collective-permute-done((bf16[2,64,2048]{2,1,0:T(8,128)(2,1)S(1)}, bf16[2,64,2048]{2,1,0:T(8,128)(2,1)S(1)}, u32[]{:S(2)}, u32[]{:S(2)}) %collective-permute-start.14) | collective-permute-done | bytes 524320 | tf_op jit(solution)/shard_map/ppermute | solution.py:530
  236.3 8.0 %all-gather.6.cloned.1.call-done = bf16[2048,1408]{1,0:T(8,128)(2,1)} async-done(((bf16[512,1408]{1,0:T(8,128)(2,1)}), bf16[2048,1408]{1,0:T(8,128)(2,1)}) %all-gather.6.cloned.1.call-update) | async-done | bytes 5767184 | tf_op jit(solution)/shard_map/all_gather | solution.py:600
  273.6 9.2 %collective-permute-done.19 = bf16[128,2048]{1,0:T(8,128)(2,1)S(1)} collective-permute-done((bf16[128,2048]{1,0:T(8,128)(2,1)S(1)}, bf16[128,2048]{1,0:T(8,128)(2,1)S(1)}, u32[]{:S(2)}, u32[]{:S(2)}) %collective-permute-start.19) | collective-permute-done | bytes 524320 | tf_op jit(solution)/shard_map/ppermute | solution.py:530
  287.9 6.6 %fusion = f32[1024,1408]{1,0:T(8,128)S(1)} fusion(bf16[1024,2048]{1,0:T(8,128)(2,1)S(1)} %constant_dynamic-update-slice_fusion.10, bf16[2048,1408]{1,0:T(8,128)(2,1)S(1)} %bitcast.240), kind=kOutput, calls=%fused_computation.9 | convolution fusion | flops 5908463616 | bytes 15728640 | tf_op jit(solution)/shard_map/dot_general | solution.py:735
  298.3 4.5 convolution_convert_fusion.8
  302.8 4.9 all-gather.8.cloned.1.call-done
  308.0 9.1 %fusion.23 = (f32[1024,704]{1,0:T(8,128)S(1)}, f32[1024,704]{1,0:T(8,128)S(1)}) fusion(f32[1024,1408]{1,0:T(8,128)} %copy-done.17, bf16[1024,2048]{1,0:T(8,128)(2,1)} %copy-done.55, bf16[2048,704]{1,0:T(8,128)(2,1)} %all-gather.8.cloned.1.call-done), kind=kOutput, calls=%fused_computation.105 | convolution fusion | flops 2961440768 | bytes 18612224 | tf_op jit(solution)/shard_map/dot_general | solution.py:735
  317.2 8.8 %convolution_convert_fusion.4 = bf16[1024,2048]{1,0:T(8,128)(2,1)S(1)} fusion(bf16[2048,1408]{1,0:T(8,128)(2,1)} %all-gather.6.cloned.1.call-done, f32[1024,704]{1,0:T(8,128)S(1)} %get-tuple-element.110, f32[1024,704]{1,0:T(8,128)S(1)} %get-tuple-element.109), kind=kOutput, calls=%fused_computation.11 | convolution fusion | flops 5910560768 | bytes 15728640 | tf_op jit(solution)/shard_map/dot_general | solution.py:739
  338.5 8.9 %convolution_convert_fusion.1 = bf16[2048,1408]{1,0:T(8,128)(2,1)} fusion(bf16[1024,2048]{1,0:T(8,128)(2,1)S(1)} %copy-done.57, f32[1024,704]{1,0:T(8,128)S(1)} %get-tuple-element.110, f32[1024,704]{1,0:T(8,128)S(1)} %get-tuple-element.109), kind=kOutput, calls=%fused_computation.1 | convolution fusion | flops 5911347200 | bytes 15728640 | tf_op jit(solution)/shard_map/dot_general | solution.py:743
  355.4 5.1 collective-permute-done.31
  375.3 9.3 %collective-permute-done.34 = bf16[128,2048]{1,0:T(8,128)(2,1)S(1)} collective-permute-done((bf16[128,2048]{1,0:T(8,128)(2,1)S(1)}, bf16[128,2048]{1,0:T(8,128)(2,1)S(1)}, u32[]{:S(2)}, u32[]{:S(2)}) %collective-permute-start.34) | collective-permute-done | bytes 524320 | tf_op jit(solution)/shard_map/ppermute | solution.py:530
  392.6 32.1 %heads_backward.1 = (bf16[8,2,64,1152]{3,2,1,0:T(8,128)(2,1)}, f32[4,768]{1,0:T(4,128)S(1)}, f32[1,128]{1,0:T(1,128)S(1)}, f32[1,128]{1,0:T(1,128)S(1)}) custom-call(s32[8]{0:T(128)S(1)} %fusion.35.perm, f32[8,2,64,256]{3,2,1,0:T(8,128)S(1)} %bitcast.190, bf16[8,2,64,1152]{3,2,1,0:T(8,128)(2,1)} %bitcast.199, f32[4,768]{1,0:T(4,128)S(1)} %bitcast.192, ...), custom_call_target="tpu_custom_call" | custom-call | tf_op jit(solution)/shard_map/heads_backward/pallas_call | solution.py:499
  424.8 9.8 %convolution_convert_fusion = bf16[2048,1152]{1,0:T(8,128)(2,1)} fusion(bf16[1024,2048]{1,0:T(8,128)(2,1)} %constant_dynamic-update-slice_fusion.3, bf16[1024,1152]{1,0:T(8,128)(2,1)} %bitcast.241), kind=kOutput, calls=%fused_computation | convolution fusion | flops 4834197504 | bytes 11272192 | tf_op jit(solution)/shard_map/dot_general | solution.py:743
  434.6 5.6 convolution_convert_fusion.7
  442.8 8.3 %convolution_convert_fusion.3 = bf16[1024,2048]{1,0:T(8,128)(2,1)S(1)} fusion(bf16[1024,1152]{1,0:T(8,128)(2,1)S(1)} %bitcast.242, bf16[2048,1152]{1,0:T(8,128)(2,1)} %all-gather.4.cloned.1.call-done), kind=kOutput, calls=%fused_computation.10 | convolution fusion | flops 4833935360 | bytes 11272192 | tf_op jit(solution)/shard_map/dot_general | solution.py:739
  493.0 13.2 %all-to-all-done.2.pieces = bf16[8,64,1408]{2,1,0:T(8,128)(2,1)S(1)} async-done(((bf16[8,64,1408]{2,1,0:T(8,128)(2,1)}), bf16[8,64,1408]{2,1,0:T(8,128)(2,1)S(1)}, u32[]{:S(2)}, u32[]{:S(2)}) %all-to-all-start.2) | async-done | bytes 1441824 | tf_op jit(solution)/shard_map/all_to_all | solution.py:609
  536.9 12.8 %collective-permute-done.52 = f32[226,128]{1,0:T(8,128)S(1)} collective-permute-done((f32[226,128]{1,0:T(8,128)S(1)}, f32[226,128]{1,0:T(8,128)S(1)}, u32[]{:S(2)}, u32[]{:S(2)}) %collective-permute-start.52) | collective-permute-done | bytes 115744 | tf_op jit(solution)/shard_map/ppermute | solution.py:530
  588.5 9.9 %collective-permute-done.59 = bf16[64,2048]{1,0:T(8,128)(2,1)} collective-permute-done((bf16[64,2048]{1,0:T(8,128)(2,1)S(1)}, bf16[64,2048]{1,0:T(8,128)(2,1)}, u32[]{:S(2)}, u32[]{:S(2)}) %collective-permute-start.59) | collective-permute-done | bytes 262176 | tf_op jit(solution)/shard_map/ppermute | solution.py:530
  (457 shorter events, 290.4 us)
Async XLA Ops:
  12.1 33.4 %all-to-all-start = ((bf16[8,64,1152]{2,1,0:T(8,128)(2,1)}), bf16[8,64,1152]{2,1,0:T(8,128)(2,1)S(1)}, u32[]{:S(2)}, u32[]{:S(2)}) async-start(bf16[8,64,1152]{2,1,0:T(8,128)(2,1)} %fusion.5), calls=%async_computation | async-start | bytes 2359296 | tf_op jit(solution)/shard_map/all_to_all | solution.py:595
  17.3 119.1 %all-gather.4.cloned.1.call-start = ((), (), s32[]{:S(2)}) async-start(), calls=%async_computation.8 | async-start | bytes 5898240 | tf_op jit(solution)/shard_map/all_gather | solution.py:600
  21.5 22.9 %collective-permute-start.1 = (bf16[64,2048]{1,0:T(8,128)(2,1)S(1)}, bf16[64,2048]{1,0:T(8,128)(2,1)S(1)}, u32[]{:S(2)}, u32[]{:S(2)}) collective-permute-start(bf16[64,2048]{1,0:T(8,128)(2,1)S(1)} %copy-done.49), channel_id=1, source_target_pairs={{0,16},{8,24},{16,0},{24,8},{1,17},{9,25},{17,1},{25,9},{2,18},{10... | collective-permute-start | bytes 786440 | tf_op jit(solution)/shard_map/ppermute | solution.py:530
  21.5 22.9 %collective-permute-start = (bf16[64,2048]{1,0:T(8,128)(2,1)S(1)}, bf16[64,2048]{1,0:T(8,128)(2,1)S(1)}, u32[]{:S(2)}, u32[]{:S(2)}) collective-permute-start(bf16[64,2048]{1,0:T(8,128)(2,1)S(1)} %copy-done.49), channel_id=1, source_target_pairs={{0,8},{8,0},{16,24},{24,16},{1,9},{9,1},{17,25},{25,17},{2,10},{10... | collective-permute-start | bytes 786440 | tf_op jit(solution)/shard_map/ppermute | solution.py:530
  48.6 20.4 %collective-permute-start.3 = (bf16[64,2048]{1,0:T(8,128)(2,1)S(1)}, bf16[64,2048]{1,0:T(8,128)(2,1)S(1)}, u32[]{:S(2)}, u32[]{:S(2)}) collective-permute-start(bf16[64,2048]{1,0:T(8,128)(2,1)S(1)} %get-tuple-element.179), channel_id=1, source_target_pairs={{0,2},{1,3},{2,0},{3,1},{4,6},{5,7},{6,4},{7,5},{8,10},{9,11},{10,... | collective-permute-start | bytes 786440 | tf_op jit(solution)/shard_map/ppermute | solution.py:530
  55.4 15.9 %collective-permute-start.5 = (bf16[128,2048]{1,0:T(8,128)(2,1)}, bf16[128,2048]{1,0:T(8,128)(2,1)S(1)}, u32[]{:S(2)}, u32[]{:S(2)}) collective-permute-start(bf16[128,2048]{1,0:T(8,128)(2,1)} %pad_maximum_fusion.10), channel_id=1, source_target_pairs={{0,2},{1,3},{2,0},{3,1},{4,6},{5,7},{6,4},{7,5},{8,10},{9,11},{10,... | collective-permute-start | bytes 1572872 | tf_op jit(solution)/shard_map/ppermute | solution.py:530
  84.0 20.4 %collective-permute-start.7 = (bf16[512,2048]{1,0:T(8,128)(2,1)}, bf16[512,2048]{1,0:T(8,128)(2,1)}, u32[]{:S(2)}, u32[]{:S(2)}) collective-permute-start(bf16[512,2048]{1,0:T(8,128)(2,1)} %get-tuple-element.174), channel_id=1, source_target_pairs={{0,1},{1,0},{2,3},{3,2},{4,5},{5,4},{6,7},{7,6},{8,9},{9,8},{10,11... | collective-permute-start | bytes 6291464 | tf_op jit(solution)/shard_map/ppermute | solution.py:530
  96.0 32.6 %all-to-all-start.1 = ((bf16[8,64,2112]{2,1,0:T(8,128)(2,1)}), bf16[8,64,2112]{2,1,0:T(8,128)(2,1)}, u32[]{:S(2)}, u32[]{:S(2)}) async-start(bf16[8,64,2112]{2,1,0:T(8,128)(2,1)} %reshape.293), calls=%async_computation.1 | async-start | bytes 4456448 | tf_op jit(solution)/shard_map/all_to_all | solution.py:595
  100.5 143.8 %all-gather.6.cloned.1.call-start = ((), (), s32[]{:S(2)}) async-start(), calls=%async_computation.9 | async-start | bytes 7208960 | tf_op jit(solution)/shard_map/all_gather | solution.py:600
  139.0 168.7 %all-gather.8.cloned.1.call-start = ((), (), s32[]{:S(2)}) async-start(), calls=%async_computation.10 | async-start | bytes 3932160 | tf_op jit(solution)/shard_map/all_gather | solution.py:600
  182.2 18.6 %collective-permute-start.22 = (bf16[64,2048]{1,0:T(8,128)(2,1)}, bf16[64,2048]{1,0:T(8,128)(2,1)}, u32[]{:S(2)}, u32[]{:S(2)}) collective-permute-start(bf16[64,2048]{1,0:T(8,128)(2,1)} %get-tuple-element.173), channel_id=1, source_target_pairs={{0,2},{1,3},{2,0},{3,1},{4,6},{5,7},{6,4},{7,5},{8,10},{9,11},{10,... | collective-permute-start | bytes 786440 | tf_op jit(solution)/shard_map/ppermute | solution.py:530
  192.6 24.7 %collective-permute-start.12 = (bf16[4,128,2048]{2,1,0:T(8,128)(2,1)}, bf16[4,128,2048]{2,1,0:T(8,128)(2,1)}, u32[]{:S(2)}, u32[]{:S(2)}) collective-permute-start(bf16[4,128,2048]{2,1,0:T(8,128)(2,1)} %bitcast.33), channel_id=1, source_target_pairs={{0,1},{1,0},{2,3},{3,2},{4,5},{5,4},{6,7},{7,6},{8,9},{9,8},{10,11... | collective-permute-start | bytes 6291464 | tf_op jit(solution)/shard_map/ppermute | solution.py:530
  200.5 192.1 %reduce-scatter.4.cloned.1.call-start = ((), (), s32[]{:S(2)}) async-start(), calls=%async_computation.11 | async-start | bytes 3604480 | tf_op jit(solution)/shard_map/reduce_scatter | solution.py:604
  224.9 58.7 %collective-permute-start.26 = (bf16[512,2048]{1,0:T(8,128)(2,1)}, bf16[512,2048]{1,0:T(8,128)(2,1)}, u32[]{:S(2)}, u32[]{:S(2)}) collective-permute-start(bf16[512,2048]{1,0:T(8,128)(2,1)} %get-tuple-element.168), channel_id=1, source_target_pairs={{0,1},{1,0},{2,3},{3,2},{4,5},{5,4},{6,7},{7,6},{8,9},{9,8},{10,11... | collective-permute-start | bytes 6291464 | tf_op jit(solution)/shard_map/ppermute | solution.py:530
  307.8 170.5 %reduce-scatter.6.cloned.1.call-start = ((), (), s32[]{:S(2)}) async-start(), calls=%async_computation.12 | async-start | bytes 7208960 | tf_op jit(solution)/shard_map/reduce_scatter | solution.py:604
  347.4 217.8 %reduce-scatter.8.cloned.1.call-start = ((), (), s32[]{:S(2)}) async-start(), calls=%async_computation.13 | async-start | bytes 5898240 | tf_op jit(solution)/shard_map/reduce_scatter | solution.py:604
  466.2 20.1 %collective-permute-start.44 = (bf16[2,64,2048]{2,1,0:T(8,128)(2,1)}, bf16[2,64,2048]{2,1,0:T(8,128)(2,1)S(1)}, u32[]{:S(2)}, u32[]{:S(2)}) collective-permute-start(bf16[2,64,2048]{2,1,0:T(8,128)(2,1)} %slice.425), channel_id=1, source_target_pairs={{0,4},{1,5},{2,6},{3,7},{4,0},{5,1},{6,2},{7,3},{8,12},{9,13},{10,... | collective-permute-start | bytes 1572872 | tf_op jit(solution)/shard_map/ppermute | solution.py:530
  468.5 17.7 %collective-permute-start.43 = (bf16[2,64,2048]{2,1,0:T(8,128)(2,1)}, bf16[2,64,2048]{2,1,0:T(8,128)(2,1)S(1)}, u32[]{:S(2)}, u32[]{:S(2)}) collective-permute-start(bf16[2,64,2048]{2,1,0:T(8,128)(2,1)} %slice.361), channel_id=1, source_target_pairs={{0,2},{1,3},{2,0},{3,1},{4,6},{5,7},{6,4},{7,5},{8,10},{9,11},{10,... | collective-permute-start | bytes 1572872 | tf_op jit(solution)/shard_map/ppermute | solution.py:530
  478.2 28.0 %all-to-all-start.2 = ((bf16[8,64,1408]{2,1,0:T(8,128)(2,1)}), bf16[8,64,1408]{2,1,0:T(8,128)(2,1)S(1)}, u32[]{:S(2)}, u32[]{:S(2)}) async-start(bf16[8,64,1408]{2,1,0:T(8,128)(2,1)} %bitcast.217), calls=%async_computation.4 | async-start | bytes 2883584 | tf_op jit(solution)/shard_map/all_to_all | solution.py:609
  506.2 58.0 %all-to-all-start.3 = ((bf16[8,64,704]{2,1,0:T(8,128)(2,1)}), bf16[8,64,704]{2,1,0:T(8,128)(2,1)}, u32[]{:S(2)}, u32[]{:S(2)}) async-start(bf16[8,64,704]{2,1,0:T(8,128)(2,1)} %bitcast.215), calls=%async_computation.6 | async-start | bytes 1572864 | tf_op jit(solution)/shard_map/all_to_all | solution.py:609
  511.5 16.6 %collective-permute-start.46 = (bf16[64,2048]{1,0:T(8,128)(2,1)S(1)}, bf16[64,2048]{1,0:T(8,128)(2,1)S(1)}, u32[]{:S(2)}, u32[]{:S(2)}) collective-permute-start(bf16[64,2048]{1,0:T(8,128)(2,1)S(1)} %fusion.31), channel_id=1, source_target_pairs={{0,2},{1,3},{2,0},{3,1},{4,6},{5,7},{6,4},{7,5},{8,10},{9,11},{10,... | collective-permute-start | bytes 786440 | tf_op jit(solution)/shard_map/ppermute | solution.py:530
  513.5 15.5 %collective-permute-start.45 = (bf16[64,2048]{1,0:T(8,128)(2,1)S(1)}, bf16[64,2048]{1,0:T(8,128)(2,1)S(1)}, u32[]{:S(2)}, u32[]{:S(2)}) collective-permute-start(bf16[64,2048]{1,0:T(8,128)(2,1)S(1)} %fusion.30), channel_id=1, source_target_pairs={{0,4},{1,5},{2,6},{3,7},{4,0},{5,1},{6,2},{7,3},{8,12},{9,13},{10,... | collective-permute-start | bytes 786440 | tf_op jit(solution)/shard_map/ppermute | solution.py:530
  518.7 16.0 %collective-permute-start.50 = (bf16[64,2048]{1,0:T(8,128)(2,1)S(1)}, bf16[64,2048]{1,0:T(8,128)(2,1)S(1)}, u32[]{:S(2)}, u32[]{:S(2)}) collective-permute-start(bf16[64,2048]{1,0:T(8,128)(2,1)S(1)} %get-tuple-element.145), channel_id=1, source_target_pairs={{6,0},{0,1},{2,2},{4,3},{7,4},{1,5},{3,6},{5,7},{14,8},{8,9},{10,1... | collective-permute-start | bytes 786440 | tf_op jit(solution)/shard_map/ppermute | solution.py:719
  520.8 15.2 %collective-permute-start.49 = (bf16[64,2048]{1,0:T(8,128)(2,1)S(1)}, bf16[64,2048]{1,0:T(8,128)(2,1)S(1)}, u32[]{:S(2)}, u32[]{:S(2)}) collective-permute-start(bf16[64,2048]{1,0:T(8,128)(2,1)S(1)} %get-tuple-element.146), channel_id=1, source_target_pairs={{4,0},{6,1},{0,2},{2,3},{5,4},{7,5},{1,6},{3,7},{12,8},{14,9},{8,1... | collective-permute-start | bytes 786440 | tf_op jit(solution)/shard_map/ppermute | solution.py:719
  520.9 15.9 %collective-permute-start.48 = (bf16[64,2048]{1,0:T(8,128)(2,1)S(1)}, bf16[64,2048]{1,0:T(8,128)(2,1)S(1)}, u32[]{:S(2)}, u32[]{:S(2)}) collective-permute-start(bf16[64,2048]{1,0:T(8,128)(2,1)S(1)} %get-tuple-element.147), channel_id=1, source_target_pairs={{2,0},{4,1},{6,2},{0,3},{3,4},{5,5},{7,6},{1,7},{10,8},{12,9},{14,... | collective-permute-start | bytes 786440 | tf_op jit(solution)/shard_map/ppermute | solution.py:719
  529.6 20.1 %collective-permute-start.52 = (f32[226,128]{1,0:T(8,128)S(1)}, f32[226,128]{1,0:T(8,128)S(1)}, u32[]{:S(2)}, u32[]{:S(2)}) collective-permute-start(f32[226,128]{1,0:T(8,128)S(1)} %bitcast.234), channel_id=1, source_target_pairs={{0,16},{8,24},{16,0},{24,8},{1,17},{9,25},{17,1},{25,9},{2,18},{10... | collective-permute-start | bytes 347144 | tf_op jit(solution)/shard_map/ppermute | solution.py:530
  534.7 15.0 %collective-permute-start.53 = (f32[226,128]{1,0:T(8,128)S(1)}, f32[226,128]{1,0:T(8,128)S(1)}, u32[]{:S(2)}, u32[]{:S(2)}) collective-permute-start(f32[226,128]{1,0:T(8,128)S(1)} %bitcast.235), channel_id=1, source_target_pairs={{0,24},{8,16},{16,8},{24,0},{1,25},{9,17},{17,9},{25,1},{2,26},{10... | collective-permute-start | bytes 347144 | tf_op jit(solution)/shard_map/ppermute | solution.py:530
  536.0 16.5 %collective-permute-start.51 = (f32[226,128]{1,0:T(8,128)S(1)}, f32[226,128]{1,0:T(8,128)S(1)}, u32[]{:S(2)}, u32[]{:S(2)}) collective-permute-start(f32[226,128]{1,0:T(8,128)S(1)} %bitcast.236), channel_id=1, source_target_pairs={{0,8},{8,0},{16,24},{24,16},{1,9},{9,1},{17,25},{25,17},{2,10},{10... | collective-permute-start | bytes 347144 | tf_op jit(solution)/shard_map/ppermute | solution.py:530
  565.2 35.3 %all-to-all-start.4 = ((bf16[8,64,1152]{2,1,0:T(8,128)(2,1)}), bf16[8,64,1152]{2,1,0:T(8,128)(2,1)S(1)}, u32[]{:S(2)}, u32[]{:S(2)}) async-start(bf16[8,64,1152]{2,1,0:T(8,128)(2,1)} %bitcast.218), calls=%async_computation.7 | async-start | bytes 2359296 | tf_op jit(solution)/shard_map/all_to_all | solution.py:609
  570.8 17.8 %collective-permute-start.60 = (bf16[64,2048]{1,0:T(8,128)(2,1)}, bf16[64,2048]{1,0:T(8,128)(2,1)}, u32[]{:S(2)}, u32[]{:S(2)}) collective-permute-start(bf16[64,2048]{1,0:T(8,128)(2,1)} %get-tuple-element.138), channel_id=1, source_target_pairs={{0,24},{8,16},{16,8},{24,0},{1,25},{9,17},{17,9},{25,1},{2,26},{10... | collective-permute-start | bytes 786440 | tf_op jit(solution)/shard_map/ppermute | solution.py:530
  573.6 24.9 %collective-permute-start.59 = (bf16[64,2048]{1,0:T(8,128)(2,1)S(1)}, bf16[64,2048]{1,0:T(8,128)(2,1)}, u32[]{:S(2)}, u32[]{:S(2)}) collective-permute-start(bf16[64,2048]{1,0:T(8,128)(2,1)S(1)} %get-tuple-element.139), channel_id=1, source_target_pairs={{0,16},{8,24},{16,0},{24,8},{1,17},{9,25},{17,1},{25,9},{2,18},{10... | collective-permute-start | bytes 786440 | tf_op jit(solution)/shard_map/ppermute | solution.py:530
  576.4 22.0 %collective-permute-start.58 = (bf16[64,2048]{1,0:T(8,128)(2,1)S(1)}, bf16[64,2048]{1,0:T(8,128)(2,1)}, u32[]{:S(2)}, u32[]{:S(2)}) collective-permute-start(bf16[64,2048]{1,0:T(8,128)(2,1)S(1)} %get-tuple-element.137), channel_id=1, source_target_pairs={{0,8},{8,0},{16,24},{24,16},{1,9},{9,1},{17,25},{25,17},{2,10},{10... | collective-permute-start | bytes 786440 | tf_op jit(solution)/shard_map/ppermute | solution.py:530
  (112 other events, 1277.2 us)
Sparse Core Ops, SparseCore 0:
  46.7 89.6 all-gather.3
  139.1 105.1 all-gather.5
  245.9 61.7 all-gather.7
  310.5 54.8 reduce-scatter.3
  367.5 102.0 reduce-scatter.5
  471.8 93.4 reduce-scatter.7

commit v5 on v4

--- a/solution.py
+++ b/solution.py
@@ -683,6 +683,22 @@
     )(pieces)
 
 
+def pack_rows(blocks, logit_cols):
+    rows, cols = blocks.shape[1], blocks.shape[2] - LANES
+    below = blocks[:, :, cols : cols + logit_cols].swapaxes(1, 2)
+    below = jnp.pad(below, ((0, 0), (0, 16 - logit_cols), (0, cols - rows)))
+    return jnp.concatenate([blocks[:, :, :cols], below], axis=1).reshape(-1, cols)
+
+
+def unpack_rows(packed, count):
+    blocks = packed.reshape(count, -1, packed.shape[1])
+    rows = blocks.shape[1] - 16
+    logits = blocks[:, rows:, :rows].swapaxes(1, 2)
+    logits = jnp.pad(logits, ((0, 0), (0, 0), (0, LANES - 16)))
+    blocks = jnp.concatenate([blocks[:, :rows], logits], axis=2)
+    return blocks.reshape(-1, blocks.shape[2])
+
+
 def hop(step, back):
     groups, peers = lax.axis_size("dp"), lax.axis_size("seq")
     ratio = peers // groups
@@ -790,13 +806,14 @@
     gate_up = mlp_in_rows.reshape(own_rows, 2, peers, own_units).transpose(2, 0, 1, 3)
     down = mlp_out_rows.reshape(own_rows, peers, 1, own_units).transpose(1, 0, 2, 3)
     mlp_pieces = jnp.concatenate([gate_up, down], axis=2).reshape(peers, own_rows, 3 * own_units)
-    mix_here = gather_dp(mix_rows)
+    mix_here = gather_dp(pack_rows(mix_rows[None], logit_cols))
     normed_all = gather_seq(normed_low)
     mlp_rows = to_columns(mlp_pieces)
     cotangent = valid * grad_out.reshape(-1, width).astype(f32)
     mix_here, out_parts, mlp_rows, normed_all, cot_low = tie(
         mix_here, out_parts, mlp_rows, normed_all, cotangent.astype(low)
     )
+    mix_here = unpack_rows(mix_here, groups)
     out_here = out_rows_here(out_parts)
     in_here = gather_dp(mlp_rows[:, : 2 * own_units])
     down_here = gather_dp(mlp_rows[:, 2 * own_units :])
@@ -853,10 +870,9 @@
     grad_projected = grad_projected.reshape(-1, wide_cols)
     grad_mix_term = t_dot(normed_all, grad_projected).astype(low)
     grad_mix_term, grad_projected = tie(grad_mix_term, grad_projected)
-    mix_own = sum_dp(grad_mix_term)
-    grad_normed, grad_in, mixed_low = scatter_seq(
-        dot_t(grad_projected, mix_here), (to_owners(grad_in), mixed_low)
-    )
+    mix_own = sum_dp(pack_rows(grad_mix_term.reshape(groups, -1, wide_cols), logit_cols))
+    grad_normed, mixed_low = scatter_seq(dot_t(grad_projected, mix_here), (mixed_low,))
+    grad_in = to_owners(grad_in)
     grad_down = to_owners(grad_down)
     out_parts = out_rows_sent(t_dot(mixed_low, branch_all).astype(low))
     grad_inputs_norm, grad_norm_gain = norm_back(grad_normed)
@@ -887,7 +903,7 @@
     mix_own, out_parts, summed, grad_in, grad_down = tie(
         mix_own, out_parts, summed, grad_in, grad_down
     )
-    grad_mix = to_owners(mix_own)
+    grad_mix = to_owners(unpack_rows(mix_own, 1))
     grad_out_own = out_rows_sum(out_parts)
     grad_in = order_units(grad_in, own_units)
     grad_down = grad_down.transpose(1, 0, 2).reshape(own_rows, units).astype(f32)

time: 618 us -> 615 us (level)
  local copies, waits for them, and re-layouts: 86.6 us -> 98.7 us
  waiting for transfers between devices: 216 us -> 204 us
    ppermute x53, waiting for transfers between devices: 155 us -> 172 us  [swap(): lax.ppermute(value, axis, [(i, i ^ bit) for i in range(lax.axis_size(axis...]
    all_gather x3, waiting for transfers between devices: 20.8 us -> 6.35 us  [gather_dp(): return lax.all_gather(rows_here, 'dp', axis=0, tiled=True)]
    all_to_all x3, waiting for transfers between devices: 13.2 us -> 0.01 us  [to_owners(): lax.all_to_all(pieces, 'seq', split_axis=0, concat_axis=0, tiled=True)]
    slice x0 -> x5, local copies, waits for them, and re-layouts: none -> 12.8 us  [the longest x2 5.89 us: unpack_rows(): blocks = jnp.concatenate([blocks[:, :rows], logits], axis=2)]
    concatenate x0 -> x4, other arithmetic: none -> 10.4 us  [the longest x2 6.21 us: pack_rows(): jnp.concatenate([blocks[:, :, :cols], below], axis=1).reshape(-1, cols)]
    unnamed x189 -> x175, local copies, waits for them, and re-layouts: 24.9 us -> 25.2 us
  transfers between devices with their start and end apart: 72 -> 72, of which waited for: 47 -> 38; matrix products, arithmetic and copies ran while one was open for 33% -> 34% of each run, Pallas kernels for 9% -> 9%
where the time goes in v5:
time: 615 us; the launch traced here: 606 us
  waiting for transfers between devices  204 us (33%)
  starting transfers between devices  98.8 us (16%)
  local copies, waits for them, and re-layouts  98.7 us (16%)
  matrix products  71.4 us (12%)
  Pallas kernels  58.6 us (10%)
  other arithmetic  57.8 us (9%)
  between operations  16.4 us (3%)
    ppermute x53, waiting for transfers between devices, swap(): lax.ppermute(value, axis, [(i, i ^ bit) for i in range(lax.axis_size(axis...  172 us
    ppermute x53, starting transfers between devices, swap(): lax.ppermute(value, axis, [(i, i ^ bit) for i in range(lax.axis_size(axis...  60 us
    pallas_call x1, Pallas kernels, heads_backward(): pl.pallas_call(partial(backward_kernel, local_heads, perm.shape[0]), out_...  32.5 us
    dot_general x4, matrix products, dot32(): return jnp.dot(left, right, preferred_element_type=f32)  27.3 us
    unnamed x175, local copies, waits for them, and re-layouts  25.2 us
    dot_general x4, matrix products, t_dot(): lax.dot_general(left, right, (((0,), (0,)), ((), ())), preferred_element_...  24.4 us
    pallas_call x1, Pallas kernels, heads_forward(): pl.pallas_call(partial(forward_kernel, local_heads, perm.shape[0]), out_s...  22.7 us
    all_to_all x2, waiting for transfers between devices, to_columns(): lax.all_to_all(pieces, 'seq', split_axis=0, concat_axis=0, tiled=True)  20.9 us
  transfers between devices with their start and end apart: 72, of which 38 were waited for; matrix products, arithmetic and copies ran while one was open for 34% of the time, Pallas kernels for 9%

profile of v5, /device:TPU:0, one launch (start us, length us, event | category | flops | bytes accessed | tf_op | source)
XLA Modules:
  0.0 605.9 jit_solution(6441643333453363224)
XLA Ops:
  12.1 5.2 all-to-all-start
  22.3 6.6 %collective-permute-done.2 = bf16[64,2048]{1,0:T(8,128)(2,1)S(1)} collective-permute-done((bf16[64,2048]{1,0:T(8,128)(2,1)S(1)}, bf16[64,2048]{1,0:T(8,128)(2,1)S(1)}, u32[]{:S(2)}, u32[]{:S(2)}) %collective-permute-start.2) | collective-permute-done | bytes 262176 | tf_op jit(solution)/shard_map/ppermute | solution.py:530
  29.0 15.5 %collective-permute-done.1 = bf16[64,2048]{1,0:T(8,128)(2,1)S(1)} collective-permute-done((bf16[64,2048]{1,0:T(8,128)(2,1)S(1)}, bf16[64,2048]{1,0:T(8,128)(2,1)S(1)}, u32[]{:S(2)}, u32[]{:S(2)}) %collective-permute-start.1) | collective-permute-done | bytes 262176 | tf_op jit(solution)/shard_map/ppermute | solution.py:530
  74.7 8.9 %collective-permute-done.6 = bf16[128,2048]{1,0:T(8,128)(2,1)S(1)} collective-permute-done((bf16[128,2048]{1,0:T(8,128)(2,1)S(1)}, bf16[128,2048]{1,0:T(8,128)(2,1)S(1)}, u32[]{:S(2)}, u32[]{:S(2)}) %collective-permute-start.6) | collective-permute-done | bytes 524320 | tf_op jit(solution)/shard_map/ppermute | solution.py:530
  86.6 5.1 pad_maximum_fusion
  91.7 6.9 %reshape.309 = bf16[8,64,2112]{2,1,0:T(8,128)(2,1)} reshape(bf16[8,64,3,704]{3,2,1,0:T(4,128)(2,1)} %pad_maximum_fusion) | data formatting | bytes 4325376 | tf_op jit(solution)/shard_map/reshape | solution.py:808
  98.6 4.5 all-to-all-start.1
  110.2 20.9 %all-to-all-done.1 = bf16[8,64,2112]{2,1,0:T(8,128)(2,1)} async-done(((bf16[8,64,2112]{2,1,0:T(8,128)(2,1)}), bf16[8,64,2112]{2,1,0:T(8,128)(2,1)}, u32[]{:S(2)}, u32[]{:S(2)}) %all-to-all-start.1) | async-done | bytes 2162720 | tf_op jit(solution)/shard_map/all_to_all | solution.py:595
  135.6 4.6 slice.412
  144.5 10.2 %convolution_convert_fusion.6 = bf16[1024,1152]{1,0:T(8,128)(2,1)} fusion(bf16[1024,2048]{1,0:T(8,128)(2,1)} %constant_dynamic-update-slice_fusion.3, bf16[2048,1152]{1,0:T(8,128)(2,1)S(1)} %bitcast.223), kind=kOutput, calls=%fused_computation.19 | convolution fusion | flops 4833017856 | bytes 11272192 | tf_op jit(solution)/shard_map/dot_general | solution.py:751
  154.7 22.7 %heads_forward.1 = (bf16[8,2,64,256]{3,2,1,0:T(8,128)(2,1)S(1)}, bf16[8,2,64,256]{3,2,1,0:T(8,128)(2,1)S(1)}, bf16[8,2,64,768]{3,2,1,0:T(8,128)(2,1)}, f32[8,2,6...) custom-call(s32[8]{0:T(128)S(1)} %fusion.43.perm, ...), custom_call_target="tpu_custom_call" | custom-call | tf_op jit(solution)/shard_map/heads_forward/pallas_call | solution.py:463
  215.9 5.3 collective-permute-done.25
  230.4 8.2 %collective-permute-done.14 = bf16[2,64,2048]{2,1,0:T(8,128)(2,1)S(1)} collective-permute-done((bf16[2,64,2048]{2,1,0:T(8,128)(2,1)S(1)}, bf16[2,64,2048]{2,1,0:T(8,128)(2,1)S(1)}, u32[]{:S(2)}, u32[]{:S(2)}) %collective-permute-start.14) | collective-permute-done | bytes 524320 | tf_op jit(solution)/shard_map/ppermute | solution.py:530
  270.3 7.9 %collective-permute-done.19 = bf16[128,2048]{1,0:T(8,128)(2,1)S(1)} collective-permute-done((bf16[128,2048]{1,0:T(8,128)(2,1)S(1)}, bf16[128,2048]{1,0:T(8,128)(2,1)S(1)}, u32[]{:S(2)}, u32[]{:S(2)}) %collective-permute-start.19) | collective-permute-done | bytes 524320 | tf_op jit(solution)/shard_map/ppermute | solution.py:530
  284.0 6.6 %fusion.4 = f32[1024,1408]{1,0:T(8,128)S(1)} fusion(bf16[1024,2048]{1,0:T(8,128)(2,1)S(1)} %constant_dynamic-update-slice_fusion.10, bf16[2048,1408]{1,0:T(8,128)(2,1)S(1)} %bitcast.266), kind=kOutput, calls=%fused_computation.15 | convolution fusion | flops 5908463616 | bytes 15728640 | tf_op jit(solution)/shard_map/dot_general | solution.py:751
  294.3 4.5 convolution_convert_fusion.8
  298.9 5.0 all-gather.7.cloned.1.call-done
  303.9 9.1 %fusion.31 = (f32[1024,704]{1,0:T(8,128)S(1)}, f32[1024,704]{1,0:T(8,128)S(1)}) fusion(f32[1024,1408]{1,0:T(8,128)} %copy-done.17, bf16[1024,2048]{1,0:T(8,128)(2,1)} %copy-done.44, bf16[2048,704]{1,0:T(8,128)(2,1)} %all-gather.7.cloned.1.call-done), kind=kOutput, calls=%fused_computation.117 | convolution fusion | flops 2961440768 | bytes 18612224 | tf_op jit(solution)/shard_map/dot_general | solution.py:751
  313.1 9.0 %convolution_convert_fusion.4 = bf16[1024,2048]{1,0:T(8,128)(2,1)S(1)} fusion(bf16[2048,1408]{1,0:T(8,128)(2,1)} %all-gather.5.cloned.1.call-done, f32[1024,704]{1,0:T(8,128)S(1)} %get-tuple-element.108, f32[1024,704]{1,0:T(8,128)S(1)} %get-tuple-element.107), kind=kOutput, calls=%fused_computation.17 | convolution fusion | flops 5910560768 | bytes 15728640 | tf_op jit(solution)/shard_map/dot_general | solution.py:755
  334.7 8.9 %convolution_convert_fusion.1 = bf16[2048,1408]{1,0:T(8,128)(2,1)} fusion(bf16[1024,2048]{1,0:T(8,128)(2,1)S(1)} %copy-done.46, f32[1024,704]{1,0:T(8,128)S(1)} %get-tuple-element.108, f32[1024,704]{1,0:T(8,128)S(1)} %get-tuple-element.107), kind=kOutput, calls=%fused_computation.5 | convolution fusion | flops 5911347200 | bytes 15728640 | tf_op jit(solution)/shard_map/dot_general | solution.py:759
  351.6 5.1 collective-permute-done.31
  370.9 9.3 %collective-permute-done.34 = bf16[128,2048]{1,0:T(8,128)(2,1)S(1)} collective-permute-done((bf16[128,2048]{1,0:T(8,128)(2,1)S(1)}, bf16[128,2048]{1,0:T(8,128)(2,1)S(1)}, u32[]{:S(2)}, u32[]{:S(2)}) %collective-permute-start.34) | collective-permute-done | bytes 524320 | tf_op jit(solution)/shard_map/ppermute | solution.py:530
  388.2 32.5 %heads_backward.1 = (bf16[8,2,64,1152]{3,2,1,0:T(8,128)(2,1)}, f32[4,768]{1,0:T(4,128)S(1)}, f32[1,128]{1,0:T(1,128)S(1)}, f32[1,128]{1,0:T(1,128)S(1)}) custom-call(s32[8]{0:T(128)S(1)} %fusion.43.perm, f32[8,2,64,256]{3,2,1,0:T(8,128)S(1)} %bitcast.204, bf16[8,2,64,1152]{3,2,1,0:T(8,128)(2,1)} %bitcast.214, f32[4,768]{1,0:T(4,128)S(1)} %bitcast.206, ...), custom_call_target="tpu_custom_call" | custom-call | tf_op jit(solution)/shard_map/heads_backward/pallas_call | solution.py:499
  420.6 9.7 %convolution_convert_fusion = bf16[2048,1152]{1,0:T(8,128)(2,1)} fusion(bf16[1024,2048]{1,0:T(8,128)(2,1)} %constant_dynamic-update-slice_fusion.3, bf16[1024,1152]{1,0:T(8,128)(2,1)} %bitcast.267), kind=kOutput, calls=%fused_computation.4 | convolution fusion | flops 4834197504 | bytes 11272192 | tf_op jit(solution)/shard_map/dot_general | solution.py:759
  430.4 5.8 convolution_convert_fusion.3
  446.8 4.7 slice.464
  472.9 9.2 %collective-permute-done.44 = bf16[2,64,2048]{2,1,0:T(8,128)(2,1)S(1)} collective-permute-done((bf16[2,64,2048]{2,1,0:T(8,128)(2,1)S(1)}, bf16[2,64,2048]{2,1,0:T(8,128)(2,1)S(1)}, u32[]{:S(2)}, u32[]{:S(2)}) %collective-permute-start.44) | collective-permute-done | bytes 524320 | tf_op jit(solution)/shard_map/ppermute | solution.py:530
  485.3 8.7 %collective-permute-done.38 = bf16[2,64,2048]{2,1,0:T(8,128)(2,1)S(1)} collective-permute-done((bf16[2,64,2048]{2,1,0:T(8,128)(2,1)S(1)}, bf16[2,64,2048]{2,1,0:T(8,128)(2,1)S(1)}, u32[]{:S(2)}, u32[]{:S(2)}) %collective-permute-start.38) | collective-permute-done | bytes 524320 | tf_op jit(solution)/shard_map/ppermute | solution.py:530
  514.1 9.7 %collective-permute-done.52 = f32[226,128]{1,0:T(8,128)S(1)} collective-permute-done((f32[226,128]{1,0:T(8,128)S(1)}, f32[226,128]{1,0:T(8,128)S(1)}, u32[]{:S(2)}, u32[]{:S(2)}) %collective-permute-start.52) | collective-permute-done | bytes 115744 | tf_op jit(solution)/shard_map/ppermute | solution.py:530
  523.8 6.8 %collective-permute-done.51 = f32[226,128]{1,0:T(8,128)S(1)} collective-permute-done((f32[226,128]{1,0:T(8,128)S(1)}, f32[226,128]{1,0:T(8,128)S(1)}, u32[]{:S(2)}, u32[]{:S(2)}) %collective-permute-start.51) | collective-permute-done | bytes 115744 | tf_op jit(solution)/shard_map/ppermute | solution.py:530
  539.7 18.8 %collective-permute-done.56 = f32[226,128]{1,0:T(8,128)S(1)} collective-permute-done((f32[226,128]{1,0:T(8,128)S(1)}, f32[226,128]{1,0:T(8,128)S(1)}, u32[]{:S(2)}, u32[]{:S(2)}) %collective-permute-start.56) | collective-permute-done | bytes 115744 | tf_op jit(solution)/shard_map/ppermute | solution.py:530
  586.1 8.9 %collective-permute-done.59 = bf16[64,2048]{1,0:T(8,128)(2,1)} collective-permute-done((bf16[64,2048]{1,0:T(8,128)(2,1)S(1)}, bf16[64,2048]{1,0:T(8,128)(2,1)}, u32[]{:S(2)}, u32[]{:S(2)}) %collective-permute-start.59) | collective-permute-done | bytes 262176 | tf_op jit(solution)/shard_map/ppermute | solution.py:530
  (456 shorter events, 284.6 us)
Async XLA Ops:
  12.1 33.5 %all-to-all-start = ((bf16[8,64,1152]{2,1,0:T(8,128)(2,1)}), bf16[8,64,1152]{2,1,0:T(8,128)(2,1)S(1)}, u32[]{:S(2)}, u32[]{:S(2)}) async-start(bf16[8,64,1152]{2,1,0:T(8,128)(2,1)} %fusion.12), calls=%async_computation | async-start | bytes 2359296 | tf_op jit(solution)/shard_map/all_to_all | solution.py:595
  17.3 115.2 %all-gather.9.cloned.1.call-start = ((), (), s32[]{:S(2)}) async-start(), calls=%async_computation.13 | async-start | bytes 5406720 | tf_op jit(solution)/shard_map/all_gather | solution.py:600
  21.5 22.9 %collective-permute-start.1 = (bf16[64,2048]{1,0:T(8,128)(2,1)S(1)}, bf16[64,2048]{1,0:T(8,128)(2,1)S(1)}, u32[]{:S(2)}, u32[]{:S(2)}) collective-permute-start(bf16[64,2048]{1,0:T(8,128)(2,1)S(1)} %copy-done.39), channel_id=1, source_target_pairs={{0,16},{8,24},{16,0},{24,8},{1,17},{9,25},{17,1},{25,9},{2,18},{10... | collective-permute-start | bytes 786440 | tf_op jit(solution)/shard_map/ppermute | solution.py:530
  21.5 22.9 %collective-permute-start = (bf16[64,2048]{1,0:T(8,128)(2,1)S(1)}, bf16[64,2048]{1,0:T(8,128)(2,1)S(1)}, u32[]{:S(2)}, u32[]{:S(2)}) collective-permute-start(bf16[64,2048]{1,0:T(8,128)(2,1)S(1)} %copy-done.39), channel_id=1, source_target_pairs={{0,8},{8,0},{16,24},{24,16},{1,9},{9,1},{17,25},{25,17},{2,10},{10... | collective-permute-start | bytes 786440 | tf_op jit(solution)/shard_map/ppermute | solution.py:530
  51.6 19.9 %collective-permute-start.3 = (bf16[64,2048]{1,0:T(8,128)(2,1)S(1)}, bf16[64,2048]{1,0:T(8,128)(2,1)S(1)}, u32[]{:S(2)}, u32[]{:S(2)}) collective-permute-start(bf16[64,2048]{1,0:T(8,128)(2,1)S(1)} %get-tuple-element.177), channel_id=1, source_target_pairs={{0,2},{1,3},{2,0},{3,1},{4,6},{5,7},{6,4},{7,5},{8,10},{9,11},{10,... | collective-permute-start | bytes 786440 | tf_op jit(solution)/shard_map/ppermute | solution.py:530
  86.6 20.4 %collective-permute-start.7 = (bf16[512,2048]{1,0:T(8,128)(2,1)}, bf16[512,2048]{1,0:T(8,128)(2,1)}, u32[]{:S(2)}, u32[]{:S(2)}) collective-permute-start(bf16[512,2048]{1,0:T(8,128)(2,1)} %get-tuple-element.172), channel_id=1, source_target_pairs={{0,1},{1,0},{2,3},{3,2},{4,5},{5,4},{6,7},{7,6},{8,9},{9,8},{10,11... | collective-permute-start | bytes 6291464 | tf_op jit(solution)/shard_map/ppermute | solution.py:530
  98.6 32.6 %all-to-all-start.1 = ((bf16[8,64,2112]{2,1,0:T(8,128)(2,1)}), bf16[8,64,2112]{2,1,0:T(8,128)(2,1)}, u32[]{:S(2)}, u32[]{:S(2)}) async-start(bf16[8,64,2112]{2,1,0:T(8,128)(2,1)} %reshape.309), calls=%async_computation.1 | async-start | bytes 4456448 | tf_op jit(solution)/shard_map/all_to_all | solution.py:595
  103.1 138.8 %all-gather.5.cloned.1.call-start = ((), (), s32[]{:S(2)}) async-start(), calls=%async_computation.8 | async-start | bytes 7208960 | tf_op jit(solution)/shard_map/all_gather | solution.py:600
  135.1 168.8 %all-gather.7.cloned.1.call-start = ((), (), s32[]{:S(2)}) async-start(), calls=%async_computation.9 | async-start | bytes 3932160 | tf_op jit(solution)/shard_map/all_gather | solution.py:600
  187.4 18.8 %collective-permute-start.22 = (bf16[64,2048]{1,0:T(8,128)(2,1)}, bf16[64,2048]{1,0:T(8,128)(2,1)}, u32[]{:S(2)}, u32[]{:S(2)}) collective-permute-start(bf16[64,2048]{1,0:T(8,128)(2,1)} %get-tuple-element.171), channel_id=1, source_target_pairs={{0,2},{1,3},{2,0},{3,1},{4,6},{5,7},{6,4},{7,5},{8,10},{9,11},{10,... | collective-permute-start | bytes 786440 | tf_op jit(solution)/shard_map/ppermute | solution.py:530
  197.8 25.0 %collective-permute-start.12 = (bf16[4,128,2048]{2,1,0:T(8,128)(2,1)}, bf16[4,128,2048]{2,1,0:T(8,128)(2,1)}, u32[]{:S(2)}, u32[]{:S(2)}) collective-permute-start(bf16[4,128,2048]{2,1,0:T(8,128)(2,1)} %bitcast.39), channel_id=1, source_target_pairs={{0,1},{1,0},{2,3},{3,2},{4,5},{5,4},{6,7},{7,6},{8,9},{9,8},{10,11... | collective-permute-start | bytes 6291464 | tf_op jit(solution)/shard_map/ppermute | solution.py:530
  205.7 182.5 %reduce-scatter.4.cloned.1.call-start = ((), (), s32[]{:S(2)}) async-start(), calls=%async_computation.10 | async-start | bytes 3604480 | tf_op jit(solution)/shard_map/reduce_scatter | solution.py:604
  230.4 49.3 %collective-permute-start.26 = (bf16[512,2048]{1,0:T(8,128)(2,1)}, bf16[512,2048]{1,0:T(8,128)(2,1)}, u32[]{:S(2)}, u32[]{:S(2)}) collective-permute-start(bf16[512,2048]{1,0:T(8,128)(2,1)} %get-tuple-element.166), channel_id=1, source_target_pairs={{0,1},{1,0},{2,3},{3,2},{4,5},{5,4},{6,7},{7,6},{8,9},{9,8},{10,11... | collective-permute-start | bytes 6291464 | tf_op jit(solution)/shard_map/ppermute | solution.py:530
  303.9 227.3 %reduce-scatter.8.cloned.1.call-start = ((), (), s32[]{:S(2)}) async-start(), calls=%async_computation.12 | async-start | bytes 7208960 | tf_op jit(solution)/shard_map/reduce_scatter | solution.py:604
  439.0 23.7 %collective-permute-start.42 = (bf16[4,128,2048]{2,1,0:T(8,128)(2,1)}, bf16[4,128,2048]{2,1,0:T(8,128)(2,1)}, u32[]{:S(2)}, u32[]{:S(2)}) collective-permute-start(bf16[4,128,2048]{2,1,0:T(8,128)(2,1)} %bitcast.62), channel_id=1, source_target_pairs={{0,1},{1,0},{2,3},{3,2},{4,5},{5,4},{6,7},{7,6},{8,9},{9,8},{10,11... | collective-permute-start | bytes 6291464 | tf_op jit(solution)/shard_map/ppermute | solution.py:530
  445.6 23.9 %collective-permute-start.37 = (bf16[4,128,2048]{2,1,0:T(8,128)(2,1)}, bf16[4,128,2048]{2,1,0:T(8,128)(2,1)}, u32[]{:S(2)}, u32[]{:S(2)}) collective-permute-start(bf16[4,128,2048]{2,1,0:T(8,128)(2,1)} %bitcast.53), channel_id=1, source_target_pairs={{0,1},{1,0},{2,3},{3,2},{4,5},{5,4},{6,7},{7,6},{8,9},{9,8},{10,11... | collective-permute-start | bytes 6291464 | tf_op jit(solution)/shard_map/ppermute | solution.py:530
  454.1 77.1 %all-to-all-start.3 = ((bf16[8,64,704]{2,1,0:T(8,128)(2,1)}), bf16[8,64,704]{2,1,0:T(8,128)(2,1)}, u32[]{:S(2)}, u32[]{:S(2)}) async-start(bf16[8,64,704]{2,1,0:T(8,128)(2,1)} %bitcast.86), calls=%async_computation.6 | async-start | bytes 1572864 | tf_op jit(solution)/shard_map/all_to_all | solution.py:609
  458.3 100.3 %reduce-scatter.6.cloned.1.call-start = ((), (), s32[]{:S(2)}) async-start(), calls=%async_computation.11 | async-start | bytes 5406720 | tf_op jit(solution)/shard_map/reduce_scatter | solution.py:604
  472.2 21.9 %collective-permute-start.38 = (bf16[2,64,2048]{2,1,0:T(8,128)(2,1)S(1)}, bf16[2,64,2048]{2,1,0:T(8,128)(2,1)S(1)}, u32[]{:S(2)}, u32[]{:S(2)}) collective-permute-start(bf16[2,64,2048]{2,1,0:T(8,128)(2,1)S(1)} %slice.377), channel_id=1, source_target_pairs={{0,2},{1,3},{2,0},{3,1},{4,6},{5,7},{6,4},{7,5},{8,10},{9,11},{10,... | collective-permute-start | bytes 1572872 | tf_op jit(solution)/shard_map/ppermute | solution.py:530
  472.8 21.3 %collective-permute-start.40 = (bf16[2,64,2048]{2,1,0:T(8,128)(2,1)S(1)}, bf16[2,64,2048]{2,1,0:T(8,128)(2,1)S(1)}, u32[]{:S(2)}, u32[]{:S(2)}) collective-permute-start(bf16[2,64,2048]{2,1,0:T(8,128)(2,1)S(1)} %slice.454), channel_id=1, source_target_pairs={{0,4},{1,5},{2,6},{3,7},{4,0},{5,1},{6,2},{7,3},{8,12},{9,13},{10,... | collective-permute-start | bytes 1572872 | tf_op jit(solution)/shard_map/ppermute | solution.py:530
  483.1 16.9 %collective-permute-start.46 = (bf16[64,2048]{1,0:T(8,128)(2,1)S(1)}, bf16[64,2048]{1,0:T(8,128)(2,1)S(1)}, u32[]{:S(2)}, u32[]{:S(2)}) collective-permute-start(bf16[64,2048]{1,0:T(8,128)(2,1)S(1)} %fusion.39), channel_id=1, source_target_pairs={{0,2},{1,3},{2,0},{3,1},{4,6},{5,7},{6,4},{7,5},{8,10},{9,11},{10,... | collective-permute-start | bytes 786440 | tf_op jit(solution)/shard_map/ppermute | solution.py:530
  484.7 16.5 %collective-permute-start.45 = (bf16[64,2048]{1,0:T(8,128)(2,1)S(1)}, bf16[64,2048]{1,0:T(8,128)(2,1)S(1)}, u32[]{:S(2)}, u32[]{:S(2)}) collective-permute-start(bf16[64,2048]{1,0:T(8,128)(2,1)S(1)} %fusion.38), channel_id=1, source_target_pairs={{0,4},{1,5},{2,6},{3,7},{4,0},{5,1},{6,2},{7,3},{8,12},{9,13},{10,... | collective-permute-start | bytes 786440 | tf_op jit(solution)/shard_map/ppermute | solution.py:530
  506.7 17.1 %collective-permute-start.52 = (f32[226,128]{1,0:T(8,128)S(1)}, f32[226,128]{1,0:T(8,128)S(1)}, u32[]{:S(2)}, u32[]{:S(2)}) collective-permute-start(f32[226,128]{1,0:T(8,128)S(1)} %bitcast.259), channel_id=1, source_target_pairs={{0,16},{8,24},{16,0},{24,8},{1,17},{9,25},{17,1},{25,9},{2,18},{10... | collective-permute-start | bytes 347144 | tf_op jit(solution)/shard_map/ppermute | solution.py:530
  512.2 18.4 %collective-permute-start.51 = (f32[226,128]{1,0:T(8,128)S(1)}, f32[226,128]{1,0:T(8,128)S(1)}, u32[]{:S(2)}, u32[]{:S(2)}) collective-permute-start(f32[226,128]{1,0:T(8,128)S(1)} %bitcast.261), channel_id=1, source_target_pairs={{0,8},{8,0},{16,24},{24,16},{1,9},{9,1},{17,25},{25,17},{2,10},{10... | collective-permute-start | bytes 347144 | tf_op jit(solution)/shard_map/ppermute | solution.py:530
  531.2 27.4 %all-to-all-start.2 = ((bf16[8,64,1408]{2,1,0:T(8,128)(2,1)}), bf16[8,64,1408]{2,1,0:T(8,128)(2,1)S(1)}, u32[]{:S(2)}, u32[]{:S(2)}) async-start(bf16[8,64,1408]{2,1,0:T(8,128)(2,1)} %bitcast.241), calls=%async_computation.5 | async-start | bytes 2883584 | tf_op jit(solution)/shard_map/all_to_all | solution.py:609
  535.0 23.5 %collective-permute-start.56 = (f32[226,128]{1,0:T(8,128)S(1)}, f32[226,128]{1,0:T(8,128)S(1)}, u32[]{:S(2)}, u32[]{:S(2)}) collective-permute-start(f32[226,128]{1,0:T(8,128)S(1)} %add.370), channel_id=1, source_target_pairs={{0,4},{1,5},{2,6},{3,7},{4,0},{5,1},{6,2},{7,3},{8,12},{9,13},{10,... | collective-permute-start | bytes 347144 | tf_op jit(solution)/shard_map/ppermute | solution.py:530
  537.0 21.5 %collective-permute-start.57 = (f32[226,128]{1,0:T(8,128)S(1)}, f32[226,128]{1,0:T(8,128)S(1)}, u32[]{:S(2)}, u32[]{:S(2)}) collective-permute-start(f32[226,128]{1,0:T(8,128)S(1)} %add.370), channel_id=1, source_target_pairs={{0,6},{1,7},{2,4},{3,5},{4,2},{5,3},{6,0},{7,1},{8,14},{9,15},{10,... | collective-permute-start | bytes 347144 | tf_op jit(solution)/shard_map/ppermute | solution.py:530
  538.4 20.2 %collective-permute-start.55 = (f32[226,128]{1,0:T(8,128)S(1)}, f32[226,128]{1,0:T(8,128)S(1)}, u32[]{:S(2)}, u32[]{:S(2)}) collective-permute-start(f32[226,128]{1,0:T(8,128)S(1)} %add.370), channel_id=1, source_target_pairs={{0,2},{1,3},{2,0},{3,1},{4,6},{5,7},{6,4},{7,5},{8,10},{9,11},{10,... | collective-permute-start | bytes 347144 | tf_op jit(solution)/shard_map/ppermute | solution.py:530
  561.9 35.2 %all-to-all-start.4 = ((bf16[8,64,1152]{2,1,0:T(8,128)(2,1)}), bf16[8,64,1152]{2,1,0:T(8,128)(2,1)S(1)}, u32[]{:S(2)}, u32[]{:S(2)}) async-start(bf16[8,64,1152]{2,1,0:T(8,128)(2,1)} %bitcast.229), calls=%async_computation.7 | async-start | bytes 2359296 | tf_op jit(solution)/shard_map/all_to_all | solution.py:609
  567.4 18.7 %collective-permute-start.60 = (bf16[64,2048]{1,0:T(8,128)(2,1)}, bf16[64,2048]{1,0:T(8,128)(2,1)}, u32[]{:S(2)}, u32[]{:S(2)}) collective-permute-start(bf16[64,2048]{1,0:T(8,128)(2,1)} %get-tuple-element.136), channel_id=1, source_target_pairs={{0,24},{8,16},{16,8},{24,0},{1,25},{9,17},{17,9},{25,1},{2,26},{10... | collective-permute-start | bytes 786440 | tf_op jit(solution)/shard_map/ppermute | solution.py:530
  570.0 24.9 %collective-permute-start.59 = (bf16[64,2048]{1,0:T(8,128)(2,1)S(1)}, bf16[64,2048]{1,0:T(8,128)(2,1)}, u32[]{:S(2)}, u32[]{:S(2)}) collective-permute-start(bf16[64,2048]{1,0:T(8,128)(2,1)S(1)} %get-tuple-element.137), channel_id=1, source_target_pairs={{0,16},{8,24},{16,0},{24,8},{1,17},{9,25},{17,1},{25,9},{2,18},{10... | collective-permute-start | bytes 786440 | tf_op jit(solution)/shard_map/ppermute | solution.py:530
  574.5 20.4 %collective-permute-start.58 = (bf16[64,2048]{1,0:T(8,128)(2,1)S(1)}, bf16[64,2048]{1,0:T(8,128)(2,1)}, u32[]{:S(2)}, u32[]{:S(2)}) collective-permute-start(bf16[64,2048]{1,0:T(8,128)(2,1)S(1)} %get-tuple-element.135), channel_id=1, source_target_pairs={{0,8},{8,0},{16,24},{24,16},{1,9},{9,1},{17,25},{25,17},{2,10},{10... | collective-permute-start | bytes 786440 | tf_op jit(solution)/shard_map/ppermute | solution.py:530
  (103 other events, 1194.5 us)
Sparse Core Ops, SparseCore 0:
  49.3 83.1 all-gather.8
  135.2 105.2 all-gather.4
  242.0 61.7 all-gather.6
  306.6 54.8 reduce-scatter.3
  363.6 102.0 reduce-scatter.7
  467.9 87.0 reduce-scatter.5

commit v6 on v5

--- a/solution.py
+++ b/solution.py
@@ -800,14 +800,15 @@
     normed, norm_back = jax.vjp(rms_scale, inputs, norm_gain)
     normed_low, out_mine = tie(normed.astype(low), out_weight)
     out_parts = out_rows_near(out_mine)
-    mix_rows, normed_low, mlp_in_rows, mlp_out_rows, out_parts = tie(
-        mix_rows, normed_low, mlp_in_weight, mlp_out_weight, out_parts
+    mix_rows, normed_low, mlp_in_rows, mlp_out_rows = tie(
+        mix_rows, normed_low, mlp_in_weight, mlp_out_weight
     )
     gate_up = mlp_in_rows.reshape(own_rows, 2, peers, own_units).transpose(2, 0, 1, 3)
     down = mlp_out_rows.reshape(own_rows, peers, 1, own_units).transpose(1, 0, 2, 3)
     mlp_pieces = jnp.concatenate([gate_up, down], axis=2).reshape(peers, own_rows, 3 * own_units)
     mix_here = gather_dp(pack_rows(mix_rows[None], logit_cols))
     normed_all = gather_seq(normed_low)
+    mlp_pieces, out_parts = tie(mlp_pieces, out_parts)
     mlp_rows = to_columns(mlp_pieces)
     cotangent = valid * grad_out.reshape(-1, width).astype(f32)
     mix_here, out_parts, mlp_rows, normed_all, cot_low = tie(

time: 615 us -> 605 us (0.984)
  waiting for transfers between devices: 204 us -> 196 us
    ppermute x53, waiting for transfers between devices: 172 us -> 154 us  [swap(): lax.ppermute(value, axis, [(i, i ^ bit) for i in range(lax.axis_size(axis...]
    all_to_all x2, waiting for transfers between devices: 20.9 us -> 32.7 us  [to_columns(): lax.all_to_all(pieces, 'seq', split_axis=0, concat_axis=0, tiled=True)]
  transfers between devices with their start and end apart: 72 -> 72, of which waited for: 38 -> 37; matrix products, arithmetic and copies ran while one was open for 34% -> 35% of each run, Pallas kernels for 9% -> 10%
where the time goes in v6:
time: 605 us; the launch traced here: 596 us
  waiting for transfers between devices  196 us (32%)
  local copies, waits for them, and re-layouts  98.2 us (16%)
  starting transfers between devices  96.5 us (16%)
  matrix products  71.4 us (12%)
  other arithmetic  58.8 us (10%)
  Pallas kernels  58.6 us (10%)
  between operations  16.4 us (3%)
    ppermute x53, waiting for transfers between devices, swap(): lax.ppermute(value, axis, [(i, i ^ bit) for i in range(lax.axis_size(axis...  154 us
    ppermute x53, starting transfers between devices, swap(): lax.ppermute(value, axis, [(i, i ^ bit) for i in range(lax.axis_size(axis...  59.5 us
    all_to_all x2, waiting for transfers between devices, to_columns(): lax.all_to_all(pieces, 'seq', split_axis=0, concat_axis=0, tiled=True)  32.7 us
    pallas_call x1, Pallas kernels, heads_backward(): pl.pallas_call(partial(backward_kernel, local_heads, perm.shape[0]), out_...  32.5 us
    dot_general x4, matrix products, dot32(): return jnp.dot(left, right, preferred_element_type=f32)  27.2 us
    unnamed x175, local copies, waits for them, and re-layouts  24.7 us
    dot_general x4, matrix products, t_dot(): lax.dot_general(left, right, (((0,), (0,)), ((), ())), preferred_element_...  24.4 us
    pallas_call x1, Pallas kernels, heads_forward(): pl.pallas_call(partial(forward_kernel, local_heads, perm.shape[0]), out_s...  22.7 us
  transfers between devices with their start and end apart: 72, of which 37 were waited for; matrix products, arithmetic and copies ran while one was open for 35% of the time, Pallas kernels for 10%

profile of v6, /device:TPU:0, one launch (start us, length us, event | category | flops | bytes accessed | tf_op | source)
XLA Modules:
  0.0 595.5 jit_solution(13820793467024844811)
XLA Ops:
  12.1 5.2 all-to-all-start
  22.3 11.8 %all-to-all-done = bf16[8,64,1152]{2,1,0:T(8,128)(2,1)S(1)} async-done(((bf16[8,64,1152]{2,1,0:T(8,128)(2,1)}), bf16[8,64,1152]{2,1,0:T(8,128)(2,1)S(1)}, u32[]{:S(2)}, u32[]{:S(2)}) %all-to-all-start) | async-done | bytes 1179680 | tf_op jit(solution)/shard_map/all_to_all | solution.py:595
  38.5 6.0 %collective-permute-done.1 = bf16[64,2048]{1,0:T(8,128)(2,1)} collective-permute-done((bf16[64,2048]{1,0:T(8,128)(2,1)S(1)}, bf16[64,2048]{1,0:T(8,128)(2,1)}, u32[]{:S(2)}, u32[]{:S(2)}) %collective-permute-start.1) | collective-permute-done | bytes 262176 | tf_op jit(solution)/shard_map/ppermute | solution.py:530
  66.6 8.3 %collective-permute-done.6 = bf16[128,2048]{1,0:T(8,128)(2,1)S(1)} collective-permute-done((bf16[128,2048]{1,0:T(8,128)(2,1)S(1)}, bf16[128,2048]{1,0:T(8,128)(2,1)S(1)}, u32[]{:S(2)}, u32[]{:S(2)}) %collective-permute-start.6) | collective-permute-done | bytes 524320 | tf_op jit(solution)/shard_map/ppermute | solution.py:530
  77.9 5.1 pad_maximum_fusion
  83.0 6.9 %reshape.309 = bf16[8,64,2112]{2,1,0:T(8,128)(2,1)} reshape(bf16[8,64,3,704]{3,2,1,0:T(4,128)(2,1)} %pad_maximum_fusion) | data formatting | bytes 4325376 | tf_op jit(solution)/shard_map/reshape | solution.py:808
  89.9 4.5 all-to-all-start.1
  101.5 20.9 %all-to-all-done.1 = bf16[8,64,2112]{2,1,0:T(8,128)(2,1)} async-done(((bf16[8,64,2112]{2,1,0:T(8,128)(2,1)}), bf16[8,64,2112]{2,1,0:T(8,128)(2,1)}, u32[]{:S(2)}, u32[]{:S(2)}) %all-to-all-start.1) | async-done | bytes 2162720 | tf_op jit(solution)/shard_map/all_to_all | solution.py:595
  125.6 4.7 slice.412
  134.5 10.2 %convolution_convert_fusion.6 = bf16[1024,1152]{1,0:T(8,128)(2,1)} fusion(bf16[1024,2048]{1,0:T(8,128)(2,1)} %constant_dynamic-update-slice_fusion.3, bf16[2048,1152]{1,0:T(8,128)(2,1)S(1)} %bitcast.223), kind=kOutput, calls=%fused_computation.19 | convolution fusion | flops 4833017856 | bytes 11272192 | tf_op jit(solution)/shard_map/dot_general | solution.py:751
  144.7 22.7 %heads_forward.1 = (bf16[8,2,64,256]{3,2,1,0:T(8,128)(2,1)S(1)}, bf16[8,2,64,256]{3,2,1,0:T(8,128)(2,1)S(1)}, bf16[8,2,64,768]{3,2,1,0:T(8,128)(2,1)}, f32[8,2,6...) custom-call(s32[8]{0:T(128)S(1)} %fusion.43.perm, ...), custom_call_target="tpu_custom_call" | custom-call | tf_op jit(solution)/shard_map/heads_forward/pallas_call | solution.py:463
  204.3 5.6 collective-permute-done.25
  219.0 8.7 %collective-permute-done.14 = bf16[2,64,2048]{2,1,0:T(8,128)(2,1)S(1)} collective-permute-done((bf16[2,64,2048]{2,1,0:T(8,128)(2,1)S(1)}, bf16[2,64,2048]{2,1,0:T(8,128)(2,1)S(1)}, u32[]{:S(2)}, u32[]{:S(2)}) %collective-permute-start.14) | collective-permute-done | bytes 524320 | tf_op jit(solution)/shard_map/ppermute | solution.py:530
  260.1 8.6 %collective-permute-done.19 = bf16[128,2048]{1,0:T(8,128)(2,1)S(1)} collective-permute-done((bf16[128,2048]{1,0:T(8,128)(2,1)S(1)}, bf16[128,2048]{1,0:T(8,128)(2,1)S(1)}, u32[]{:S(2)}, u32[]{:S(2)}) %collective-permute-start.19) | collective-permute-done | bytes 524320 | tf_op jit(solution)/shard_map/ppermute | solution.py:530
  273.7 6.6 %fusion.4 = f32[1024,1408]{1,0:T(8,128)S(1)} fusion(bf16[1024,2048]{1,0:T(8,128)(2,1)S(1)} %constant_dynamic-update-slice_fusion.10, bf16[2048,1408]{1,0:T(8,128)(2,1)S(1)} %bitcast.264), kind=kOutput, calls=%fused_computation.15 | convolution fusion | flops 5908463616 | bytes 15728640 | tf_op jit(solution)/shard_map/dot_general | solution.py:751
  284.1 4.5 convolution_convert_fusion.8
  288.6 5.0 all-gather.7.cloned.1.call-done
  293.7 9.1 %fusion.31 = (f32[1024,704]{1,0:T(8,128)S(1)}, f32[1024,704]{1,0:T(8,128)S(1)}) fusion(f32[1024,1408]{1,0:T(8,128)} %copy-done.17, bf16[1024,2048]{1,0:T(8,128)(2,1)} %copy-done.44, bf16[2048,704]{1,0:T(8,128)(2,1)} %all-gather.7.cloned.1.call-done), kind=kOutput, calls=%fused_computation.117 | convolution fusion | flops 2961440768 | bytes 18612224 | tf_op jit(solution)/shard_map/dot_general | solution.py:751
  302.8 9.0 %convolution_convert_fusion.4 = bf16[1024,2048]{1,0:T(8,128)(2,1)S(1)} fusion(bf16[2048,1408]{1,0:T(8,128)(2,1)} %all-gather.5.cloned.1.call-done, f32[1024,704]{1,0:T(8,128)S(1)} %get-tuple-element.110, f32[1024,704]{1,0:T(8,128)S(1)} %get-tuple-element.109), kind=kOutput, calls=%fused_computation.17 | convolution fusion | flops 5910560768 | bytes 15728640 | tf_op jit(solution)/shard_map/dot_general | solution.py:755
  324.4 8.9 %convolution_convert_fusion.1 = bf16[2048,1408]{1,0:T(8,128)(2,1)} fusion(bf16[1024,2048]{1,0:T(8,128)(2,1)S(1)} %copy-done.46, f32[1024,704]{1,0:T(8,128)S(1)} %get-tuple-element.110, f32[1024,704]{1,0:T(8,128)S(1)} %get-tuple-element.109), kind=kOutput, calls=%fused_computation.5 | convolution fusion | flops 5911347200 | bytes 15728640 | tf_op jit(solution)/shard_map/dot_general | solution.py:759
  341.2 5.1 collective-permute-done.31
  360.6 9.3 %collective-permute-done.34 = bf16[128,2048]{1,0:T(8,128)(2,1)S(1)} collective-permute-done((bf16[128,2048]{1,0:T(8,128)(2,1)S(1)}, bf16[128,2048]{1,0:T(8,128)(2,1)S(1)}, u32[]{:S(2)}, u32[]{:S(2)}) %collective-permute-start.34) | collective-permute-done | bytes 524320 | tf_op jit(solution)/shard_map/ppermute | solution.py:530
  377.8 32.5 %heads_backward.1 = (bf16[8,2,64,1152]{3,2,1,0:T(8,128)(2,1)}, f32[4,768]{1,0:T(4,128)S(1)}, f32[1,128]{1,0:T(1,128)S(1)}, f32[1,128]{1,0:T(1,128)S(1)}) custom-call(s32[8]{0:T(128)S(1)} %fusion.43.perm, f32[8,2,64,256]{3,2,1,0:T(8,128)S(1)} %bitcast.204, bf16[8,2,64,1152]{3,2,1,0:T(8,128)(2,1)} %bitcast.214, f32[4,768]{1,0:T(4,128)S(1)} %bitcast.206, ...), custom_call_target="tpu_custom_call" | custom-call | tf_op jit(solution)/shard_map/heads_backward/pallas_call | solution.py:499
  410.3 9.7 %convolution_convert_fusion = bf16[2048,1152]{1,0:T(8,128)(2,1)} fusion(bf16[1024,2048]{1,0:T(8,128)(2,1)} %constant_dynamic-update-slice_fusion.3, bf16[1024,1152]{1,0:T(8,128)(2,1)} %bitcast.265), kind=kOutput, calls=%fused_computation.4 | convolution fusion | flops 4834197504 | bytes 11272192 | tf_op jit(solution)/shard_map/dot_general | solution.py:759
  420.1 5.8 convolution_convert_fusion.3
  436.4 4.6 slice.464
  462.5 9.2 %collective-permute-done.44 = bf16[2,64,2048]{2,1,0:T(8,128)(2,1)S(1)} collective-permute-done((bf16[2,64,2048]{2,1,0:T(8,128)(2,1)S(1)}, bf16[2,64,2048]{2,1,0:T(8,128)(2,1)S(1)}, u32[]{:S(2)}, u32[]{:S(2)}) %collective-permute-start.44) | collective-permute-done | bytes 524320 | tf_op jit(solution)/shard_map/ppermute | solution.py:530
  474.8 8.7 %collective-permute-done.38 = bf16[2,64,2048]{2,1,0:T(8,128)(2,1)S(1)} collective-permute-done((bf16[2,64,2048]{2,1,0:T(8,128)(2,1)S(1)}, bf16[2,64,2048]{2,1,0:T(8,128)(2,1)S(1)}, u32[]{:S(2)}, u32[]{:S(2)}) %collective-permute-start.38) | collective-permute-done | bytes 524320 | tf_op jit(solution)/shard_map/ppermute | solution.py:530
  503.6 9.7 %collective-permute-done.52 = f32[226,128]{1,0:T(8,128)S(1)} collective-permute-done((f32[226,128]{1,0:T(8,128)S(1)}, f32[226,128]{1,0:T(8,128)S(1)}, u32[]{:S(2)}, u32[]{:S(2)}) %collective-permute-start.52) | collective-permute-done | bytes 115744 | tf_op jit(solution)/shard_map/ppermute | solution.py:530
  513.3 6.9 %collective-permute-done.51 = f32[226,128]{1,0:T(8,128)S(1)} collective-permute-done((f32[226,128]{1,0:T(8,128)S(1)}, f32[226,128]{1,0:T(8,128)S(1)}, u32[]{:S(2)}, u32[]{:S(2)}) %collective-permute-start.51) | collective-permute-done | bytes 115744 | tf_op jit(solution)/shard_map/ppermute | solution.py:530
  529.3 18.8 %collective-permute-done.56 = f32[226,128]{1,0:T(8,128)S(1)} collective-permute-done((f32[226,128]{1,0:T(8,128)S(1)}, f32[226,128]{1,0:T(8,128)S(1)}, u32[]{:S(2)}, u32[]{:S(2)}) %collective-permute-start.56) | collective-permute-done | bytes 115744 | tf_op jit(solution)/shard_map/ppermute | solution.py:530
  575.6 9.0 %collective-permute-done.59 = bf16[64,2048]{1,0:T(8,128)(2,1)} collective-permute-done((bf16[64,2048]{1,0:T(8,128)(2,1)S(1)}, bf16[64,2048]{1,0:T(8,128)(2,1)}, u32[]{:S(2)}, u32[]{:S(2)}) %collective-permute-start.59) | collective-permute-done | bytes 262176 | tf_op jit(solution)/shard_map/ppermute | solution.py:530
  (456 shorter events, 277.4 us)
Async XLA Ops:
  12.1 22.0 %all-to-all-start = ((bf16[8,64,1152]{2,1,0:T(8,128)(2,1)}), bf16[8,64,1152]{2,1,0:T(8,128)(2,1)S(1)}, u32[]{:S(2)}, u32[]{:S(2)}) async-start(bf16[8,64,1152]{2,1,0:T(8,128)(2,1)} %fusion.12), calls=%async_computation | async-start | bytes 2359296 | tf_op jit(solution)/shard_map/all_to_all | solution.py:595
  17.3 105.2 %all-gather.9.cloned.1.call-start = ((), (), s32[]{:S(2)}) async-start(), calls=%async_computation.13 | async-start | bytes 5406720 | tf_op jit(solution)/shard_map/all_gather | solution.py:600
  17.9 20.7 %collective-permute-start.2 = (bf16[64,2048]{1,0:T(8,128)(2,1)S(1)}, bf16[64,2048]{1,0:T(8,128)(2,1)S(1)}, u32[]{:S(2)}, u32[]{:S(2)}) collective-permute-start(bf16[64,2048]{1,0:T(8,128)(2,1)S(1)} %copy-done.39), channel_id=1, source_target_pairs={{0,24},{8,16},{16,8},{24,0},{1,25},{9,17},{17,9},{25,1},{2,26},{10... | collective-permute-start | bytes 786440 | tf_op jit(solution)/shard_map/ppermute | solution.py:530
  21.5 23.0 %collective-permute-start.1 = (bf16[64,2048]{1,0:T(8,128)(2,1)S(1)}, bf16[64,2048]{1,0:T(8,128)(2,1)}, u32[]{:S(2)}, u32[]{:S(2)}) collective-permute-start(bf16[64,2048]{1,0:T(8,128)(2,1)S(1)} %copy-done.39), channel_id=1, source_target_pairs={{0,16},{8,24},{16,0},{24,8},{1,17},{9,25},{17,1},{25,9},{2,18},{10... | collective-permute-start | bytes 786440 | tf_op jit(solution)/shard_map/ppermute | solution.py:530
  21.5 23.0 %collective-permute-start = (bf16[64,2048]{1,0:T(8,128)(2,1)S(1)}, bf16[64,2048]{1,0:T(8,128)(2,1)}, u32[]{:S(2)}, u32[]{:S(2)}) collective-permute-start(bf16[64,2048]{1,0:T(8,128)(2,1)S(1)} %copy-done.39), channel_id=1, source_target_pairs={{0,8},{8,0},{16,24},{24,16},{1,9},{9,1},{17,25},{25,17},{2,10},{10... | collective-permute-start | bytes 786440 | tf_op jit(solution)/shard_map/ppermute | solution.py:530
  49.3 16.6 %collective-permute-start.5 = (bf16[128,2048]{1,0:T(8,128)(2,1)}, bf16[128,2048]{1,0:T(8,128)(2,1)S(1)}, u32[]{:S(2)}, u32[]{:S(2)}) collective-permute-start(bf16[128,2048]{1,0:T(8,128)(2,1)} %pad_maximum_fusion.10), channel_id=1, source_target_pairs={{0,2},{1,3},{2,0},{3,1},{4,6},{5,7},{6,4},{7,5},{8,10},{9,11},{10,... | collective-permute-start | bytes 1572872 | tf_op jit(solution)/shard_map/ppermute | solution.py:530
  77.9 20.4 %collective-permute-start.7 = (bf16[512,2048]{1,0:T(8,128)(2,1)}, bf16[512,2048]{1,0:T(8,128)(2,1)}, u32[]{:S(2)}, u32[]{:S(2)}) collective-permute-start(bf16[512,2048]{1,0:T(8,128)(2,1)} %get-tuple-element.174), channel_id=1, source_target_pairs={{0,1},{1,0},{2,3},{3,2},{4,5},{5,4},{6,7},{7,6},{8,9},{9,8},{10,11... | collective-permute-start | bytes 6291464 | tf_op jit(solution)/shard_map/ppermute | solution.py:530
  89.9 32.6 %all-to-all-start.1 = ((bf16[8,64,2112]{2,1,0:T(8,128)(2,1)}), bf16[8,64,2112]{2,1,0:T(8,128)(2,1)}, u32[]{:S(2)}, u32[]{:S(2)}) async-start(bf16[8,64,2112]{2,1,0:T(8,128)(2,1)} %reshape.309), calls=%async_computation.1 | async-start | bytes 4456448 | tf_op jit(solution)/shard_map/all_to_all | solution.py:595
  94.4 136.2 %all-gather.5.cloned.1.call-start = ((), (), s32[]{:S(2)}) async-start(), calls=%async_computation.8 | async-start | bytes 7208960 | tf_op jit(solution)/shard_map/all_gather | solution.py:600
  125.1 168.5 %all-gather.7.cloned.1.call-start = ((), (), s32[]{:S(2)}) async-start(), calls=%async_computation.9 | async-start | bytes 3932160 | tf_op jit(solution)/shard_map/all_gather | solution.py:600
  175.6 18.8 %collective-permute-start.22 = (bf16[64,2048]{1,0:T(8,128)(2,1)}, bf16[64,2048]{1,0:T(8,128)(2,1)}, u32[]{:S(2)}, u32[]{:S(2)}) collective-permute-start(bf16[64,2048]{1,0:T(8,128)(2,1)} %get-tuple-element.173), channel_id=1, source_target_pairs={{0,2},{1,3},{2,0},{3,1},{4,6},{5,7},{6,4},{7,5},{8,10},{9,11},{10,... | collective-permute-start | bytes 786440 | tf_op jit(solution)/shard_map/ppermute | solution.py:530
  186.5 25.0 %collective-permute-start.12 = (bf16[4,128,2048]{2,1,0:T(8,128)(2,1)}, bf16[4,128,2048]{2,1,0:T(8,128)(2,1)}, u32[]{:S(2)}, u32[]{:S(2)}) collective-permute-start(bf16[4,128,2048]{2,1,0:T(8,128)(2,1)} %bitcast.39), channel_id=1, source_target_pairs={{0,1},{1,0},{2,3},{3,2},{4,5},{5,4},{6,7},{7,6},{8,9},{9,8},{10,11... | collective-permute-start | bytes 6291464 | tf_op jit(solution)/shard_map/ppermute | solution.py:530
  193.9 183.9 %reduce-scatter.4.cloned.1.call-start = ((), (), s32[]{:S(2)}) async-start(), calls=%async_computation.10 | async-start | bytes 3604480 | tf_op jit(solution)/shard_map/reduce_scatter | solution.py:604
  219.0 50.5 %collective-permute-start.26 = (bf16[512,2048]{1,0:T(8,128)(2,1)}, bf16[512,2048]{1,0:T(8,128)(2,1)}, u32[]{:S(2)}, u32[]{:S(2)}) collective-permute-start(bf16[512,2048]{1,0:T(8,128)(2,1)} %get-tuple-element.168), channel_id=1, source_target_pairs={{0,1},{1,0},{2,3},{3,2},{4,5},{5,4},{6,7},{7,6},{8,9},{9,8},{10,11... | collective-permute-start | bytes 6291464 | tf_op jit(solution)/shard_map/ppermute | solution.py:530
  293.6 227.2 %reduce-scatter.8.cloned.1.call-start = ((), (), s32[]{:S(2)}) async-start(), calls=%async_computation.12 | async-start | bytes 7208960 | tf_op jit(solution)/shard_map/reduce_scatter | solution.py:604
  428.6 23.6 %collective-permute-start.42 = (bf16[4,128,2048]{2,1,0:T(8,128)(2,1)}, bf16[4,128,2048]{2,1,0:T(8,128)(2,1)}, u32[]{:S(2)}, u32[]{:S(2)}) collective-permute-start(bf16[4,128,2048]{2,1,0:T(8,128)(2,1)} %bitcast.62), channel_id=1, source_target_pairs={{0,1},{1,0},{2,3},{3,2},{4,5},{5,4},{6,7},{7,6},{8,9},{9,8},{10,11... | collective-permute-start | bytes 6291464 | tf_op jit(solution)/shard_map/ppermute | solution.py:530
  435.2 23.8 %collective-permute-start.37 = (bf16[4,128,2048]{2,1,0:T(8,128)(2,1)}, bf16[4,128,2048]{2,1,0:T(8,128)(2,1)}, u32[]{:S(2)}, u32[]{:S(2)}) collective-permute-start(bf16[4,128,2048]{2,1,0:T(8,128)(2,1)} %bitcast.53), channel_id=1, source_target_pairs={{0,1},{1,0},{2,3},{3,2},{4,5},{5,4},{6,7},{7,6},{8,9},{9,8},{10,11... | collective-permute-start | bytes 6291464 | tf_op jit(solution)/shard_map/ppermute | solution.py:530
  443.6 77.2 %all-to-all-start.3 = ((bf16[8,64,704]{2,1,0:T(8,128)(2,1)}), bf16[8,64,704]{2,1,0:T(8,128)(2,1)}, u32[]{:S(2)}, u32[]{:S(2)}) async-start(bf16[8,64,704]{2,1,0:T(8,128)(2,1)} %bitcast.86), calls=%async_computation.6 | async-start | bytes 1572864 | tf_op jit(solution)/shard_map/all_to_all | solution.py:609
  447.8 100.4 %reduce-scatter.6.cloned.1.call-start = ((), (), s32[]{:S(2)}) async-start(), calls=%async_computation.11 | async-start | bytes 5406720 | tf_op jit(solution)/shard_map/reduce_scatter | solution.py:604
  461.7 21.9 %collective-permute-start.38 = (bf16[2,64,2048]{2,1,0:T(8,128)(2,1)S(1)}, bf16[2,64,2048]{2,1,0:T(8,128)(2,1)S(1)}, u32[]{:S(2)}, u32[]{:S(2)}) collective-permute-start(bf16[2,64,2048]{2,1,0:T(8,128)(2,1)S(1)} %slice.377), channel_id=1, source_target_pairs={{0,2},{1,3},{2,0},{3,1},{4,6},{5,7},{6,4},{7,5},{8,10},{9,11},{10,... | collective-permute-start | bytes 1572872 | tf_op jit(solution)/shard_map/ppermute | solution.py:530
  462.3 21.3 %collective-permute-start.40 = (bf16[2,64,2048]{2,1,0:T(8,128)(2,1)S(1)}, bf16[2,64,2048]{2,1,0:T(8,128)(2,1)S(1)}, u32[]{:S(2)}, u32[]{:S(2)}) collective-permute-start(bf16[2,64,2048]{2,1,0:T(8,128)(2,1)S(1)} %slice.454), channel_id=1, source_target_pairs={{0,4},{1,5},{2,6},{3,7},{4,0},{5,1},{6,2},{7,3},{8,12},{9,13},{10,... | collective-permute-start | bytes 1572872 | tf_op jit(solution)/shard_map/ppermute | solution.py:530
  472.6 16.9 %collective-permute-start.46 = (bf16[64,2048]{1,0:T(8,128)(2,1)S(1)}, bf16[64,2048]{1,0:T(8,128)(2,1)S(1)}, u32[]{:S(2)}, u32[]{:S(2)}) collective-permute-start(bf16[64,2048]{1,0:T(8,128)(2,1)S(1)} %fusion.39), channel_id=1, source_target_pairs={{0,2},{1,3},{2,0},{3,1},{4,6},{5,7},{6,4},{7,5},{8,10},{9,11},{10,... | collective-permute-start | bytes 786440 | tf_op jit(solution)/shard_map/ppermute | solution.py:530
  496.2 17.1 %collective-permute-start.52 = (f32[226,128]{1,0:T(8,128)S(1)}, f32[226,128]{1,0:T(8,128)S(1)}, u32[]{:S(2)}, u32[]{:S(2)}) collective-permute-start(f32[226,128]{1,0:T(8,128)S(1)} %bitcast.257), channel_id=1, source_target_pairs={{0,16},{8,24},{16,0},{24,8},{1,17},{9,25},{17,1},{25,9},{2,18},{10... | collective-permute-start | bytes 347144 | tf_op jit(solution)/shard_map/ppermute | solution.py:530
  501.7 18.5 %collective-permute-start.51 = (f32[226,128]{1,0:T(8,128)S(1)}, f32[226,128]{1,0:T(8,128)S(1)}, u32[]{:S(2)}, u32[]{:S(2)}) collective-permute-start(f32[226,128]{1,0:T(8,128)S(1)} %bitcast.259), channel_id=1, source_target_pairs={{0,8},{8,0},{16,24},{24,16},{1,9},{9,1},{17,25},{25,17},{2,10},{10... | collective-permute-start | bytes 347144 | tf_op jit(solution)/shard_map/ppermute | solution.py:530
  520.9 27.4 %all-to-all-start.2 = ((bf16[8,64,1408]{2,1,0:T(8,128)(2,1)}), bf16[8,64,1408]{2,1,0:T(8,128)(2,1)S(1)}, u32[]{:S(2)}, u32[]{:S(2)}) async-start(bf16[8,64,1408]{2,1,0:T(8,128)(2,1)} %bitcast.241), calls=%async_computation.5 | async-start | bytes 2883584 | tf_op jit(solution)/shard_map/all_to_all | solution.py:609
  524.6 23.5 %collective-permute-start.56 = (f32[226,128]{1,0:T(8,128)S(1)}, f32[226,128]{1,0:T(8,128)S(1)}, u32[]{:S(2)}, u32[]{:S(2)}) collective-permute-start(f32[226,128]{1,0:T(8,128)S(1)} %add.370), channel_id=1, source_target_pairs={{0,4},{1,5},{2,6},{3,7},{4,0},{5,1},{6,2},{7,3},{8,12},{9,13},{10,... | collective-permute-start | bytes 347144 | tf_op jit(solution)/shard_map/ppermute | solution.py:530
  526.6 21.5 %collective-permute-start.57 = (f32[226,128]{1,0:T(8,128)S(1)}, f32[226,128]{1,0:T(8,128)S(1)}, u32[]{:S(2)}, u32[]{:S(2)}) collective-permute-start(f32[226,128]{1,0:T(8,128)S(1)} %add.370), channel_id=1, source_target_pairs={{0,6},{1,7},{2,4},{3,5},{4,2},{5,3},{6,0},{7,1},{8,14},{9,15},{10,... | collective-permute-start | bytes 347144 | tf_op jit(solution)/shard_map/ppermute | solution.py:530
  528.0 20.2 %collective-permute-start.55 = (f32[226,128]{1,0:T(8,128)S(1)}, f32[226,128]{1,0:T(8,128)S(1)}, u32[]{:S(2)}, u32[]{:S(2)}) collective-permute-start(f32[226,128]{1,0:T(8,128)S(1)} %add.370), channel_id=1, source_target_pairs={{0,2},{1,3},{2,0},{3,1},{4,6},{5,7},{6,4},{7,5},{8,10},{9,11},{10,... | collective-permute-start | bytes 347144 | tf_op jit(solution)/shard_map/ppermute | solution.py:530
  551.5 35.2 %all-to-all-start.4 = ((bf16[8,64,1152]{2,1,0:T(8,128)(2,1)}), bf16[8,64,1152]{2,1,0:T(8,128)(2,1)S(1)}, u32[]{:S(2)}, u32[]{:S(2)}) async-start(bf16[8,64,1152]{2,1,0:T(8,128)(2,1)} %bitcast.229), calls=%async_computation.7 | async-start | bytes 2359296 | tf_op jit(solution)/shard_map/all_to_all | solution.py:609
  557.0 18.6 %collective-permute-start.60 = (bf16[64,2048]{1,0:T(8,128)(2,1)}, bf16[64,2048]{1,0:T(8,128)(2,1)}, u32[]{:S(2)}, u32[]{:S(2)}) collective-permute-start(bf16[64,2048]{1,0:T(8,128)(2,1)} %get-tuple-element.138), channel_id=1, source_target_pairs={{0,24},{8,16},{16,8},{24,0},{1,25},{9,17},{17,9},{25,1},{2,26},{10... | collective-permute-start | bytes 786440 | tf_op jit(solution)/shard_map/ppermute | solution.py:530
  559.7 24.9 %collective-permute-start.59 = (bf16[64,2048]{1,0:T(8,128)(2,1)S(1)}, bf16[64,2048]{1,0:T(8,128)(2,1)}, u32[]{:S(2)}, u32[]{:S(2)}) collective-permute-start(bf16[64,2048]{1,0:T(8,128)(2,1)S(1)} %get-tuple-element.139), channel_id=1, source_target_pairs={{0,16},{8,24},{16,0},{24,8},{1,17},{9,25},{17,1},{25,9},{2,18},{10... | collective-permute-start | bytes 786440 | tf_op jit(solution)/shard_map/ppermute | solution.py:530
  564.0 20.5 %collective-permute-start.58 = (bf16[64,2048]{1,0:T(8,128)(2,1)S(1)}, bf16[64,2048]{1,0:T(8,128)(2,1)}, u32[]{:S(2)}, u32[]{:S(2)}) collective-permute-start(bf16[64,2048]{1,0:T(8,128)(2,1)S(1)} %get-tuple-element.137), channel_id=1, source_target_pairs={{0,8},{8,0},{16,24},{24,16},{1,9},{9,1},{17,25},{25,17},{2,10},{10... | collective-permute-start | bytes 786440 | tf_op jit(solution)/shard_map/ppermute | solution.py:530
  (103 other events, 1184.4 us)
Sparse Core Ops, SparseCore 0:
  37.8 82.3 all-gather.8
  125.2 104.9 all-gather.4
  231.8 61.7 all-gather.6
  296.3 54.8 reduce-scatter.3
  353.3 102.0 reduce-scatter.7
  457.6 87.0 reduce-scatter.5
